TPU v7x, 32 devices: a whole 2x2x4 slice. The times are simulated.
32 devices in a mesh: grp: 2 (over y), seq: 4 (over z), head: 2 (over x), sub: 2 (over core).
Axes of the slice: x: 2, y: 2, z: 4, core: 2. Of those that a mesh axis runs over, the one named last changes fastest.
Arguments:
- queries: float32 [1536, 2048], P(('grp', 'seq'), ('head', 'sub')), parts along dimension 0, may hold values from -6 to 6
- keys: float32 [1536, 2048], P(('grp', 'seq'), ('head', 'sub')), parts along dimension 0, may hold values from -6 to 6
- values: float32 [1536, 2048], P(('grp', 'seq'), ('head', 'sub')), parts along dimension 0, may hold values from -40 to 40
- opt_queries: float32 [16, 64, 2048], P(('grp', 'seq'), None, ('head', 'sub')), parts along dimension 0, may hold values from -6 to 6
- opt_keys: float32 [16, 64, 2048], P(('grp', 'seq'), None, ('head', 'sub')), parts along dimension 0, may hold values from -6 to 6
- opt_values: float32 [16, 64, 2048], P(('grp', 'seq'), None, ('head', 'sub')), parts along dimension 0, may hold values from -40 to 40
- opt_offsets: int32 [16], P(('grp', 'seq')), parts along dimension 0, may hold values from 0 to 192
- opt_lengths: int32 [16], P(('grp', 'seq')), parts along dimension 0, may hold values from 1 to 64, 320 in all
- norm_gain: float32 [2048], P(('head', 'sub')), may hold values from 0.5 to 2
- out_weight: bfloat16 [2048, 4096], P(('head', 'sub')), may hold values from -0.125 to 0.125
Outputs:
- ctx_out: bfloat16 [1536, 4096], P(('grp', 'seq'), ('head', 'sub')), parts along dimension 0
- opt_out: bfloat16 [16, 64, 4096], P(('grp', 'seq'), None, ('head', 'sub')), parts along dimension 0
There are 2 independent parts, one for each index of `grp`. A program takes and returns all parts, laid end to end along the dimension named above; an argument that names none is the same for every part. Nothing has to cross between parts.
Inputs may be any that keep to these rules, and one draw needn't show every extreme that they name: `opt_lengths`: within each scoring group the 8 lengths sum to 320, and the longest option of each group has exactly 64 tokens in every draw.
All inputs are finite; a program needn't handle non-finite values.
Results may differ from a plain program's by a relative error of at most 0.017.
Values may be sent and summed in bfloat16 or wider, within the bound.
No kernel may reach another device: no remote copies, remote signals or barrier semaphores. Data moves between devices by JAX's collectives and lax.ppermute only.
A program may use at most 64 MiB of HBM per device.

v0:
```python
import jax
import jax.numpy as jnp
from jax import lax
from jax.sharding import PartitionSpec as P

DH = 128


norm_epsilon = 1e-05


def entering(value, axis, join, neutral):
    place = lax.axis_index(axis)
    gathered = lax.all_gather(value.astype(jnp.bfloat16), axis)
    state = jnp.zeros_like(value) + jnp.asarray(neutral, value.dtype)

    def one(hop, state):
        return join(state, lax.dynamic_index_in_dim(gathered, hop, 0, False).astype(value.dtype))

    return lax.fori_loop(0, place, one, state)


def head_norm(attended, gain, mask):
    mean_square = jnp.mean(attended * attended, axis=-1, keepdims=True)
    return (attended * lax.rsqrt(mean_square + norm_epsilon) * gain * mask).astype(jnp.bfloat16)


def combine_sum(earlier, later):
    return earlier + later


def grouped_project(rows, weight_columns, groups):
    count = rows.shape[0]
    flat = rows.reshape(count, groups, rows.shape[1] // groups)
    weight_groups = weight_columns.reshape(
        groups, weight_columns.shape[0] // groups, weight_columns.shape[1]
    )
    partial_value = jnp.einsum(
        "rgk,gkd->grd", flat, weight_groups, preferred_element_type=jnp.float32
    )
    partial_value = lax.optimization_barrier(partial_value.astype(jnp.bfloat16)).astype(jnp.float32)
    return jnp.sum(partial_value, axis=0).astype(jnp.bfloat16)


def on_device(
    queries,
    keys,
    values,
    opt_queries,
    opt_keys,
    opt_values,
    opt_offsets,
    opt_lengths,
    norm_gain,
    out_weight,
):
    highest = lax.Precision.HIGHEST
    tok_rows = queries.shape[0]
    heads = queries.shape[1] // DH
    opt_count = opt_queries.shape[0]
    slot_count = opt_queries.shape[1]
    group_count = lax.axis_size(("head", "sub"))
    weight_columns = lax.all_to_all(
        out_weight, ("head", "sub"), split_axis=1, concat_axis=0, tiled=True
    )
    block_q = queries.reshape(tok_rows, heads, DH)
    block_k = keys.reshape(tok_rows, heads, DH)
    block_v = values.reshape(tok_rows, heads, DH)
    gain = norm_gain.reshape(heads, DH)
    states = jnp.einsum("thd,the->hde", block_k, block_v, precision=highest)
    positions = jnp.arange(tok_rows, dtype=jnp.int32)
    causal = (positions[:, None] >= positions[None, :]).astype(jnp.float32)
    scores = jnp.einsum("thd,shd->hts", block_q, block_k, precision=highest) * causal[None]
    intra = jnp.einsum("hts,she->the", scores, block_v, precision=highest)
    opt_q = opt_queries.reshape(opt_count, slot_count, heads, DH)
    opt_k = opt_keys.reshape(opt_count, slot_count, heads, DH)
    opt_v = opt_values.reshape(opt_count, slot_count, heads, DH)
    before = (positions[None, :] < opt_offsets[:, None]).astype(jnp.float32)
    local = jnp.einsum("ot,thd,the->ohde", before, block_k, block_v, precision=highest)
    slots = jnp.arange(slot_count, dtype=jnp.int32)
    slot_causal = (slots[:, None] >= slots[None, :]).astype(jnp.float32)
    opt_scores = (
        jnp.einsum("oihd,ojhd->ohij", opt_q, opt_k, precision=highest) * slot_causal[None, None]
    )
    opt_intra = jnp.einsum("ohij,ojhe->oihe", opt_scores, opt_v, precision=highest)
    prefix = entering(states, "seq", combine_sum, jnp.zeros_like(states))
    inter = jnp.einsum("thd,hde->the", block_q, prefix, precision=highest)
    context_normed = head_norm(inter + intra, gain, 1.0).reshape(tok_rows, heads * DH)
    opt_state = prefix[None] + local
    opt_inter = jnp.einsum("oihd,ohde->oihe", opt_q, opt_state, precision=highest)
    valid = (slots[None, :] < opt_lengths[:, None]).astype(jnp.float32)
    opt_normed = head_norm(opt_inter + opt_intra, gain, valid[:, :, None, None]).reshape(
        opt_count * slot_count, heads * DH
    )
    gathered_ctx, gathered_opt = (
        lax.all_gather(context_normed, ("head", "sub"), axis=1, tiled=True),
        lax.all_gather(opt_normed, ("head", "sub"), axis=1, tiled=True),
    )
    context_out = grouped_project(gathered_ctx, weight_columns, group_count)
    opt_rows = grouped_project(gathered_opt, weight_columns, group_count)
    option_out = opt_rows.reshape(opt_count, slot_count, opt_rows.shape[1])
    return (context_out, option_out)


def solution(mesh):
    placed = (
        P(("grp", "seq"), ("head", "sub")),
        P(("grp", "seq"), ("head", "sub")),
        P(("grp", "seq"), ("head", "sub")),
        P(("grp", "seq"), None, ("head", "sub")),
        P(("grp", "seq"), None, ("head", "sub")),
        P(("grp", "seq"), None, ("head", "sub")),
        P(("grp", "seq")),
        P(("grp", "seq")),
        P(("head", "sub")),
        P(("head", "sub"), None),
    )
    return jax.shard_map(
        on_device,
        mesh=mesh,
        in_specs=placed,
        out_specs=(P(("grp", "seq"), ("head", "sub")), P(("grp", "seq"), None, ("head", "sub"))),
        check_vma=False,
    )
```

profile of v0, /device:TPU:0, one launch (start us, length us, event | category | flops | bytes accessed | tf_op | source)
XLA Modules:
  0.0 91.5 jit_solution(10964770409362976219)
XLA Ops:
  0.6 0.0 copy-start
  0.6 6.5 %copy.40 = bf16[512,4096]{0,1:T(8,128)(2,1)} copy(bf16[512,4096]{1,0:T(8,128)(2,1)} %param.21) | data formatting | bytes 8388608 | tf_op args[9]
  7.2 6.3 %copy.41 = bf16[512,4,1024]{2,0,1:T(8,128)(2,1)} copy(bf16[512,4,1024]{0,2,1:T(8,128)(2,1)} %bitcast.132) | data formatting | bytes 8388608 | tf_op jit(solution)/shard_map/all_to_all | solution.py:63
  13.5 0.0 copy-start.1
  13.5 5.0 %all-to-all-start = ((bf16[512,4,1024]{2,0,1:T(8,128)(2,1)}), bf16[512,4,1024]{2,0,1:T(8,128)(2,1)}, u32[]{:S(2)}, u32[]{:S(2)}) async-start(bf16[512,4,1024]{2,0,1:T(8,128)(2,1)} %copy.41), calls=%async_computation | async-start | bytes 8388608 | tf_op jit(solution)/shard_map/all_to_all | solution.py:63
  18.5 0.0 copy-start.8
  18.5 0.0 copy-start.4
  18.5 0.0 copy-start.5
  18.5 0.0 copy-start.9
  18.6 0.0 copy-done
  18.6 0.0 copy-done.1
  18.6 0.0 copy-start.6
  18.6 1.1 %convolution_convert_fusion = bf16[4,128,128]{2,1,0:T(8,128)(2,1)S(1)} fusion(f32[192,512]{1,0:T(8,128)S(1)} %copy-done.1, f32[192,512]{1,0:T(8,128)S(1)} %copy-done), kind=kOutput, calls=%fused_computation.17 | convolution fusion | flops 151060480 | bytes 917504 | tf_op jit(solution)/shard_map/thd,the->hde/dot_general | solution.py:70
  19.7 17.9 %all-gather = bf16[16,128,128]{2,1,0:T(8,128)(2,1)S(1)} all-gather(bf16[4,128,128]{2,1,0:T(8,128)(2,1)S(1)} %convolution_convert_fusion), channel_id=2, replica_groups=mesh['grp'=2,'seq'=4,'head'=2,'sub'=2] {'seq'}, dimensions={0}, use_global_device_ids=true | all-gather | bytes 655360 | tf_op jit(solution)/shard_map/all_gather | solution.py:14
  37.6 0.0 copy-start.7
  37.6 0.0 copy-done.8
  37.6 0.0 copy-start.3
  37.6 0.1 fusion.39
  37.7 0.0 copy-done.4
  37.7 0.0 copy-done.5
  37.7 0.5 convolution_multiply_fusion.1
  38.3 0.0 copy-done.9
  38.3 0.1 compare_convert_fusion.1
  38.4 1.9 %fusion.10 = f32[2,4,128,128]{3,2,1,0:T(8,128)S(1)} fusion(f32[192,4,128]{2,0,1:T(8,128)S(1)} %copy_bitcast_fusion, f32[192,2]{0,1:T(2,128)S(1)} %fusion.39, f32[4,128,128]{2,1,0:T(8,128)S(1)} %get-tuple-element.25, f32[192,512]{1,0:T(8,128)S(1)} %copy-done.1), kind=kOutput, calls=%fused_computation.9 | convolution fusion | flops 302317568 | bytes 1574400 | tf_op jit(solution)/shard_map/ot,thd,the->ohde/dot_general | solution.py:79
  40.3 0.6 convolution_bitcast_fusion.3
  40.9 0.0 copy-done.6
  40.9 0.5 multiply_reduce_fusion.1
  41.4 0.0 copy-done.7
  41.4 0.2 multiply_convert_fusion.1
  41.6 0.1 copy.49
  41.7 29.2 %all_gather.15 = bf16[128,2048]{1,0:T(8,128)(2,1)S(1)} all-gather(bf16[128,512]{1,0:T(8,128)(2,1)S(1)} %bitcast.136), channel_id=1, replica_groups=mesh['grp'=2,'seq'=4,'head'=2,'sub'=2] {'head','sub'}, dimensions={1}, use_global_device_ids=true | all-gather | bytes 655360 | tf_op jit(solution)/shard_map/all_gather | solution.py:97
  70.9 1.0 %copy.50 = bf16[128,2048]{0,1:T(8,128)(2,1)} copy(bf16[128,2048]{1,0:T(8,128)(2,1)S(1)} %all_gather.15) | data formatting | bytes 1048576 | tf_op jit(solution)/shard_map/all_gather | solution.py:97
  72.0 0.0 copy-done.3
  72.0 0.5 convolution_bitcast_fusion.1
  72.5 0.8 convolution_multiply_fusion
  73.3 1.0 %multiply_reduce_fusion = (f32[192,4]{0,1:T(4,128)S(1)}, f32[192,4,128]{2,0,1:T(8,128)S(1)}) fusion(f32[192,4,128]{2,0,1:T(8,128)S(1)} %convolution_bitcast_fusion.1, f32[4,192,192]{2,1,0:T(8,128)S(1)} %convolution_multiply_fusion, f32[192,512]{1,0:T(8,128)S(1)} %copy-done.1), kind=kOutput, calls=%fused_computation.31 | convolution fusion | flops 226786560 | bytes 1772544 | tf_op jit(solution)/shard_map/hts,she->the/dot_general | solution.py:74
  74.3 0.2 copy_bitcast_fusion.1
  74.4 8.7 %all_gather.14 = bf16[192,2048]{1,0:T(8,128)(2,1)S(1)} all-gather(bf16[192,512]{1,0:T(8,128)(2,1)S(1)} %copy_bitcast_fusion.1), channel_id=1, replica_groups=mesh['grp'=2,'seq'=4,'head'=2,'sub'=2] {'head','sub'}, dimensions={1}, use_global_device_ids=true | all-gather | bytes 983040 | tf_op jit(solution)/shard_map/all_gather | solution.py:96
  83.2 0.0 all-to-all-done
  83.2 0.0 copy-start.2
  83.2 3.2 %fusion.4 = bf16[4,192,1024]{2,1,0:T(8,128)(2,1)S(1)} fusion(bf16[512,4,1024]{2,0,1:T(8,128)(2,1)} %all-to-all-done, bf16[24,4,8,512]{3,2,1,0:T(8,128)(2,1)S(1)} %bitcast.133), kind=kOutput, calls=%fused_computation.5 | convolution fusion | flops 806092800 | bytes 6553600 | tf_op jit(solution)/shard_map/rgk,gkd->grd/dot_general | solution.py:38
  86.4 0.0 copy-done.2
  86.4 3.0 %fusion.7 = bf16[4,128,1024]{2,1,0:T(8,128)(2,1)S(1)} fusion(bf16[128,4,512]{0,2,1:T(8,128)(2,1)S(1)} %bitcast.134, bf16[512,4,1024]{2,0,1:T(8,128)(2,1)} %all-to-all-done), kind=kOutput, calls=%fused_computation.6 | convolution fusion | flops 537395200 | bytes 5767168 | tf_op jit(solution)/shard_map/rgk,gkd->grd/dot_general | solution.py:38
  89.4 1.1 %reduce_sum.43 = bf16[192,1024]{1,0:T(8,128)(2,1)} reduce(bf16[4,192,1024]{2,1,0:T(8,128)(2,1)S(1)} %fusion.4, bf16[]{:T(256)} %constant.28.clone.1), dimensions={0}, to_apply=%region_3.4 | reduce | flops 589824 | bytes 1966082 | tf_op jit(solution)/shard_map/reduce_sum | solution.py:42
  90.6 0.9 %reduce_sum.45 = bf16[128,1024]{1,0:T(8,128)(2,1)} reduce(bf16[4,128,1024]{2,1,0:T(8,128)(2,1)S(1)} %fusion.7, bf16[]{:T(256)} %constant.28.clone.1), dimensions={0}, to_apply=%region_5.6 | reduce | flops 393216 | bytes 1310722 | tf_op jit(solution)/shard_map/reduce_sum | solution.py:42
  (8 shorter events, 0.1 us)
Async XLA Ops:
  0.6 17.9 %copy-start = (f32[192,512]{1,0:T(8,128)S(1)}, f32[192,512]{1,0:T(8,128)}, u32[]{:S(2)}) copy-start(f32[192,512]{1,0:T(8,128)} %param.13) | copy-start | bytes 1179652
  13.5 5.1 %copy-start.1 = (f32[192,512]{1,0:T(8,128)S(1)}, f32[192,512]{1,0:T(8,128)}, u32[]{:S(2)}) copy-start(f32[192,512]{1,0:T(8,128)} %param.14) | copy-start | bytes 1179652
  13.5 69.7 %all-to-all-start = ((bf16[512,4,1024]{2,0,1:T(8,128)(2,1)}), bf16[512,4,1024]{2,0,1:T(8,128)(2,1)}, u32[]{:S(2)}, u32[]{:S(2)}) async-start(bf16[512,4,1024]{2,0,1:T(8,128)(2,1)} %copy.41), calls=%async_computation | async-start | bytes 8388608 | tf_op jit(solution)/shard_map/all_to_all | solution.py:63
  18.5 19.1 %copy-start.8 = (s32[2]{0:T(128)S(1)}, s32[2]{0:T(128)}, u32[]{:S(2)}) copy-start(s32[2]{0:T(128)} %param.18) | copy-start | bytes 28
  18.5 19.2 %copy-start.4 = (f32[2,64,512]{2,1,0:T(8,128)S(1)}, f32[2,64,512]{2,1,0:T(8,128)}, u32[]{:S(2)}) copy-start(f32[2,64,512]{2,1,0:T(8,128)} %param.15) | copy-start | bytes 786436
  18.5 19.2 %copy-start.5 = (f32[2,64,512]{2,1,0:T(8,128)S(1)}, f32[2,64,512]{2,1,0:T(8,128)}, u32[]{:S(2)}) copy-start(f32[2,64,512]{2,1,0:T(8,128)} %param.16) | copy-start | bytes 786436
  18.5 19.8 %copy-start.9 = (s32[2]{0:T(128)S(1)}, s32[2]{0:T(128)}, u32[]{:S(2)}) copy-start(s32[2]{0:T(128)} %param.19) | copy-start | bytes 28
  18.6 22.3 %copy-start.6 = (f32[2,64,512]{2,1,0:T(8,128)S(1)}, f32[2,64,512]{2,1,0:T(8,128)}, u32[]{:S(2)}) copy-start(f32[2,64,512]{2,1,0:T(8,128)} %param.17) | copy-start | bytes 786436
  37.6 3.8 %copy-start.7 = (f32[512]{0:T(512)S(1)}, f32[512]{0:T(512)}, u32[]{:S(2)}) copy-start(f32[512]{0:T(512)} %param.20) | copy-start | bytes 6148
  37.6 34.3 %copy-start.3 = (f32[192,512]{1,0:T(8,128)S(1)}, f32[192,512]{1,0:T(8,128)}, u32[]{:S(2)}) copy-start(f32[192,512]{1,0:T(8,128)} %param.12) | copy-start | bytes 1179652
  83.2 3.2 %copy-start.2 = (bf16[128,2048]{0,1:T(8,128)(2,1)S(1)}, bf16[128,2048]{0,1:T(8,128)(2,1)}, u32[]{:S(2)}) copy-start(bf16[128,2048]{0,1:T(8,128)(2,1)} %copy.50) | copy-start | bytes 1572868
where the time goes:
time: 92 us; the launch traced here: 91.5 us
  blocking collectives  55.8 us (61%)
  local copies, waits for them, and re-layouts  14.1 us (15%)
  matrix products  13.1 us (14%)
  starting transfers between devices  4.97 us (5%)
  other arithmetic  2.58 us (3%)
    all_gather x1, blocking collectives, on_device(): lax.all_gather(opt_normed, ('head', 'sub'), axis=1, tiled=True)  29.2 us
    all_gather x1, blocking collectives, entering(): gathered = lax.all_gather(value.astype(jnp.bfloat16), axis)  17.9 us
    all_gather x1, blocking collectives, on_device(): lax.all_gather(context_normed, ('head', 'sub'), axis=1, tiled=True)  8.72 us
    unnamed x22, local copies, waits for them, and re-layouts  6.62 us
    all_to_all x1, local copies, waits for them, and re-layouts, on_device(): lax.all_to_all(out_weight, ('head', 'sub'), split_axis=1, concat_axis=0,...  6.33 us
    dot_general x2, matrix products, grouped_project(): jnp.einsum('rgk,gkd->grd', flat, weight_groups, preferred_element_type=jn...  6.22 us
    all_to_all x1, starting transfers between devices, on_device(): lax.all_to_all(out_weight, ('head', 'sub'), split_axis=1, concat_axis=0,...  4.97 us
    reduce_sum x2, other arithmetic, grouped_project(): return jnp.sum(partial_value, axis=0).astype(jnp.bfloat16)  2.06 us
  transfers between devices with their start and end apart: 1, of which 0 were waited for; matrix products, arithmetic and copies ran while one was open for 9% of the time, Pallas kernels for 0%

commit v1 on v0

v1 whole, which is shorter than its diff:
```python
import functools

import jax
import jax.numpy as jnp
from jax import lax
from jax.experimental import pallas as pl
from jax.experimental.pallas import tpu as pltpu
from jax.sharding import PartitionSpec as P

DH = 128
EPS = 1e-05
RADIX = 4
f32 = jnp.float32
bf16 = jnp.bfloat16
HIGHEST = lax.Precision.HIGHEST
VMEM_LIMIT = 40 * 1024 * 1024

VMEM = pl.BlockSpec(memory_space=pltpu.VMEM)
SMEM = pl.BlockSpec(memory_space=pltpu.SMEM)


def call(body, out_shape, specs, flops, nbytes, out_specs=None, **more):
    single = not isinstance(out_shape, (tuple, list))
    if out_specs is None:
        out_specs = VMEM if single else [VMEM] * len(out_shape)
    return pl.pallas_call(
        body,
        out_shape=out_shape,
        in_specs=specs,
        out_specs=out_specs,
        compiler_params=pltpu.CompilerParams(vmem_limit_bytes=VMEM_LIMIT),
        cost_estimate=pl.CostEstimate(flops=flops, bytes_accessed=nbytes, transcendentals=0),
        **more,
    )


def states_kernel(k_ref, v_ref, out_ref):
    for h in range(out_ref.shape[0]):
        cols = slice(h * DH, (h + 1) * DH)
        out_ref[h] = lax.dot_general(
            k_ref[:, cols], v_ref[:, cols], (((0,), (0,)), ((), ())),
            precision=HIGHEST, preferred_element_type=f32,
        ).astype(out_ref.dtype)


def joined(ctx_ref, opt_ref, cols):
    return jnp.concatenate([ctx_ref[:, cols]] + [opt_ref[o, :, cols] for o in range(opt_ref.shape[0])], axis=0)


def base_kernel(offsets_ref, q_ref, k_ref, v_ref, oq_ref, ok_ref, ov_ref, out_ref):
    tokens, opts, slots = q_ref.shape[0], oq_ref.shape[0], oq_ref.shape[1]
    rows = tokens + opts * slots
    i = lax.broadcasted_iota(jnp.int32, (rows, rows), 0)
    j = lax.broadcasted_iota(jnp.int32, (rows, rows), 1)
    limit, first = i + 1, jnp.full((rows, rows), rows, jnp.int32)
    for o in range(opts):
        own = i >= tokens + o * slots
        limit = jnp.where(own, offsets_ref[o], limit)
        first = jnp.where(own, tokens + o * slots, first)
    mask = (j < limit) | ((j >= first) & (j <= i))
    for h in range(q_ref.shape[1] // DH):
        cols = slice(h * DH, (h + 1) * DH)
        q, k, v = joined(q_ref, oq_ref, cols), joined(k_ref, ok_ref, cols), joined(v_ref, ov_ref, cols)
        scores = lax.dot_general(q, k, (((1,), (1,)), ((), ())), precision=HIGHEST, preferred_element_type=f32)
        scores = jnp.where(mask, scores, 0.0)
        out_ref[:, cols] = jnp.dot(scores, v, precision=HIGHEST, preferred_element_type=f32)


def normed_kernel(shifts, place_ref, lengths_ref, q_ref, oq_ref, base_ref, gain_ref, *rest):
    parts, out_ref = rest[:-1], rest[-1]
    tokens, opts, slots = q_ref.shape[0], oq_ref.shape[0], oq_ref.shape[1]
    place = place_ref[0]
    row = lax.broadcasted_iota(jnp.int32, (tokens + opts * slots, 1), 0)
    valid = row < tokens
    for o in range(opts):
        start = tokens + o * slots
        valid = valid | ((row >= start) & (row < start + lengths_ref[o]))
    for h in range(q_ref.shape[1] // DH):
        cols = slice(h * DH, (h + 1) * DH)
        prefix = jnp.zeros((DH, DH), f32)
        for shift, part in zip(shifts, parts):
            prefix = prefix + jnp.where(place >= shift, part[h].astype(f32), 0.0)
        rows = base_ref[:, cols] + jnp.dot(
            joined(q_ref, oq_ref, cols), prefix, precision=HIGHEST, preferred_element_type=f32
        )
        scale = lax.rsqrt(jnp.mean(rows * rows, axis=1, keepdims=True) + EPS)
        out = rows * scale * gain_ref[:, cols]
        out_ref[:, cols] = jnp.where(valid, out, 0.0).astype(out_ref.dtype)


def project_kernel(*refs):
    half = (len(refs) - 1) // 2
    out_ref = refs[-1]
    total = jnp.dot(refs[0][...], refs[half][...], preferred_element_type=f32)
    for a, w in zip(refs[1:half], refs[half + 1:-1]):
        total = total + jnp.dot(a[...], w[...], preferred_element_type=f32)
    out_ref[...] = total.astype(out_ref.dtype)


def project(normeds, weights, dtype):
    rows, depth = normeds[0].shape
    width = weights[0].shape[1]
    n = len(normeds)
    return call(
        project_kernel, jax.ShapeDtypeStruct((rows, width), dtype), [VMEM] * (2 * n),
        2 * n * rows * depth * width, 2 * n * depth * (rows + width),
    )(*normeds, *weights)


def final_kernel(own_ref, *rest):
    parts, ctx_ref, opt_ref = rest[:-2], rest[-2], rest[-1]
    tokens, (opts, slots, width) = ctx_ref.shape[0], opt_ref.shape
    step = parts[0].shape[1]
    per = width // step
    for c in range(per):
        cols = slice(c * step, (c + 1) * step)
        total = own_ref[:, cols]
        for part in parts[c::per]:
            total = total + part[...].astype(f32)
        total = total.astype(ctx_ref.dtype)
        ctx_ref[:, cols] = total[:tokens]
        for o in range(opts):
            opt_ref[o, :, cols] = total[tokens + o * slots:tokens + (o + 1) * slots]


def ring(value, axis, size, shift):
    return lax.ppermute(value, axis, [(i, (i + shift) % size) for i in range(size)])


def on_device(sizes, q, k, v, oq, ok, ov, offsets, lengths, gain, weight):
    n_seq, n_head, n_sub = sizes
    tokens, feats = q.shape
    opts, slots, _ = oq.shape
    rows = tokens + opts * slots
    heads = feats // DH
    width = weight.shape[1] // (n_head * n_sub)
    place = lax.axis_index("seq")
    head, sub = lax.axis_index("head"), lax.axis_index("sub")

    state = call(
        states_kernel, jax.ShapeDtypeStruct((heads, DH, DH), bf16), [VMEM, VMEM],
        2 * tokens * DH * feats, 8 * tokens * feats,
    )(k, v)

    shifts, parts, window, step = [], [], state, 1
    while step < n_seq:
        now = [s for s in range(step, min(RADIX * step, n_seq), step)]
        got = [ring(window, "seq", n_seq, s) for s in now]
        shifts, parts = shifts + now, parts + got
        step *= RADIX
        if step < n_seq:
            add = window.astype(f32)
            for s, g in zip(now, got):
                add = add + jnp.where(place >= s, g.astype(f32), 0.0)
            window = add.astype(bf16)

    base = call(
        base_kernel, jax.ShapeDtypeStruct((rows, feats), f32), [SMEM] + [VMEM] * 6,
        4 * rows * rows * feats, 16 * rows * feats,
    )(offsets, q, k, v, oq, ok, ov)

    def columns(h, s):
        return lax.dynamic_slice_in_dim(weight, (h * n_sub + s) * width, width, 1)

    targets = [(head + d) % n_head for d in range(n_head)]
    weights = []
    for h in targets:
        ws = [columns(h, sub)]
        for d in range(1, n_sub):
            ws.append(ring(columns(h, (sub + d) % n_sub), "sub", n_sub, d))
        weights.append(ws)

    normed = call(
        functools.partial(normed_kernel, tuple(shifts)), jax.ShapeDtypeStruct((rows, feats), bf16),
        [SMEM, SMEM] + [VMEM] * (4 + len(parts)), 2 * rows * DH * feats, 10 * rows * feats,
    )(place[None], lengths, q, oq, base, gain[None], *parts)
    normeds = [normed] + [ring(normed, "sub", n_sub, d) for d in range(1, n_sub)]

    pieces = 4
    step = width // pieces
    received = []
    for d in range(1, n_head):
        for c in range(pieces):
            out = project(normeds, [w[:, c * step:(c + 1) * step] for w in weights[d]], bf16)
            received.append(ring(out, "head", n_head, d))
    own = project(normeds, weights[0], f32)
    ctx, opt = call(
        final_kernel,
        (jax.ShapeDtypeStruct((tokens, width), bf16), jax.ShapeDtypeStruct((opts, slots, width), bf16)),
        [VMEM] * (1 + len(received)), rows * width, 8 * rows * width,
    )(own, *received)
    return ctx, opt


def solution(mesh):
    placed = (
        P(("grp", "seq"), ("head", "sub")),
        P(("grp", "seq"), ("head", "sub")),
        P(("grp", "seq"), ("head", "sub")),
        P(("grp", "seq"), None, ("head", "sub")),
        P(("grp", "seq"), None, ("head", "sub")),
        P(("grp", "seq"), None, ("head", "sub")),
        P(("grp", "seq")),
        P(("grp", "seq")),
        P(("head", "sub")),
        P(("head", "sub"), None),
    )
    sizes = tuple(mesh.shape[a] for a in ("seq", "head", "sub"))
    return jax.shard_map(
        functools.partial(on_device, sizes),
        mesh=mesh,
        in_specs=placed,
        out_specs=(P(("grp", "seq"), ("head", "sub")), P(("grp", "seq"), None, ("head", "sub"))),
        check_vma=False,
    )
```

time: 92 us -> 44.5 us (0.48)
  blocking collectives: 55.8 us -> 0 us
  matrix products: 13.1 us -> 0 us
  waiting for transfers between devices: 0.01 us -> 12.4 us
  Pallas kernels: 0 us -> 10.8 us
  starting transfers between devices: 4.97 us -> 11.9 us
  local copies, waits for them, and re-layouts: 14.1 us -> 8.07 us
  other arithmetic: 2.58 us -> 0 us
    all_gather x3 -> x0, blocking collectives: 55.8 us -> none  [the longest x1 29.2 us: on_device(): lax.all_gather(opt_normed, ('head', 'sub'), axis=1, tiled=True)]
    dot_general x10 -> x0, matrix products: 13.1 us -> none  [the longest x2 6.22 us: grouped_project(): jnp.einsum('rgk,gkd->grd', flat, weight_groups, preferred_element_type=jn...]
    ppermute x0 -> x10, waiting for transfers between devices: none -> 12.4 us  [ring(): lax.ppermute(value, axis, [(i, (i + shift) % size) for i in range(size)])]
    ppermute x0 -> x10, starting transfers between devices: none -> 11.9 us  [ring(): lax.ppermute(value, axis, [(i, (i + shift) % size) for i in range(size)])]
    pallas_call x0 -> x9, Pallas kernels: none -> 10.8 us  [the longest x1 4.46 us: on_device(): call(base_kernel, jax.ShapeDtypeStruct((rows, feats), f32), [SMEM] + [VME...]
    all_to_all x1 -> x0, local copies, waits for them, and re-layouts: 6.33 us -> none  [on_device(): lax.all_to_all(out_weight, ('head', 'sub'), split_axis=1, concat_axis=0,...]
    all_to_all x1 -> x0, starting transfers between devices: 4.97 us -> none  [on_device(): lax.all_to_all(out_weight, ('head', 'sub'), split_axis=1, concat_axis=0,...]
    unnamed x22 -> x18, local copies, waits for them, and re-layouts: 6.62 us -> 1.92 us
  transfers between devices with their start and end apart: 1 -> 10, of which waited for: 0 -> 5; matrix products, arithmetic and copies ran while one was open for 9% -> 6% of each run, Pallas kernels for 0% -> 22%
where the time goes in v1:
time: 44.5 us; the launch traced here: 44 us
  waiting for transfers between devices  12.4 us (28%)
  starting transfers between devices  11.9 us (27%)
  Pallas kernels  10.8 us (24%)
  local copies, waits for them, and re-layouts  8.07 us (18%)
  between operations  0.84 us (2%)
    ppermute x10, waiting for transfers between devices, ring(): lax.ppermute(value, axis, [(i, (i + shift) % size) for i in range(size)])  12.4 us
    ppermute x10, starting transfers between devices, ring(): lax.ppermute(value, axis, [(i, (i + shift) % size) for i in range(size)])  11.9 us
    pallas_call x1, Pallas kernels, on_device(): call(base_kernel, jax.ShapeDtypeStruct((rows, feats), f32), [SMEM] + [VME...  4.46 us
    dynamic_slice x1, local copies, waits for them, and re-layouts, columns(): return lax.dynamic_slice_in_dim(weight, (h * n_sub + s) * width, width, 1)  3.59 us
    slice x2, local copies, waits for them, and re-layouts, on_device(): w[:, c * step:(c + 1) * step]  2.55 us
    pallas_call x5, Pallas kernels, project(): call(project_kernel, jax.ShapeDtypeStruct((rows, width), dtype), [VMEM] *...  2.2 us
    unnamed x18, local copies, waits for them, and re-layouts  1.92 us
    pallas_call x1, Pallas kernels, on_device(): call(functools.partial(normed_kernel, tuple(shifts)), jax.ShapeDtypeStruc...  1.9 us
  transfers between devices with their start and end apart: 10, of which 5 were waited for; matrix products, arithmetic and copies ran while one was open for 6% of the time, Pallas kernels for 22%

profile of v1, /device:TPU:0, one launch (start us, length us, event | category | flops | bytes accessed | tf_op | source)
XLA Modules:
  0.0 44.0 jit_solution(6645618287238207075)
XLA Ops:
  0.6 0.0 copy-start
  0.6 0.0 copy-start.1
  0.7 0.0 copy-start.2
  0.7 0.0 copy-start.3
  0.7 0.0 copy-start.8
  0.7 0.0 copy-start.6
  0.7 0.0 copy-start.7
  0.7 3.6 %constant_dynamic-slice_fusion.3 = (bf16[512,1024]{1,0:T(8,128)(2,1)}, bf16[512,1024]{1,0:T(8,128)(2,1)}, bf16[512,1024]{1,0:T(8,128)(2,1)S(1)}) fusion(bf16[512,4096]{1,0:T(8,128)(2,1)} %param.19, s32[]{:T(128)S(6)} %select_n.35, s32[]{:T(128)S(6)} %select_n.32, s32[]{:T(128)S(6)} %select_n.30), kind=kLoop, calls=%fused_computation.3 | loop fusion | bytes 6291468 | tf_op jit(solution)/shard_map/dynamic_slice | solution.py:163
  4.3 0.5 %collective-permute-start.5 = (bf16[512,1024]{1,0:T(8,128)(2,1)}, bf16[512,1024]{1,0:T(8,128)(2,1)}, u32[]{:S(2)}, u32[]{:S(2)}) collective-permute-start(bf16[512,1024]{1,0:T(8,128)(2,1)} %get-tuple-element.6), channel_id=1, source_target_pairs={{0,1},{1,0},{2,3},{3,2},{4,5},{5,4},{6,7},{7,6},{8,9},{9,8},{10,11... | collective-permute-start | bytes 3145736 | tf_op jit(solution)/shard_map/ppermute | solution.py:127
  4.8 0.1 collective-permute-start.4
  4.9 0.0 copy-done
  4.9 0.0 copy-done.1
  4.9 1.3 %shard_map.114 = bf16[4,128,128]{2,1,0:T(8,128)(2,1)} custom-call(f32[192,512]{1,0:T(8,128)S(1)} %copy-done, f32[192,512]{1,0:T(8,128)S(1)} %copy-done.1), custom_call_target="tpu_custom_call" | custom-call | flops 25165824 | bytes 786432 | tf_op jit(solution)/shard_map/pallas_call | solution.py:140
  6.2 3.0 %collective-permute-start = (bf16[4,128,128]{2,1,0:T(8,128)(2,1)}, bf16[4,128,128]{2,1,0:T(8,128)(2,1)}, u32[]{:S(2)}, u32[]{:S(2)}) collective-permute-start(bf16[4,128,128]{2,1,0:T(8,128)(2,1)} %shard_map.114), channel_id=1, source_target_pairs={{0,4},{4,8},{8,12},{12,0},{1,5},{5,9},{9,13},{13,1},{2,6},{6,10},{... | collective-permute-start | bytes 393224 | tf_op jit(solution)/shard_map/ppermute | solution.py:127
  9.2 2.6 %collective-permute-start.1 = (bf16[4,128,128]{2,1,0:T(8,128)(2,1)}, bf16[4,128,128]{2,1,0:T(8,128)(2,1)}, u32[]{:S(2)}, u32[]{:S(2)}) collective-permute-start(bf16[4,128,128]{2,1,0:T(8,128)(2,1)} %shard_map.114), channel_id=1, source_target_pairs={{0,8},{4,12},{8,0},{12,4},{1,9},{5,13},{9,1},{13,5},{2,10},{6,14},... | collective-permute-start | bytes 393224 | tf_op jit(solution)/shard_map/ppermute | solution.py:127
  11.8 1.3 %collective-permute-start.2 = (bf16[4,128,128]{2,1,0:T(8,128)(2,1)}, bf16[4,128,128]{2,1,0:T(8,128)(2,1)}, u32[]{:S(2)}, u32[]{:S(2)}) collective-permute-start(bf16[4,128,128]{2,1,0:T(8,128)(2,1)} %shard_map.114), channel_id=1, source_target_pairs={{0,12},{4,0},{8,4},{12,8},{1,13},{5,1},{9,5},{13,9},{2,14},{6,2},{... | collective-permute-start | bytes 393224 | tf_op jit(solution)/shard_map/ppermute | solution.py:127
  13.1 0.0 copy-done.2
  13.1 0.0 copy-done.3
  13.1 0.0 copy-done.8
  13.1 0.0 copy-start.4
  13.2 0.9 %copy-done.4 = f32[2,64,512]{2,1,0:T(8,128)S(1)} copy-done((f32[2,64,512]{2,1,0:T(8,128)S(1)}, f32[2,64,512]{2,1,0:T(8,128)}, u32[]{:S(2)}) %copy-start.4) | copy-done | bytes 262168
  14.1 0.0 copy-start.5
  14.1 0.9 %copy-done.5 = f32[2,64,512]{2,1,0:T(8,128)S(1)} copy-done((f32[2,64,512]{2,1,0:T(8,128)S(1)}, f32[2,64,512]{2,1,0:T(8,128)}, u32[]{:S(2)}) %copy-start.5) | copy-done | bytes 262168
  15.1 4.5 %shard_map.113.base_ref = f32[320,512]{1,0:T(8,128)S(1)} custom-call(s32[2]{0:T(128)S(1)} %copy-done.8, f32[192,512]{1,0:T(8,128)S(1)} %copy-done.2, f32[192,512]{1,0:T(8,128)S(1)} %copy-done, f32[192,512]{1,0:T(8,128)S(1)} %copy-done.1, f32[2,64,512]{2,1,0:T(8,128)S(1)} %copy-done.3, f32[2,64,512]{2,1,0:T(8,128)S(1)} %copy-done.4, f32[2,64,512]{2,1,0:T(8,128)S(1)} %copy-done.5), custom_call_target="tpu_custom_call" | custom-call | flops 209715200 | bytes 2621440 | tf_op jit(solution)/shard_map/pallas_call | solution.py:157
  19.5 0.0 collective-permute-done.rest_0_
  19.5 1.4 %collective-permute-done.1.rest_1_ = bf16[4,128,128]{2,1,0:T(8,128)(2,1)} collective-permute-done((bf16[4,128,128]{2,1,0:T(8,128)(2,1)}, bf16[4,128,128]{2,1,0:T(8,128)(2,1)}, u32[]{:S(2)}, u32[]{:S(2)}) %collective-permute-start.1) | collective-permute-done | bytes 131104 | tf_op jit(solution)/shard_map/ppermute | solution.py:127
  20.9 0.0 collective-permute-done.2.rest_2_
  20.9 0.0 copy-done.6
  20.9 0.0 copy-done.7
  20.9 1.9 %shard_map.115.refs_0_ = bf16[320,512]{1,0:T(8,128)(2,1)S(1)} custom-call(s32[1]{0:T(128)} %bitcast.place_ref, s32[2]{0:T(128)S(1)} %copy-done.7, f32[192,512]{1,0:T(8,128)S(1)} %copy-done.2, f32[2,64,512]{2,1,0:T(8,128)S(1)} %copy-done.3, f32[320,512]{1,0:T(8,128)S(1)} %shard_map.113.base_ref, f32[1,512]{1,0:T(1,128)S(1)} %bitcast.2, ...), custom_call_target="tpu_custom_call" | custom-call | flops 41943040 | bytes 1638400 | tf_op jit(solution)/shard_map/pallas_call | solution.py:173
  22.8 0.1 collective-permute-start.3
  22.9 1.3 %constant_dynamic-slice_fusion.4 = (bf16[512,256]{1,0:T(8,128)(2,1)S(1)}, bf16[512,256]{1,0:T(8,128)(2,1)S(1)}, bf16[512,256]{1,0:T(8,128)(2,1)S(1)}, bf16[512,256]{1,0:T(8,128)(2,1)S(1)}) fusion(bf16[512,4096]{1,0:T(8,128)(2,1)} %param.19, s32[]{:T(128)S(6)} %add.57, s32[]{:T(128)S(6)} %add.56, s32[]{:T(128)S(6)} %add.55, s32[]{:T(128)S(6)} %select_n.34), kind=kLoop, calls=%fused_computation.4 | loop fusion | bytes 2097168 | tf_op jit(solution)/shard_map/slice | solution.py:184
  24.2 0.0 collective-permute-done.5
  24.2 1.3 %fusion = (bf16[512,256]{1,0:T(8,128)(2,1)S(1)}, bf16[512,256]{1,0:T(8,128)(2,1)S(1)}, bf16[512,256]{1,0:T(8,128)(2,1)S(1)}, bf16[512,256]{1,0:T(8,128)(2,1)S(1)}) fusion(bf16[512,1024]{1,0:T(8,128)(2,1)} %collective-permute-done.5), kind=kLoop, calls=%fused_computation.7 | loop fusion | bytes 2097152 | tf_op jit(solution)/shard_map/slice | solution.py:184
  25.5 0.0 collective-permute-done.3.refs_1_
  25.5 0.3 shard_map.117
  25.8 1.6 %collective-permute-start.6 = (bf16[320,256]{1,0:T(8,128)(2,1)S(1)}, bf16[320,256]{1,0:T(8,128)(2,1)S(1)}, u32[]{:S(2)}, u32[]{:S(2)}) collective-permute-start(bf16[320,256]{1,0:T(8,128)(2,1)S(1)} %shard_map.117), channel_id=1, source_target_pairs={{0,2},{2,0},{1,3},{3,1},{4,6},{6,4},{5,7},{7,5},{8,10},{10,8},{9,1... | collective-permute-start | bytes 491528 | tf_op jit(solution)/shard_map/ppermute | solution.py:127
  27.4 0.3 shard_map.118
  27.7 0.6 %collective-permute-start.7 = (bf16[320,256]{1,0:T(8,128)(2,1)S(1)}, bf16[320,256]{1,0:T(8,128)(2,1)S(1)}, u32[]{:S(2)}, u32[]{:S(2)}) collective-permute-start(bf16[320,256]{1,0:T(8,128)(2,1)S(1)} %shard_map.118), channel_id=1, source_target_pairs={{0,2},{2,0},{1,3},{3,1},{4,6},{6,4},{5,7},{7,5},{8,10},{10,8},{9,1... | collective-permute-start | bytes 491528 | tf_op jit(solution)/shard_map/ppermute | solution.py:127
  28.3 0.3 shard_map.119
  28.7 1.6 %collective-permute-start.8 = (bf16[320,256]{1,0:T(8,128)(2,1)S(1)}, bf16[320,256]{1,0:T(8,128)(2,1)S(1)}, u32[]{:S(2)}, u32[]{:S(2)}) collective-permute-start(bf16[320,256]{1,0:T(8,128)(2,1)S(1)} %shard_map.119), channel_id=1, source_target_pairs={{0,2},{2,0},{1,3},{3,1},{4,6},{6,4},{5,7},{7,5},{8,10},{10,8},{9,1... | collective-permute-start | bytes 491528 | tf_op jit(solution)/shard_map/ppermute | solution.py:127
  30.2 0.3 shard_map.120
  30.6 0.6 %collective-permute-start.9 = (bf16[320,256]{1,0:T(8,128)(2,1)S(1)}, bf16[320,256]{1,0:T(8,128)(2,1)S(1)}, u32[]{:S(2)}, u32[]{:S(2)}) collective-permute-start(bf16[320,256]{1,0:T(8,128)(2,1)S(1)} %shard_map.120), channel_id=1, source_target_pairs={{0,2},{2,0},{1,3},{3,1},{4,6},{6,4},{5,7},{7,5},{8,10},{10,8},{9,1... | collective-permute-start | bytes 491528 | tf_op jit(solution)/shard_map/ppermute | solution.py:127
  31.2 0.0 collective-permute-done.4.refs_3_
  31.2 0.9 %shard_map.116.own_ref = f32[320,1024]{1,0:T(8,128)S(1)} custom-call(bf16[320,512]{1,0:T(8,128)(2,1)S(1)} %shard_map.115.refs_0_, bf16[320,512]{1,0:T(8,128)(2,1)S(1)} %collective-permute-done.3.refs_1_, bf16[512,1024]{1,0:T(8,128)(2,1)S(1)} %get-tuple-element.8.refs_2_, bf16[512,1024]{1,0:T(8,128)(2,1)S(1)} %collective-permute-done.4.refs_3_), custom_call_target="tpu_custom_call" | custom-call | flops 671088640 | bytes 2752512 | tf_op jit(solution)/shard_map/pallas_call | solution.py:104
  32.0 0.8 %collective-permute-done.6.rest_0_ = bf16[320,256]{1,0:T(8,128)(2,1)S(1)} collective-permute-done((bf16[320,256]{1,0:T(8,128)(2,1)S(1)}, bf16[320,256]{1,0:T(8,128)(2,1)S(1)}, u32[]{:S(2)}, u32[]{:S(2)}) %collective-permute-start.6) | collective-permute-done | bytes 163872 | tf_op jit(solution)/shard_map/ppermute | solution.py:127
  32.9 3.5 %collective-permute-done.7.rest_1_ = bf16[320,256]{1,0:T(8,128)(2,1)S(1)} collective-permute-done((bf16[320,256]{1,0:T(8,128)(2,1)S(1)}, bf16[320,256]{1,0:T(8,128)(2,1)S(1)}, u32[]{:S(2)}, u32[]{:S(2)}) %collective-permute-start.7) | collective-permute-done | bytes 163872 | tf_op jit(solution)/shard_map/ppermute | solution.py:127
  36.4 3.5 %collective-permute-done.8.rest_2_ = bf16[320,256]{1,0:T(8,128)(2,1)S(1)} collective-permute-done((bf16[320,256]{1,0:T(8,128)(2,1)S(1)}, bf16[320,256]{1,0:T(8,128)(2,1)S(1)}, u32[]{:S(2)}, u32[]{:S(2)}) %collective-permute-start.8) | collective-permute-done | bytes 163872 | tf_op jit(solution)/shard_map/ppermute | solution.py:127
  39.9 3.1 %collective-permute-done.9.rest_3_ = bf16[320,256]{1,0:T(8,128)(2,1)S(1)} collective-permute-done((bf16[320,256]{1,0:T(8,128)(2,1)S(1)}, bf16[320,256]{1,0:T(8,128)(2,1)S(1)}, u32[]{:S(2)}, u32[]{:S(2)}) %collective-permute-start.9) | collective-permute-done | bytes 163872 | tf_op jit(solution)/shard_map/ppermute | solution.py:127
  43.0 0.9 %shard_map.121 = (bf16[192,1024]{1,0:T(8,128)(2,1)}, bf16[2,64,1024]{2,1,0:T(8,128)(2,1)}) custom-call(f32[320,1024]{1,0:T(8,128)S(1)} %shard_map.116.own_ref, bf16[320,256]{1,0:T(8,128)(2,1)S(1)} %collective-permute-done.6.rest_0_, bf16[320,256]{1,0:T(8,128)(2,1)S(1)} %collective-permute-done.7.rest_1_, ...), custom_call_target="tpu_custom_call" | custom-call | flops 327680 | bytes 2621440 | tf_op jit(solution)/shard_map/pallas_call | solution.py:187
Async XLA Ops:
  0.6 4.2 %copy-start = (f32[192,512]{1,0:T(8,128)S(1)}, f32[192,512]{1,0:T(8,128)}, u32[]{:S(2)}) copy-start(f32[192,512]{1,0:T(8,128)} %k_ref.3) | copy-start | bytes 1179652
  0.6 4.2 %copy-start.1 = (f32[192,512]{1,0:T(8,128)S(1)}, f32[192,512]{1,0:T(8,128)}, u32[]{:S(2)}) copy-start(f32[192,512]{1,0:T(8,128)} %v_ref.3) | copy-start | bytes 1179652
  0.7 12.5 %copy-start.2 = (f32[192,512]{1,0:T(8,128)S(1)}, f32[192,512]{1,0:T(8,128)}, u32[]{:S(2)}) copy-start(f32[192,512]{1,0:T(8,128)} %q_ref.3) | copy-start | bytes 1179652
  0.7 12.5 %copy-start.3 = (f32[2,64,512]{2,1,0:T(8,128)S(1)}, f32[2,64,512]{2,1,0:T(8,128)}, u32[]{:S(2)}) copy-start(f32[2,64,512]{2,1,0:T(8,128)} %oq_ref.3) | copy-start | bytes 786436
  0.7 12.5 %copy-start.8 = (s32[2]{0:T(128)S(1)}, s32[2]{0:T(128)}, u32[]{:S(2)}) copy-start(s32[2]{0:T(128)} %offsets_ref.1) | copy-start | bytes 28
  0.7 20.2 %copy-start.6 = (f32[512]{0:T(512)S(1)}, f32[512]{0:T(512)}, u32[]{:S(2)}) copy-start(f32[512]{0:T(512)} %param.18) | copy-start | bytes 6148
  0.7 20.2 %copy-start.7 = (s32[2]{0:T(128)S(1)}, s32[2]{0:T(128)}, u32[]{:S(2)}) copy-start(s32[2]{0:T(128)} %lengths_ref.1) | copy-start | bytes 28
  4.3 19.9 %collective-permute-start.5 = (bf16[512,1024]{1,0:T(8,128)(2,1)}, bf16[512,1024]{1,0:T(8,128)(2,1)}, u32[]{:S(2)}, u32[]{:S(2)}) collective-permute-start(bf16[512,1024]{1,0:T(8,128)(2,1)} %get-tuple-element.6), channel_id=1, source_target_pairs={{0,1},{1,0},{2,3},{3,2},{4,5},{5,4},{6,7},{7,6},{8,9},{9,8},{10,11... | collective-permute-start | bytes 3145736 | tf_op jit(solution)/shard_map/ppermute | solution.py:127
  4.8 26.4 %collective-permute-start.4 = (bf16[512,1024]{1,0:T(8,128)(2,1)}, bf16[512,1024]{1,0:T(8,128)(2,1)S(1)}, u32[]{:S(2)}, u32[]{:S(2)}) collective-permute-start(bf16[512,1024]{1,0:T(8,128)(2,1)} %get-tuple-element.7), channel_id=1, source_target_pairs={{0,1},{1,0},{2,3},{3,2},{4,5},{5,4},{6,7},{7,6},{8,9},{9,8},{10,11... | collective-permute-start | bytes 3145736 | tf_op jit(solution)/shard_map/ppermute | solution.py:127
  6.2 13.3 %collective-permute-start = (bf16[4,128,128]{2,1,0:T(8,128)(2,1)}, bf16[4,128,128]{2,1,0:T(8,128)(2,1)}, u32[]{:S(2)}, u32[]{:S(2)}) collective-permute-start(bf16[4,128,128]{2,1,0:T(8,128)(2,1)} %shard_map.114), channel_id=1, source_target_pairs={{0,4},{4,8},{8,12},{12,0},{1,5},{5,9},{9,13},{13,1},{2,6},{6,10},{... | collective-permute-start | bytes 393224 | tf_op jit(solution)/shard_map/ppermute | solution.py:127
  9.2 11.7 %collective-permute-start.1 = (bf16[4,128,128]{2,1,0:T(8,128)(2,1)}, bf16[4,128,128]{2,1,0:T(8,128)(2,1)}, u32[]{:S(2)}, u32[]{:S(2)}) collective-permute-start(bf16[4,128,128]{2,1,0:T(8,128)(2,1)} %shard_map.114), channel_id=1, source_target_pairs={{0,8},{4,12},{8,0},{12,4},{1,9},{5,13},{9,1},{13,5},{2,10},{6,14},... | collective-permute-start | bytes 393224 | tf_op jit(solution)/shard_map/ppermute | solution.py:127
  11.8 9.1 %collective-permute-start.2 = (bf16[4,128,128]{2,1,0:T(8,128)(2,1)}, bf16[4,128,128]{2,1,0:T(8,128)(2,1)}, u32[]{:S(2)}, u32[]{:S(2)}) collective-permute-start(bf16[4,128,128]{2,1,0:T(8,128)(2,1)} %shard_map.114), channel_id=1, source_target_pairs={{0,12},{4,0},{8,4},{12,8},{1,13},{5,1},{9,5},{13,9},{2,14},{6,2},{... | collective-permute-start | bytes 393224 | tf_op jit(solution)/shard_map/ppermute | solution.py:127
  13.1 1.0 %copy-start.4 = (f32[2,64,512]{2,1,0:T(8,128)S(1)}, f32[2,64,512]{2,1,0:T(8,128)}, u32[]{:S(2)}) copy-start(f32[2,64,512]{2,1,0:T(8,128)} %ok_ref.1) | copy-start | bytes 786436
  14.1 0.9 %copy-start.5 = (f32[2,64,512]{2,1,0:T(8,128)S(1)}, f32[2,64,512]{2,1,0:T(8,128)}, u32[]{:S(2)}) copy-start(f32[2,64,512]{2,1,0:T(8,128)} %ov_ref.1) | copy-start | bytes 786436
  22.8 2.7 %collective-permute-start.3 = (bf16[320,512]{1,0:T(8,128)(2,1)S(1)}, bf16[320,512]{1,0:T(8,128)(2,1)S(1)}, u32[]{:S(2)}, u32[]{:S(2)}) collective-permute-start(bf16[320,512]{1,0:T(8,128)(2,1)S(1)} %shard_map.115.refs_0_), channel_id=1, source_target_pairs={{0,1},{1,0},{2,3},{3,2},{4,5},{5,4},{6,7},{7,6},{8,9},{9,8},{10,11... | collective-permute-start | bytes 983048 | tf_op jit(solution)/shard_map/ppermute | solution.py:127
  25.8 7.1 %collective-permute-start.6 = (bf16[320,256]{1,0:T(8,128)(2,1)S(1)}, bf16[320,256]{1,0:T(8,128)(2,1)S(1)}, u32[]{:S(2)}, u32[]{:S(2)}) collective-permute-start(bf16[320,256]{1,0:T(8,128)(2,1)S(1)} %shard_map.117), channel_id=1, source_target_pairs={{0,2},{2,0},{1,3},{3,1},{4,6},{6,4},{5,7},{7,5},{8,10},{10,8},{9,1... | collective-permute-start | bytes 491528 | tf_op jit(solution)/shard_map/ppermute | solution.py:127
  27.7 8.7 %collective-permute-start.7 = (bf16[320,256]{1,0:T(8,128)(2,1)S(1)}, bf16[320,256]{1,0:T(8,128)(2,1)S(1)}, u32[]{:S(2)}, u32[]{:S(2)}) collective-permute-start(bf16[320,256]{1,0:T(8,128)(2,1)S(1)} %shard_map.118), channel_id=1, source_target_pairs={{0,2},{2,0},{1,3},{3,1},{4,6},{6,4},{5,7},{7,5},{8,10},{10,8},{9,1... | collective-permute-start | bytes 491528 | tf_op jit(solution)/shard_map/ppermute | solution.py:127
  28.7 11.2 %collective-permute-start.8 = (bf16[320,256]{1,0:T(8,128)(2,1)S(1)}, bf16[320,256]{1,0:T(8,128)(2,1)S(1)}, u32[]{:S(2)}, u32[]{:S(2)}) collective-permute-start(bf16[320,256]{1,0:T(8,128)(2,1)S(1)} %shard_map.119), channel_id=1, source_target_pairs={{0,2},{2,0},{1,3},{3,1},{4,6},{6,4},{5,7},{7,5},{8,10},{10,8},{9,1... | collective-permute-start | bytes 491528 | tf_op jit(solution)/shard_map/ppermute | solution.py:127
  30.6 12.4 %collective-permute-start.9 = (bf16[320,256]{1,0:T(8,128)(2,1)S(1)}, bf16[320,256]{1,0:T(8,128)(2,1)S(1)}, u32[]{:S(2)}, u32[]{:S(2)}) collective-permute-start(bf16[320,256]{1,0:T(8,128)(2,1)S(1)} %shard_map.120), channel_id=1, source_target_pairs={{0,2},{2,0},{1,3},{3,1},{4,6},{6,4},{5,7},{7,5},{8,10},{10,8},{9,1... | collective-permute-start | bytes 491528 | tf_op jit(solution)/shard_map/ppermute | solution.py:127

commit v2 on v1

v2 whole, which is shorter than its diff:
```python
import functools

import jax
import jax.numpy as jnp
from jax import lax
from jax.experimental import pallas as pl
from jax.experimental.pallas import tpu as pltpu
from jax.sharding import PartitionSpec as P

DH = 128
EPS = 1e-05
SPANS = ((0, 2), (2, 3), (3, 4))
f32 = jnp.float32
bf16 = jnp.bfloat16
HIGHEST = lax.Precision.HIGHEST
VMEM_LIMIT = 32 * 1024 * 1024

VMEM = pl.BlockSpec(memory_space=pltpu.VMEM)
SMEM = pl.BlockSpec(memory_space=pltpu.SMEM)
HBM = pl.BlockSpec(memory_space=pltpu.HBM)
ANY = pl.BlockSpec(memory_space=pl.ANY)
Shape = jax.ShapeDtypeStruct


def call(body, out_shape, specs, flops, nbytes, out_specs=None, limit=VMEM_LIMIT, **more):
    single = not isinstance(out_shape, (tuple, list))
    if out_specs is None:
        out_specs = VMEM if single else [VMEM] * len(out_shape)
    return pl.pallas_call(
        body,
        out_shape=out_shape,
        in_specs=specs,
        out_specs=out_specs,
        compiler_params=pltpu.CompilerParams(vmem_limit_bytes=limit),
        cost_estimate=pl.CostEstimate(flops=flops, bytes_accessed=nbytes, transcendentals=0),
        **more,
    )


def columns(h):
    return slice(h * DH, (h + 1) * DH)


def halves(x):
    high = x.astype(bf16)
    return high, (x - high.astype(f32)).astype(bf16)


def dot3(a, b, dims):
    (ah, al), (bh, bl) = a, b
    dot = functools.partial(lax.dot_general, dimension_numbers=(dims, ((), ())), preferred_element_type=f32)
    return dot(ah, bh) + (dot(ah, bl) + dot(al, bh))


def base_kernel(tokens, offsets_ref, qh, ql, kh, kl, vh, vl, after_ref, out_ref):
    rows, opts = out_ref.shape[0], offsets_ref.shape[0]
    slots = (rows - tokens) // opts
    i = lax.broadcasted_iota(jnp.int32, (rows, rows), 0)
    j = lax.broadcasted_iota(jnp.int32, (rows, rows), 1)
    limit, first = i + 1, jnp.full((rows, rows), rows, jnp.int32)
    for o in range(opts):
        own = i >= tokens + o * slots
        limit = jnp.where(own, offsets_ref[o], limit)
        first = jnp.where(own, tokens + o * slots, first)
    mask = (j < limit) | ((j >= first) & (j <= i))
    for h in range(out_ref.shape[1] // DH):
        cols = columns(h)
        scores = dot3((qh[:, cols], ql[:, cols]), (kh[:, cols], kl[:, cols]), ((1,), (1,)))
        scores = halves(jnp.where(mask, scores, 0.0))
        out_ref[:, cols] = dot3(scores, (vh[:, cols], vl[:, cols]), ((1,), (0,)))


def add_kernel(*refs):
    total = refs[0][...].astype(f32)
    for ref in refs[1:-1]:
        total = total + ref[...].astype(f32)
    refs[-1][...] = total.astype(refs[-1].dtype)


def add(*terms):
    return call(
        add_kernel, Shape(terms[0].shape, bf16), [VMEM] * len(terms),
        len(terms) * terms[0].size, 6 * len(terms) * terms[0].size,
    )(*terms)


def normed_kernel(tokens, use_ref, lengths_ref, qh, ql, base_ref, gain_ref, *rest):
    parts, out_ref = rest[:-1], rest[-1]
    (rows, feats), opts = out_ref.shape, lengths_ref.shape[0]
    slots = (rows - tokens) // opts
    row = lax.broadcasted_iota(jnp.int32, (rows, 1), 0)
    valid = row < tokens
    for o in range(opts):
        start = tokens + o * slots
        valid = valid | ((row >= start) & (row < start + lengths_ref[o]))
    for h in range(feats // DH):
        prefix = jnp.zeros((DH, DH), f32)
        for n, part in enumerate(parts):
            prefix = prefix + jnp.where(use_ref[n] > 0, part[h].astype(f32), 0.0)
        cols = columns(h)
        out = base_ref[:, cols] + dot3((qh[:, cols], ql[:, cols]), halves(prefix), ((1,), (0,)))
        scale = lax.rsqrt(jnp.mean(out * out, axis=1, keepdims=True) + EPS)
        out_ref[:, cols] = jnp.where(valid, out * scale * gain_ref[:, cols], 0.0).astype(out_ref.dtype)


def project_kernel(spans, rows_ref, weight_ref, *outs):
    for (start, end), out in zip(spans, outs):
        out[...] = jnp.dot(rows_ref[...], weight_ref[:, start:end], preferred_element_type=f32).astype(out.dtype)


def project(rows, weight, spans, dtype):
    count, (depth, width) = rows.shape[0], weight.shape
    return call(
        functools.partial(project_kernel, spans), [Shape((count, b - a), dtype) for a, b in spans], [VMEM] * 2,
        2 * count * depth * width, 2 * depth * (count + width) + 4 * count * width,
    )(rows, weight)


def final_kernel(spans, per, *rest):
    terms, (ctx_ref, opt_ref, buf, sem) = rest[:per * len(spans)], rest[-4:]
    tokens, (opts, slots, width) = ctx_ref.shape[0], opt_ref.shape
    low, high = spans[0][0], spans[-1][1]
    for c, (start, end) in enumerate(spans):
        total = terms[c * per][...].astype(f32)
        for term in terms[c * per + 1:(c + 1) * per]:
            total = total + term[...].astype(f32)
        buf[:, start - low:end - low] = total.astype(buf.dtype)
    copies = [pltpu.make_async_copy(buf.at[:tokens], ctx_ref.at[:, low:high], sem.at[0])]
    for o in range(opts):
        start = tokens + o * slots
        copies.append(pltpu.make_async_copy(buf.at[start:start + slots], opt_ref.at[o, :, low:high], sem.at[o + 1]))
    for copy in copies:
        copy.start()
    for copy in copies:
        copy.wait()


def final(spans, terms, shapes, before=()):
    flat = sum(terms, [])
    rows, width, opts, n = flat[0].shape[0], spans[-1][1] - spans[0][0], shapes[1].shape[0], len(flat)
    return call(
        functools.partial(final_kernel, spans, len(terms[0])), shapes, [VMEM] * n + [HBM] * len(before),
        rows * width * n, 4 * rows * width * n, out_specs=[HBM, HBM],
        input_output_aliases={n: 0, n + 1: 1} if before else {},
        scratch_shapes=[pltpu.VMEM((rows, width), bf16), pltpu.SemaphoreType.DMA((1 + opts,))],
    )(*flat, *before)


def ring(value, axis, size, shift):
    return lax.ppermute(value, axis, [(i, (i + shift) % size) for i in range(size)])


def swap(value, axis, size, mask):
    return lax.ppermute(value, axis, [(i, i ^ mask) for i in range(size)])


def exclusive(state, axis, size):
    place = lax.axis_index(axis)
    parts, use, windows, step = [], [], [state], 1
    while step < size:
        parts.append(swap(windows[-1], axis, size, step))
        use.append(place & step != 0)
        step *= 2
        if step < size:
            windows.append(add(windows[-1], parts[-1]))
    return parts, jnp.stack(use).astype(jnp.int32), windows[:2][-1]


def on_device(sizes, q, k, v, oq, ok, ov, offsets, lengths, gain, weight):
    n_seq, n_head, n_sub = sizes
    tokens, feats = q.shape
    opts, slots, _ = oq.shape
    rows = tokens + opts * slots
    heads = feats // DH
    width = weight.shape[1] // (n_head * n_sub)
    head, sub = lax.axis_index("head"), lax.axis_index("sub")

    state = jnp.einsum(
        "thd,the->hde", k.reshape(tokens, heads, DH), v.reshape(tokens, heads, DH), precision=lax.Precision.DEFAULT
    ).astype(bf16)
    parts, use, window = exclusive(state, "seq", n_seq)

    q, k, v, oq, ok, ov, _ = lax.optimization_barrier((q, k, v, oq, ok, ov, state))
    halved = [halves(jnp.concatenate([x, y.reshape(-1, feats)])) for x, y in ((q, oq), (k, ok), (v, ov))]
    base = call(
        functools.partial(base_kernel, tokens), Shape((rows, feats), f32), [SMEM] + [VMEM] * 6 + [ANY],
        12 * rows * rows * feats, 16 * rows * feats,
    )(offsets, *sum(halved, ()), window)
    normed = call(
        functools.partial(normed_kernel, tokens), Shape((rows, feats), bf16),
        [SMEM, SMEM] + [VMEM] * (4 + len(parts)), 6 * rows * DH * feats, 10 * rows * feats,
    )(use, lengths, *halved[0], base, gain[None], *parts)

    def blocks(d):
        at = [((head + d) % n_head * n_sub + (sub + s) % n_sub) * width for s in range(n_sub)]
        return [lax.dynamic_slice_in_dim(later, x, width, 1) for x in at]

    def summed(d, spans):
        ours, *theirs = weights[d]
        theirs = [project(normed, w, spans, bf16) for w in theirs]
        ours = project(normed, ours, spans, f32)
        theirs = [[ring(x, "sub", n_sub, s + 1) for x in xs] for s, xs in enumerate(theirs)]
        return list(zip(ours, *theirs))

    later, _ = lax.optimization_barrier((weight, window))
    weights = [blocks(d) for d in range(n_head)]
    spans = [(width * a // 4, width * b // 4) for a, b in SPANS]
    received = {}
    for d in range(1, n_head):
        for span, terms in zip(spans, summed(d, spans)):
            received[d, span] = ring(add(*terms), "head", n_head, d)
    own = dict(zip(spans, summed(0, spans)))
    shapes = (Shape((tokens, width), bf16), Shape((opts, slots, width), bf16))
    out = ()
    for some in (spans[:-1], spans[-1:]):
        terms = [[*own[span]] + [received[d, span] for d in range(1, n_head)] for span in some]
        out = final(some, terms, shapes, out)
    return tuple(out)


def solution(mesh):
    placed = (
        P(("grp", "seq"), ("head", "sub")),
        P(("grp", "seq"), ("head", "sub")),
        P(("grp", "seq"), ("head", "sub")),
        P(("grp", "seq"), None, ("head", "sub")),
        P(("grp", "seq"), None, ("head", "sub")),
        P(("grp", "seq"), None, ("head", "sub")),
        P(("grp", "seq")),
        P(("grp", "seq")),
        P(("head", "sub")),
        P(("head", "sub"), None),
    )
    sizes = tuple(mesh.shape[a] for a in ("seq", "head", "sub"))
    return jax.shard_map(
        functools.partial(on_device, sizes),
        mesh=mesh,
        in_specs=placed,
        out_specs=(P(("grp", "seq"), ("head", "sub")), P(("grp", "seq"), None, ("head", "sub"))),
        check_vma=False,
    )
```

time: 44.5 us -> 39.6 us (0.89)
  local copies, waits for them, and re-layouts: 8.07 us -> 2.67 us
  other arithmetic: 0 us -> 3.83 us
  Pallas kernels: 10.8 us -> 7.67 us
  starting transfers between devices: 11.9 us -> 10.4 us
  matrix products: 0 us -> 1.48 us
    ppermute x10 -> x9, starting transfers between devices: 11.9 us -> 4.67 us  [ring(): lax.ppermute(value, axis, [(i, (i + shift) % size) for i in range(size)])]
    ppermute x0 -> x2, starting transfers between devices: none -> 5.74 us  [swap(): return lax.ppermute(value, axis, [(i, i ^ mask) for i in range(size)])]
    convert_element_type x0 -> x5, other arithmetic: none -> 3.83 us  [the longest x2 2.55 us: halves(): return (high, (x - high.astype(f32)).astype(bf16))]
    pallas_call x9 -> x12, Pallas kernels: 10.8 us -> 7.67 us  [the longest x1 2.74 us: on_device(): call(functools.partial(base_kernel, tokens), Shape((rows, feats), f32), [...]
    slice x2 -> x0, local copies, waits for them, and re-layouts: 2.55 us -> none  [on_device(): w[:, c * step:(c + 1) * step]]
    unnamed x18 -> x14, local copies, waits for them, and re-layouts: 1.92 us -> 0.04 us
    dot_general x0 -> x1, matrix products: none -> 1.48 us  [on_device(): jnp.einsum('thd,the->hde', k.reshape(tokens, heads, DH), v.reshape(tokens...]
    dynamic_slice x1, local copies, waits for them, and re-layouts: 3.59 us -> 2.62 us  [blocks(): return [lax.dynamic_slice_in_dim(later, x, width, 1) for x in at]]
  transfers between devices with their start and end apart: 10 -> 11, of which waited for: 5 -> 4; matrix products, arithmetic and copies ran while one was open for 6% -> 16% of each run, Pallas kernels for 22% -> 13%
where the time goes in v2:
time: 39.6 us; the launch traced here: 39.3 us
  waiting for transfers between devices  12.3 us (31%)
  starting transfers between devices  10.4 us (26%)
  Pallas kernels  7.67 us (19%)
  other arithmetic  3.83 us (10%)
  local copies, waits for them, and re-layouts  2.67 us (7%)
  matrix products  1.48 us (4%)
  between operations  0.93 us (2%)
    ppermute x9, waiting for transfers between devices, ring(): lax.ppermute(value, axis, [(i, (i + shift) % size) for i in range(size)])  11.6 us
    ppermute x2, starting transfers between devices, swap(): return lax.ppermute(value, axis, [(i, i ^ mask) for i in range(size)])  5.74 us
    ppermute x9, starting transfers between devices, ring(): lax.ppermute(value, axis, [(i, (i + shift) % size) for i in range(size)])  4.67 us
    pallas_call x1, Pallas kernels, on_device(): call(functools.partial(base_kernel, tokens), Shape((rows, feats), f32), [...  2.74 us
    dynamic_slice x1, local copies, waits for them, and re-layouts, blocks(): return [lax.dynamic_slice_in_dim(later, x, width, 1) for x in at]  2.62 us
    convert_element_type x2, other arithmetic, halves(): return (high, (x - high.astype(f32)).astype(bf16))  2.55 us
    pallas_call x4, Pallas kernels, project(): call(functools.partial(project_kernel, spans), [Shape((count, b - a), dty...  2 us
    pallas_call x2, Pallas kernels, final(): call(functools.partial(final_kernel, spans, len(terms[0])), shapes, [VMEM...  1.68 us
  transfers between devices with their start and end apart: 11, of which 4 were waited for; matrix products, arithmetic and copies ran while one was open for 16% of the time, Pallas kernels for 13%

profile of v2, /device:TPU:0, one launch (start us, length us, event | category | flops | bytes accessed | tf_op | source)
XLA Modules:
  0.0 39.3 jit_solution(1226403858580496683)
XLA Ops:
  0.6 0.0 copy-start.3
  0.6 0.0 copy-start.4
  0.7 0.0 copy-start.5
  0.7 0.0 copy-start.6
  0.7 1.5 %convolution_convert_fusion.refs_0_ = bf16[4,128,128]{2,1,0:T(8,128)(2,1)S(1)} fusion(f32[192,512]{1,0:T(8,128)} %param.12, f32[192,512]{1,0:T(8,128)} %param.11), kind=kOutput, calls=%fused_computation | convolution fusion | flops 25165824 | bytes 917504 | tf_op jit(solution)/shard_map/thd,the->hde/dot_general | solution.py:178
  2.2 3.1 %collective-permute-start = (bf16[4,128,128]{2,1,0:T(8,128)(2,1)S(1)}, bf16[4,128,128]{2,1,0:T(8,128)(2,1)S(1)}, u32[]{:S(2)}, u32[]{:S(2)}) collective-permute-start(bf16[4,128,128]{2,1,0:T(8,128)(2,1)S(1)} %convolution_convert_fusion.refs_0_), channel_id=1, source_target_pairs={{0,4},{4,0},{8,12},{12,8},{1,5},{5,1},{9,13},{13,9},{2,6},{6,2},{1... | collective-permute-start | bytes 393224 | tf_op jit(solution)/shard_map/ppermute | solution.py:154
  5.2 1.1 %subtract_convert_fusion.2.ql = bf16[320,512]{1,0:T(8,128)(2,1)S(1)} fusion(f32[128,512]{1,0:T(8,128)} %bitcast.25, f32[192,512]{1,0:T(8,128)} %param.10), kind=kLoop, calls=%fused_computation.6 | loop fusion | flops 819200 | bytes 983040 | tf_op jit(solution)/shard_map/convert_element_type | solution.py:46
  6.4 1.1 %fusion.2.qh = bf16[320,512]{1,0:T(8,128)(2,1)S(1)} fusion(f32[128,512]{1,0:T(8,128)} %bitcast.26, f32[192,512]{1,0:T(8,128)} %param.10), kind=kLoop, calls=%fused_computation.9 | loop fusion | flops 655360 | bytes 983040 | tf_op jit(solution)/shard_map/convert_element_type | solution.py:45
  7.5 0.1 add_convert_fusion.use_ref
  7.6 1.4 %subtract_convert_fusion = (bf16[320,512]{1,0:T(8,128)(2,1)S(1)}, bf16[320,512]{1,0:T(8,128)(2,1)S(1)}) fusion(f32[128,512]{1,0:T(8,128)} %bitcast.21, f32[192,512]{1,0:T(8,128)} %param.12, f32[128,512]{1,0:T(8,128)} %bitcast.23, f32[192,512]{1,0:T(8,128)} %param.11), kind=kLoop, calls=%fused_computation.4 | loop fusion | flops 1638400 | bytes 1966080 | tf_op jit(solution)/shard_map/convert_element_type | solution.py:46
  9.1 0.0 copy-done.3
  9.1 0.0 copy-done.4
  9.1 0.0 copy-done.5
  9.1 0.0 copy-done.6
  9.1 0.1 fusion
  9.2 0.0 collective-permute-done.refs_1_.rest_0_
  9.3 0.0 copy-start.1
  9.3 0.0 copy-start
  9.3 0.0 copy-start.2
  9.3 2.7 %collective-permute-start.1 = (bf16[4,128,128]{2,1,0:T(8,128)(2,1)S(1)}, bf16[4,128,128]{2,1,0:T(8,128)(2,1)S(1)}, u32[]{:S(2)}, u32[]{:S(2)}) collective-permute-start(bf16[4,128,128]{2,1,0:T(8,128)(2,1)S(1)} %shard_map.113.after_ref), channel_id=1, source_target_pairs={{0,8},{4,12},{8,0},{12,4},{1,9},{5,13},{9,1},{13,5},{2,10},{6,14},... | collective-permute-start | bytes 393224 | tf_op jit(solution)/shard_map/ppermute | solution.py:154
  11.9 2.6 %constant_dynamic-slice_fusion = (bf16[512,1024]{1,0:T(8,128)(2,1)S(1)}, bf16[512,1024]{1,0:T(8,128)(2,1)S(1)}, bf16[512,1024]{1,0:T(8,128)(2,1)S(1)}, bf16[512,1024]{1,0:T(8,128)(2,1)S(1)}) fusion(bf16[512,4096]{1,0:T(8,128)(2,1)} %param.19, s32[]{:T(128)S(6)} %select_n.46, s32[]{:T(128)S(6)} %select_n.45, s32[]{:T(128)S(6)} %select_n.43, s32[]{:T(128)S(6)} %select_n.41), kind=kLoop, calls=%fused_computation.15 | loop fusion | bytes 8388624 | tf_op jit(solution)/shard_map/dynamic_slice | solution.py:196
  14.6 0.0 copy-done.1
  14.6 2.7 %shard_map.114.base_ref = f32[320,512]{1,0:T(8,128)S(1)} custom-call(s32[2]{0:T(128)S(1)} %copy-done.1, bf16[320,512]{1,0:T(8,128)(2,1)S(1)} %fusion.2.qh, bf16[320,512]{1,0:T(8,128)(2,1)S(1)} %subtract_convert_fusion.2.ql, bf16[320,512]{1,0:T(8,128)(2,1)S(1)} %get-tuple-element.51.kh, bf16[320,512]{1,0:T(8,128)(2,1)S(1)} %get-tuple-element.49.kl, ...), custom_call_target="tpu_custom_call" | custom-call | flops 629145600 | bytes 2621440 | tf_op jit(solution)/shard_map/pallas_call | solution.py:185
  17.3 0.7 %collective-permute-done.1.rest_1_ = bf16[4,128,128]{2,1,0:T(8,128)(2,1)S(1)} collective-permute-done((bf16[4,128,128]{2,1,0:T(8,128)(2,1)S(1)}, bf16[4,128,128]{2,1,0:T(8,128)(2,1)S(1)}, u32[]{:S(2)}, u32[]{:S(2)}) %collective-permute-start.1) | collective-permute-done | bytes 131104 | tf_op jit(solution)/shard_map/ppermute | solution.py:154
  18.0 0.0 copy-done
  18.0 0.0 copy-done.2
  18.0 1.1 %shard_map.115.rows_ref = bf16[320,512]{1,0:T(8,128)(2,1)S(1)} custom-call(s32[2]{0:T(128)S(1)} %add_convert_fusion.use_ref, s32[2]{0:T(128)S(1)} %copy-done.2, bf16[320,512]{1,0:T(8,128)(2,1)S(1)} %fusion.2.qh, bf16[320,512]{1,0:T(8,128)(2,1)S(1)} %subtract_convert_fusion.2.ql, f32[320,512]{1,0:T(8,128)S(1)} %shard_map.114.base_ref, f32[1,512]{1,0:T(1,128)S(1)} %bitcast.20, ...), custom_call_target="tpu_custom_call" | custom-call | flops 125829120 | bytes 1638400 | tf_op jit(solution)/shard_map/pallas_call | solution.py:189
  19.1 0.5 %shard_map.119 = (bf16[320,512]{1,0:T(8,128)(2,1)S(1)}, bf16[320,256]{1,0:T(8,128)(2,1)S(1)}, bf16[320,256]{1,0:T(8,128)(2,1)S(1)}) custom-call(bf16[320,512]{1,0:T(8,128)(2,1)S(1)} %shard_map.115.rows_ref, bf16[512,1024]{1,0:T(8,128)(2,1)S(1)} %get-tuple-element.44.weight_ref), custom_call_target="tpu_custom_call" | custom-call | flops 335544320 | bytes 2686976 | tf_op jit(solution)/shard_map/pallas_call | solution.py:113
  19.7 0.1 collective-permute-start.6
  19.7 0.5 %collective-permute-start.9 = (bf16[320,256]{1,0:T(8,128)(2,1)S(1)}, bf16[320,256]{1,0:T(8,128)(2,1)S(1)}, u32[]{:S(2)}, u32[]{:S(2)}) collective-permute-start(bf16[320,256]{1,0:T(8,128)(2,1)S(1)} %get-tuple-element.41), channel_id=1, source_target_pairs={{0,1},{1,0},{2,3},{3,2},{4,5},{5,4},{6,7},{7,6},{8,9},{9,8},{10,11... | collective-permute-start | bytes 491528 | tf_op jit(solution)/shard_map/ppermute | solution.py:150
  20.2 0.5 %shard_map.117 = (bf16[320,512]{1,0:T(8,128)(2,1)S(1)}, bf16[320,256]{1,0:T(8,128)(2,1)S(1)}, bf16[320,256]{1,0:T(8,128)(2,1)S(1)}) custom-call(bf16[320,512]{1,0:T(8,128)(2,1)S(1)} %shard_map.115.rows_ref, bf16[512,1024]{1,0:T(8,128)(2,1)S(1)} %get-tuple-element.46.weight_ref), custom_call_target="tpu_custom_call" | custom-call | flops 335544320 | bytes 2686976 | tf_op jit(solution)/shard_map/pallas_call | solution.py:113
  20.7 0.1 collective-permute-start.5
  20.9 0.5 %shard_map.118 = (f32[320,512]{1,0:T(8,128)S(1)}, f32[320,256]{1,0:T(8,128)S(1)}, f32[320,256]{1,0:T(8,128)S(1)}) custom-call(bf16[320,512]{1,0:T(8,128)(2,1)S(1)} %shard_map.115.rows_ref, bf16[512,1024]{1,0:T(8,128)(2,1)S(1)} %get-tuple-element.45.weight_ref), custom_call_target="tpu_custom_call" | custom-call | flops 335544320 | bytes 2686976 | tf_op jit(solution)/shard_map/pallas_call | solution.py:113
  21.4 0.0 collective-permute-done.6.refs_1_
  21.4 0.1 shard_map.121
  21.5 1.5 %collective-permute-start.7 = (bf16[320,512]{1,0:T(8,128)(2,1)S(1)}, bf16[320,512]{1,0:T(8,128)(2,1)S(1)}, u32[]{:S(2)}, u32[]{:S(2)}) collective-permute-start(bf16[320,512]{1,0:T(8,128)(2,1)S(1)} %shard_map.121), channel_id=1, source_target_pairs={{0,2},{2,0},{1,3},{3,1},{4,6},{6,4},{5,7},{7,5},{8,10},{10,8},{9,1... | collective-permute-start | bytes 983048 | tf_op jit(solution)/shard_map/ppermute | solution.py:150
  23.0 0.2 collective-permute-start.3
  23.2 0.3 collective-permute-start.8
  23.5 0.0 collective-permute-done.9.refs_1_
  23.6 0.6 %collective-permute-start.10 = (bf16[320,256]{1,0:T(8,128)(2,1)S(1)}, bf16[320,256]{1,0:T(8,128)(2,1)S(1)}, u32[]{:S(2)}, u32[]{:S(2)}) collective-permute-start(bf16[320,256]{1,0:T(8,128)(2,1)S(1)} %shard_map.122), channel_id=1, source_target_pairs={{0,2},{2,0},{1,3},{3,1},{4,6},{6,4},{5,7},{7,5},{8,10},{10,8},{9,1... | collective-permute-start | bytes 491528 | tf_op jit(solution)/shard_map/ppermute | solution.py:150
  24.2 0.2 collective-permute-done.3.refs_1_
  24.4 0.2 collective-permute-start.2
  24.6 0.0 collective-permute-done.8.rest_4_
  24.6 1.1 %collective-permute-start.4 = (bf16[320,256]{1,0:T(8,128)(2,1)S(1)}, bf16[320,256]{1,0:T(8,128)(2,1)S(1)}, u32[]{:S(2)}, u32[]{:S(2)}) collective-permute-start(bf16[320,256]{1,0:T(8,128)(2,1)S(1)} %shard_map.120), channel_id=1, source_target_pairs={{0,2},{2,0},{1,3},{3,1},{4,6},{6,4},{5,7},{7,5},{8,10},{10,8},{9,1... | collective-permute-start | bytes 491528 | tf_op jit(solution)/shard_map/ppermute | solution.py:150
  25.8 0.5 %shard_map.116 = (f32[320,512]{1,0:T(8,128)S(1)}, f32[320,256]{1,0:T(8,128)S(1)}, f32[320,256]{1,0:T(8,128)S(1)}) custom-call(bf16[320,512]{1,0:T(8,128)(2,1)S(1)} %shard_map.115.rows_ref, bf16[512,1024]{1,0:T(8,128)(2,1)S(1)} %get-tuple-element.47.weight_ref), custom_call_target="tpu_custom_call" | custom-call | flops 335544320 | bytes 2686976 | tf_op jit(solution)/shard_map/pallas_call | solution.py:113
  26.3 0.0 collective-permute-done.5.rest_1_
  26.3 9.3 %collective-permute-done.10.rest_5_ = bf16[320,256]{1,0:T(8,128)(2,1)S(1)} collective-permute-done((bf16[320,256]{1,0:T(8,128)(2,1)S(1)}, bf16[320,256]{1,0:T(8,128)(2,1)S(1)}, u32[]{:S(2)}, u32[]{:S(2)}) %collective-permute-start.10) | collective-permute-done | bytes 163872 | tf_op jit(solution)/shard_map/ppermute | solution.py:150
  35.6 0.0 collective-permute-done.7.rest_2_
  35.6 0.9 %shard_map.123 = (bf16[192,1024]{1,0:T(8,128)(2,1)}, bf16[2,64,1024]{2,1,0:T(8,128)(2,1)}) custom-call(f32[320,512]{1,0:T(8,128)S(1)} %get-tuple-element.34.rest_0_, bf16[320,512]{1,0:T(8,128)(2,1)S(1)} %collective-permute-done.5.rest_1_, bf16[320,512]{1,0:T(8,128)(2,1)S(1)} %collective-permute-done.7.rest_2_, f32[320,256]{1,0:T(8,128)S(1)} %get-tuple-element.38.rest_3_, ...), custom_call_target="tpu_custom_call" | custom-call | flops 1474560 | bytes 5898240 | tf_op jit(solution)/shard_map/pallas_call | solution.py:141
  36.5 0.0 collective-permute-done.2.rest_1_
  36.5 2.1 %collective-permute-done.4.rest_2_ = bf16[320,256]{1,0:T(8,128)(2,1)S(1)} collective-permute-done((bf16[320,256]{1,0:T(8,128)(2,1)S(1)}, bf16[320,256]{1,0:T(8,128)(2,1)S(1)}, u32[]{:S(2)}, u32[]{:S(2)}) %collective-permute-start.4) | collective-permute-done | bytes 163872 | tf_op jit(solution)/shard_map/ppermute | solution.py:150
  38.6 0.7 %shard_map.124 = (bf16[192,1024]{1,0:T(8,128)(2,1)}, bf16[2,64,1024]{2,1,0:T(8,128)(2,1)}) custom-call(f32[320,256]{1,0:T(8,128)S(1)} %get-tuple-element.30.rest_0_, bf16[320,256]{1,0:T(8,128)(2,1)S(1)} %collective-permute-done.2.rest_1_, bf16[320,256]{1,0:T(8,128)(2,1)S(1)} %collective-permute-done.4.rest_2_, ...), custom_call_target="tpu_custom_call", output_to_operand_aliasing={{0}: (3, {}), {1}: (4, {})} | custom-call | flops 245760 | bytes 983040 | tf_op jit(solution)/shard_map/pallas_call | solution.py:141
  (3 shorter events, 0.1 us)
Async XLA Ops:
  0.6 8.4 %copy-start.3 = (f32[192,512]{1,0:T(8,128)S(1)}, f32[192,512]{1,0:T(8,128)}, u32[]{:S(2)}) copy-start(f32[192,512]{1,0:T(8,128)} %param.12) | copy-start | bytes 1179652
  0.6 8.4 %copy-start.4 = (f32[192,512]{1,0:T(8,128)S(1)}, f32[192,512]{1,0:T(8,128)}, u32[]{:S(2)}) copy-start(f32[192,512]{1,0:T(8,128)} %param.11) | copy-start | bytes 1179652
  0.7 8.4 %copy-start.5 = (f32[2,64,512]{2,1,0:T(8,128)S(1)}, f32[2,64,512]{2,1,0:T(8,128)}, u32[]{:S(2)}) copy-start(f32[2,64,512]{2,1,0:T(8,128)} %param.15) | copy-start | bytes 786436
  0.7 8.4 %copy-start.6 = (f32[2,64,512]{2,1,0:T(8,128)S(1)}, f32[2,64,512]{2,1,0:T(8,128)}, u32[]{:S(2)}) copy-start(f32[2,64,512]{2,1,0:T(8,128)} %param.14) | copy-start | bytes 786436
  2.2 7.0 %collective-permute-start = (bf16[4,128,128]{2,1,0:T(8,128)(2,1)S(1)}, bf16[4,128,128]{2,1,0:T(8,128)(2,1)S(1)}, u32[]{:S(2)}, u32[]{:S(2)}) collective-permute-start(bf16[4,128,128]{2,1,0:T(8,128)(2,1)S(1)} %convolution_convert_fusion.refs_0_), channel_id=1, source_target_pairs={{0,4},{4,0},{8,12},{12,8},{1,5},{5,1},{9,13},{13,9},{2,6},{6,2},{1... | collective-permute-start | bytes 393224 | tf_op jit(solution)/shard_map/ppermute | solution.py:154
  9.3 5.3 %copy-start.1 = (s32[2]{0:T(128)S(1)}, s32[2]{0:T(128)}, u32[]{:S(2)}) copy-start(s32[2]{0:T(128)} %offsets_ref.1) | copy-start | bytes 28
  9.3 8.8 %copy-start = (f32[512]{0:T(512)S(1)}, f32[512]{0:T(512)}, u32[]{:S(2)}) copy-start(f32[512]{0:T(512)} %param.18) | copy-start | bytes 6148
  9.3 8.7 %copy-start.2 = (s32[2]{0:T(128)S(1)}, s32[2]{0:T(128)}, u32[]{:S(2)}) copy-start(s32[2]{0:T(128)} %lengths_ref.1) | copy-start | bytes 28
  9.3 8.7 %collective-permute-start.1 = (bf16[4,128,128]{2,1,0:T(8,128)(2,1)S(1)}, bf16[4,128,128]{2,1,0:T(8,128)(2,1)S(1)}, u32[]{:S(2)}, u32[]{:S(2)}) collective-permute-start(bf16[4,128,128]{2,1,0:T(8,128)(2,1)S(1)} %shard_map.113.after_ref), channel_id=1, source_target_pairs={{0,8},{4,12},{8,0},{12,4},{1,9},{5,13},{9,1},{13,5},{2,10},{6,14},... | collective-permute-start | bytes 393224 | tf_op jit(solution)/shard_map/ppermute | solution.py:154
  19.7 1.7 %collective-permute-start.6 = (bf16[320,512]{1,0:T(8,128)(2,1)S(1)}, bf16[320,512]{1,0:T(8,128)(2,1)S(1)}, u32[]{:S(2)}, u32[]{:S(2)}) collective-permute-start(bf16[320,512]{1,0:T(8,128)(2,1)S(1)} %get-tuple-element.37), channel_id=1, source_target_pairs={{0,1},{1,0},{2,3},{3,2},{4,5},{5,4},{6,7},{7,6},{8,9},{9,8},{10,11... | collective-permute-start | bytes 983048 | tf_op jit(solution)/shard_map/ppermute | solution.py:150
  19.7 3.8 %collective-permute-start.9 = (bf16[320,256]{1,0:T(8,128)(2,1)S(1)}, bf16[320,256]{1,0:T(8,128)(2,1)S(1)}, u32[]{:S(2)}, u32[]{:S(2)}) collective-permute-start(bf16[320,256]{1,0:T(8,128)(2,1)S(1)} %get-tuple-element.41), channel_id=1, source_target_pairs={{0,1},{1,0},{2,3},{3,2},{4,5},{5,4},{6,7},{7,6},{8,9},{9,8},{10,11... | collective-permute-start | bytes 491528 | tf_op jit(solution)/shard_map/ppermute | solution.py:150
  20.7 5.5 %collective-permute-start.5 = (bf16[320,512]{1,0:T(8,128)(2,1)S(1)}, bf16[320,512]{1,0:T(8,128)(2,1)S(1)}, u32[]{:S(2)}, u32[]{:S(2)}) collective-permute-start(bf16[320,512]{1,0:T(8,128)(2,1)S(1)} %get-tuple-element.35), channel_id=1, source_target_pairs={{0,1},{1,0},{2,3},{3,2},{4,5},{5,4},{6,7},{7,6},{8,9},{9,8},{10,11... | collective-permute-start | bytes 983048 | tf_op jit(solution)/shard_map/ppermute | solution.py:150
  21.5 14.1 %collective-permute-start.7 = (bf16[320,512]{1,0:T(8,128)(2,1)S(1)}, bf16[320,512]{1,0:T(8,128)(2,1)S(1)}, u32[]{:S(2)}, u32[]{:S(2)}) collective-permute-start(bf16[320,512]{1,0:T(8,128)(2,1)S(1)} %shard_map.121), channel_id=1, source_target_pairs={{0,2},{2,0},{1,3},{3,1},{4,6},{6,4},{5,7},{7,5},{8,10},{10,8},{9,1... | collective-permute-start | bytes 983048 | tf_op jit(solution)/shard_map/ppermute | solution.py:150
  23.0 1.4 %collective-permute-start.3 = (bf16[320,256]{1,0:T(8,128)(2,1)S(1)}, bf16[320,256]{1,0:T(8,128)(2,1)S(1)}, u32[]{:S(2)}, u32[]{:S(2)}) collective-permute-start(bf16[320,256]{1,0:T(8,128)(2,1)S(1)} %get-tuple-element.33), channel_id=1, source_target_pairs={{0,1},{1,0},{2,3},{3,2},{4,5},{5,4},{6,7},{7,6},{8,9},{9,8},{10,11... | collective-permute-start | bytes 491528 | tf_op jit(solution)/shard_map/ppermute | solution.py:150
  23.2 1.5 %collective-permute-start.8 = (bf16[320,256]{1,0:T(8,128)(2,1)S(1)}, bf16[320,256]{1,0:T(8,128)(2,1)S(1)}, u32[]{:S(2)}, u32[]{:S(2)}) collective-permute-start(bf16[320,256]{1,0:T(8,128)(2,1)S(1)} %get-tuple-element.39), channel_id=1, source_target_pairs={{0,1},{1,0},{2,3},{3,2},{4,5},{5,4},{6,7},{7,6},{8,9},{9,8},{10,11... | collective-permute-start | bytes 491528 | tf_op jit(solution)/shard_map/ppermute | solution.py:150
  23.6 12.0 %collective-permute-start.10 = (bf16[320,256]{1,0:T(8,128)(2,1)S(1)}, bf16[320,256]{1,0:T(8,128)(2,1)S(1)}, u32[]{:S(2)}, u32[]{:S(2)}) collective-permute-start(bf16[320,256]{1,0:T(8,128)(2,1)S(1)} %shard_map.122), channel_id=1, source_target_pairs={{0,2},{2,0},{1,3},{3,1},{4,6},{6,4},{5,7},{7,5},{8,10},{10,8},{9,1... | collective-permute-start | bytes 491528 | tf_op jit(solution)/shard_map/ppermute | solution.py:150
  24.4 12.1 %collective-permute-start.2 = (bf16[320,256]{1,0:T(8,128)(2,1)S(1)}, bf16[320,256]{1,0:T(8,128)(2,1)S(1)}, u32[]{:S(2)}, u32[]{:S(2)}) collective-permute-start(bf16[320,256]{1,0:T(8,128)(2,1)S(1)} %get-tuple-element.31), channel_id=1, source_target_pairs={{0,1},{1,0},{2,3},{3,2},{4,5},{5,4},{6,7},{7,6},{8,9},{9,8},{10,11... | collective-permute-start | bytes 491528 | tf_op jit(solution)/shard_map/ppermute | solution.py:150
  24.6 14.0 %collective-permute-start.4 = (bf16[320,256]{1,0:T(8,128)(2,1)S(1)}, bf16[320,256]{1,0:T(8,128)(2,1)S(1)}, u32[]{:S(2)}, u32[]{:S(2)}) collective-permute-start(bf16[320,256]{1,0:T(8,128)(2,1)S(1)} %shard_map.120), channel_id=1, source_target_pairs={{0,2},{2,0},{1,3},{3,1},{4,6},{6,4},{5,7},{7,5},{8,10},{10,8},{9,1... | collective-permute-start | bytes 491528 | tf_op jit(solution)/shard_map/ppermute | solution.py:150

commit v3 on v2

--- a/solution.py
+++ b/solution.py
@@ -52,9 +52,15 @@
     return dot(ah, bh) + (dot(ah, bl) + dot(al, bh))
 
 
-def base_kernel(tokens, offsets_ref, qh, ql, kh, kl, vh, vl, after_ref, out_ref):
-    rows, opts = out_ref.shape[0], offsets_ref.shape[0]
-    slots = (rows - tokens) // opts
+def joined(ctx_ref, opt_ref, cols):
+    return jnp.concatenate([ctx_ref[:, cols]] + [opt_ref[o, :, cols] for o in range(opt_ref.shape[0])], axis=0)
+
+
+def base_kernel(
+    offsets_ref, lengths_ref, gain_ref, q_ref, k_ref, v_ref, oq_ref, ok_ref, ov_ref, after_ref, out_ref, qh_ref, ql_ref, gains_ref
+):
+    tokens, (opts, slots, _) = q_ref.shape[0], oq_ref.shape
+    rows = tokens + opts * slots
     i = lax.broadcasted_iota(jnp.int32, (rows, rows), 0)
     j = lax.broadcasted_iota(jnp.int32, (rows, rows), 1)
     limit, first = i + 1, jnp.full((rows, rows), rows, jnp.int32)
@@ -62,45 +68,47 @@
         own = i >= tokens + o * slots
         limit = jnp.where(own, offsets_ref[o], limit)
         first = jnp.where(own, tokens + o * slots, first)
-    mask = (j < limit) | ((j >= first) & (j <= i))
-    for h in range(out_ref.shape[1] // DH):
-        cols = columns(h)
-        scores = dot3((qh[:, cols], ql[:, cols]), (kh[:, cols], kl[:, cols]), ((1,), (1,)))
-        scores = halves(jnp.where(mask, scores, 0.0))
-        out_ref[:, cols] = dot3(scores, (vh[:, cols], vl[:, cols]), ((1,), (0,)))
-
-
-def add_kernel(*refs):
-    total = refs[0][...].astype(f32)
-    for ref in refs[1:-1]:
-        total = total + ref[...].astype(f32)
-    refs[-1][...] = total.astype(refs[-1].dtype)
-
-
-def add(*terms):
-    return call(
-        add_kernel, Shape(terms[0].shape, bf16), [VMEM] * len(terms),
-        len(terms) * terms[0].size, 6 * len(terms) * terms[0].size,
-    )(*terms)
-
-
-def normed_kernel(tokens, use_ref, lengths_ref, qh, ql, base_ref, gain_ref, *rest):
-    parts, out_ref = rest[:-1], rest[-1]
-    (rows, feats), opts = out_ref.shape, lengths_ref.shape[0]
-    slots = (rows - tokens) // opts
     row = lax.broadcasted_iota(jnp.int32, (rows, 1), 0)
     valid = row < tokens
     for o in range(opts):
         start = tokens + o * slots
         valid = valid | ((row >= start) & (row < start + lengths_ref[o]))
-    for h in range(feats // DH):
+    gains_ref[...] = jnp.where(valid, gain_ref[...], 0.0)
+    mask = (j < limit) | ((j >= first) & (j <= i))
+    for h in range(out_ref.shape[1] // DH):
+        cols = columns(h)
+        q, k, v = (halves(joined(c, o, cols)) for c, o in ((q_ref, oq_ref), (k_ref, ok_ref), (v_ref, ov_ref)))
+        qh_ref[:, cols], ql_ref[:, cols] = q
+        scores = halves(jnp.where(mask, dot3(q, k, ((1,), (1,))), 0.0))
+        out_ref[:, cols] = dot3(scores, v, ((1,), (0,)))
+
+
+def add_kernel(*refs):
+    out_ref = refs[-1]
+    total = refs[0][:out_ref.shape[0]].astype(f32)
+    for ref in refs[1:-1]:
+        total = total + ref[:out_ref.shape[0]].astype(f32)
+    out_ref[...] = total.astype(out_ref.dtype)
+
+
+def add(*terms, rows=None):
+    shape = (rows or terms[0].shape[0],) + terms[0].shape[1:]
+    return call(
+        add_kernel, Shape(shape, bf16), [VMEM] * len(terms), len(terms) * terms[0].size, 6 * len(terms) * terms[0].size,
+    )(*terms)
+
+
+def normed_kernel(spans, use_ref, qh, ql, base_ref, gains_ref, *rest):
+    parts, out_ref = rest[:-1], rest[-1]
+    for h in range(out_ref.shape[1] // DH):
         prefix = jnp.zeros((DH, DH), f32)
-        for n, part in enumerate(parts):
-            prefix = prefix + jnp.where(use_ref[n] > 0, part[h].astype(f32), 0.0)
+        for n, (low, high) in enumerate(spans):
+            if low <= h < high:
+                prefix = prefix + jnp.where(use_ref[n:n + 1] > 0.0, parts[n][h - low].astype(f32), 0.0)
         cols = columns(h)
         out = base_ref[:, cols] + dot3((qh[:, cols], ql[:, cols]), halves(prefix), ((1,), (0,)))
         scale = lax.rsqrt(jnp.mean(out * out, axis=1, keepdims=True) + EPS)
-        out_ref[:, cols] = jnp.where(valid, out * scale * gain_ref[:, cols], 0.0).astype(out_ref.dtype)
+        out_ref[:, cols] = (out * scale * gains_ref[:, cols]).astype(out_ref.dtype)
 
 
 def project_kernel(spans, rows_ref, weight_ref, *outs):
@@ -163,7 +171,7 @@
         step *= 2
         if step < size:
             windows.append(add(windows[-1], parts[-1]))
-    return parts, jnp.stack(use).astype(jnp.int32), windows[:2][-1]
+    return parts, use, windows[:2][-1]
 
 
 def on_device(sizes, q, k, v, oq, ok, ov, offsets, lengths, gain, weight):
@@ -179,17 +187,17 @@
         "thd,the->hde", k.reshape(tokens, heads, DH), v.reshape(tokens, heads, DH), precision=lax.Precision.DEFAULT
     ).astype(bf16)
     parts, use, window = exclusive(state, "seq", n_seq)
-
-    q, k, v, oq, ok, ov, _ = lax.optimization_barrier((q, k, v, oq, ok, ov, state))
-    halved = [halves(jnp.concatenate([x, y.reshape(-1, feats)])) for x, y in ((q, oq), (k, ok), (v, ov))]
-    base = call(
-        functools.partial(base_kernel, tokens), Shape((rows, feats), f32), [SMEM] + [VMEM] * 6 + [ANY],
+    parts = [(part, (0, heads), used) for part, used in zip(parts, use)]
+
+    base, qh, ql, gains = call(
+        base_kernel, [Shape((rows, feats), t) for t in (f32, bf16, bf16, f32)], [SMEM] * 2 + [VMEM] * 7 + [ANY],
         12 * rows * rows * feats, 16 * rows * feats,
-    )(offsets, *sum(halved, ()), window)
+    )(offsets, lengths, gain[None], q, k, v, oq, ok, ov, window)
+    use = jnp.broadcast_to(jnp.stack([p[2] for p in parts]).astype(f32)[:, None], (len(parts), DH))
     normed = call(
-        functools.partial(normed_kernel, tokens), Shape((rows, feats), bf16),
-        [SMEM, SMEM] + [VMEM] * (4 + len(parts)), 6 * rows * DH * feats, 10 * rows * feats,
-    )(use, lengths, *halved[0], base, gain[None], *parts)
+        functools.partial(normed_kernel, [p[1] for p in parts]), Shape((rows, feats), bf16),
+        [VMEM] * (5 + len(parts)), 6 * rows * DH * feats, 10 * rows * feats,
+    )(use, qh, ql, base, gains, *[p[0] for p in parts])
 
     def blocks(d):
         at = [((head + d) % n_head * n_sub + (sub + s) % n_sub) * width for s in range(n_sub)]
@@ -202,7 +210,7 @@
         theirs = [[ring(x, "sub", n_sub, s + 1) for x in xs] for s, xs in enumerate(theirs)]
         return list(zip(ours, *theirs))
 
-    later, _ = lax.optimization_barrier((weight, window))
+    later, _ = lax.optimization_barrier((weight, state))
     weights = [blocks(d) for d in range(n_head)]
     spans = [(width * a // 4, width * b // 4) for a, b in SPANS]
     received = {}

time: 39.6 us -> 38.1 us (0.962)
  other arithmetic: 3.83 us -> 0.08 us
  waiting for transfers between devices: 12.3 us -> 15 us
  Pallas kernels: 7.67 us -> 7.15 us
    convert_element_type x5 -> x1, other arithmetic: 3.83 us -> 0.08 us  [on_device(): jnp.stack([p[2] for p in parts]).astype(f32)[:, None]]
    ppermute x2, waiting for transfers between devices: 0.7 us -> 3.38 us  [swap(): return lax.ppermute(value, axis, [(i, i ^ mask) for i in range(size)])]
    pallas_call x6, Pallas kernels: 4 us -> 3.48 us  [the longest x1 2.77 us: on_device(): call(base_kernel, [Shape((rows, feats), t) for t in (f32, bf16, bf16, f32...]
  transfers between devices with their start and end apart: 11 -> 11, of which waited for: 4 -> 5; matrix products, arithmetic and copies ran while one was open for 16% -> 7% of each run, Pallas kernels for 13% -> 14%
where the time goes in v3:
time: 38.1 us; the launch traced here: 37.9 us
  waiting for transfers between devices  15 us (39%)
  starting transfers between devices  10.6 us (28%)
  Pallas kernels  7.15 us (19%)
  local copies, waits for them, and re-layouts  2.88 us (8%)
  matrix products  1.39 us (4%)
  between operations  0.84 us (2%)
    ppermute x9, waiting for transfers between devices, ring(): lax.ppermute(value, axis, [(i, (i + shift) % size) for i in range(size)])  11.6 us
    ppermute x2, starting transfers between devices, swap(): return lax.ppermute(value, axis, [(i, i ^ mask) for i in range(size)])  5.91 us
    ppermute x9, starting transfers between devices, ring(): lax.ppermute(value, axis, [(i, (i + shift) % size) for i in range(size)])  4.67 us
    ppermute x2, waiting for transfers between devices, swap(): return lax.ppermute(value, axis, [(i, i ^ mask) for i in range(size)])  3.38 us
    pallas_call x1, Pallas kernels, on_device(): call(base_kernel, [Shape((rows, feats), t) for t in (f32, bf16, bf16, f32...  2.77 us
    dynamic_slice x1, local copies, waits for them, and re-layouts, blocks(): return [lax.dynamic_slice_in_dim(later, x, width, 1) for x in at]  2.76 us
    pallas_call x4, Pallas kernels, project(): call(functools.partial(project_kernel, spans), [Shape((count, b - a), dty...  2 us
    pallas_call x2, Pallas kernels, final(): call(functools.partial(final_kernel, spans, len(terms[0])), shapes, [VMEM...  1.68 us
  transfers between devices with their start and end apart: 11, of which 5 were waited for; matrix products, arithmetic and copies ran while one was open for 7% of the time, Pallas kernels for 14%

profile of v3, /device:TPU:0, one launch (start us, length us, event | category | flops | bytes accessed | tf_op | source)
XLA Modules:
  0.0 37.9 jit_solution(11034779932645707252)
XLA Ops:
  0.6 1.4 %convolution_convert_fusion.refs_0_ = bf16[4,128,128]{2,1,0:T(8,128)(2,1)S(1)} fusion(f32[192,512]{1,0:T(8,128)} %v_ref.1, f32[192,512]{1,0:T(8,128)} %k_ref.1), kind=kOutput, calls=%fused_computation | convolution fusion | flops 25165824 | bytes 917504 | tf_op jit(solution)/shard_map/thd,the->hde/dot_general | solution.py:186
  2.0 3.1 %collective-permute-start = (bf16[4,128,128]{2,1,0:T(8,128)(2,1)S(1)}, bf16[4,128,128]{2,1,0:T(8,128)(2,1)S(1)}, u32[]{:S(2)}, u32[]{:S(2)}) collective-permute-start(bf16[4,128,128]{2,1,0:T(8,128)(2,1)S(1)} %convolution_convert_fusion.refs_0_), channel_id=1, source_target_pairs={{0,4},{4,0},{8,12},{12,8},{1,5},{5,1},{9,13},{13,9},{2,6},{6,2},{1... | collective-permute-start | bytes 393224 | tf_op jit(solution)/shard_map/ppermute | solution.py:162
  5.1 0.0 copy-start
  5.1 0.0 copy-start.1
  5.1 0.0 copy-start.2
  5.1 0.0 copy-start.3
  5.1 0.0 copy-start.4
  5.1 0.0 copy-start.5
  5.1 0.0 copy-start.6
  5.2 0.0 copy-start.7
  5.2 0.0 copy-start.8
  5.2 2.8 %constant_dynamic-slice_fusion = (bf16[512,1024]{1,0:T(8,128)(2,1)S(1)}, bf16[512,1024]{1,0:T(8,128)(2,1)S(1)}, bf16[512,1024]{1,0:T(8,128)(2,1)S(1)}, bf16[512,1024]{1,0:T(8,128)(2,1)S(1)}) fusion(bf16[512,4096]{1,0:T(8,128)(2,1)} %param.19, s32[]{:T(128)S(6)} %select_n.46, s32[]{:T(128)S(6)} %select_n.45, s32[]{:T(128)S(6)} %select_n.43, s32[]{:T(128)S(6)} %select_n.41), kind=kLoop, calls=%fused_computation.6 | loop fusion | bytes 8388624 | tf_op jit(solution)/shard_map/dynamic_slice | solution.py:204
  7.9 0.7 %collective-permute-done.refs_1_.rest_0_ = bf16[4,128,128]{2,1,0:T(8,128)(2,1)S(1)} collective-permute-done((bf16[4,128,128]{2,1,0:T(8,128)(2,1)S(1)}, bf16[4,128,128]{2,1,0:T(8,128)(2,1)S(1)}, u32[]{:S(2)}, u32[]{:S(2)}) %collective-permute-start) | collective-permute-done | bytes 131104 | tf_op jit(solution)/shard_map/ppermute | solution.py:162
  8.6 2.8 %collective-permute-start.1 = (bf16[4,128,128]{2,1,0:T(8,128)(2,1)S(1)}, bf16[4,128,128]{2,1,0:T(8,128)(2,1)S(1)}, u32[]{:S(2)}, u32[]{:S(2)}) collective-permute-start(bf16[4,128,128]{2,1,0:T(8,128)(2,1)S(1)} %shard_map.113.after_ref), channel_id=1, source_target_pairs={{0,8},{4,12},{8,0},{12,4},{1,9},{5,13},{9,1},{13,5},{2,10},{6,14},... | collective-permute-start | bytes 393224 | tf_op jit(solution)/shard_map/ppermute | solution.py:162
  11.5 0.1 add_convert_fusion
  11.5 0.0 copy-done
  11.5 0.0 copy-done.1
  11.5 0.0 copy-done.2
  11.5 0.0 copy-done.3
  11.6 0.0 copy-done.4
  11.6 0.0 copy-done.5
  11.6 0.0 copy-done.6
  11.6 0.0 copy-done.7
  11.6 0.0 copy-done.8
  11.6 2.8 %shard_map.114 = (f32[320,512]{1,0:T(8,128)S(1)}, bf16[320,512]{1,0:T(8,128)(2,1)S(1)}, bf16[320,512]{1,0:T(8,128)(2,1)S(1)}, f32[320,512]{1,0:T(8,128)S(1)}) custom-call(s32[2]{0:T(128)S(1)} %copy-done.7, s32[2]{0:T(128)S(1)} %copy-done.8, f32[1,512]{1,0:T(1,128)S(1)} %bitcast.17, f32[192,512]{1,0:T(8,128)S(1)} %copy-done.2, f32[192,512]{1,0:T(8,128)S(1)} %copy-done, ...), custom_call_target="tpu_custom_call" | custom-call | flops 629145600 | bytes 2621440 | tf_op jit(solution)/shard_map/pallas_call | solution.py:192
  14.4 2.7 %collective-permute-done.1.rest_1_ = bf16[4,128,128]{2,1,0:T(8,128)(2,1)S(1)} collective-permute-done((bf16[4,128,128]{2,1,0:T(8,128)(2,1)S(1)}, bf16[4,128,128]{2,1,0:T(8,128)(2,1)S(1)}, u32[]{:S(2)}, u32[]{:S(2)}) %collective-permute-start.1) | collective-permute-done | bytes 131104 | tf_op jit(solution)/shard_map/ppermute | solution.py:162
  17.1 0.1 broadcast_in_dim.4.use_ref
  17.2 0.6 %shard_map.115.rows_ref = bf16[320,512]{1,0:T(8,128)(2,1)S(1)} custom-call(f32[2,128]{1,0:T(2,128)S(1)} %broadcast_in_dim.4.use_ref, bf16[320,512]{1,0:T(8,128)(2,1)S(1)} %get-tuple-element.21.qh, bf16[320,512]{1,0:T(8,128)(2,1)S(1)} %get-tuple-element.22.ql, f32[320,512]{1,0:T(8,128)S(1)} %get-tuple-element.23.base_ref, ...), custom_call_target="tpu_custom_call" | custom-call | flops 125829120 | bytes 1638400 | tf_op jit(solution)/shard_map/pallas_call | solution.py:197
  17.7 0.5 %shard_map.119 = (bf16[320,512]{1,0:T(8,128)(2,1)S(1)}, bf16[320,256]{1,0:T(8,128)(2,1)S(1)}, bf16[320,256]{1,0:T(8,128)(2,1)S(1)}) custom-call(bf16[320,512]{1,0:T(8,128)(2,1)S(1)} %shard_map.115.rows_ref, bf16[512,1024]{1,0:T(8,128)(2,1)S(1)} %get-tuple-element.40.weight_ref), custom_call_target="tpu_custom_call" | custom-call | flops 335544320 | bytes 2686976 | tf_op jit(solution)/shard_map/pallas_call | solution.py:121
  18.2 0.1 collective-permute-start.6
  18.3 0.5 %collective-permute-start.9 = (bf16[320,256]{1,0:T(8,128)(2,1)S(1)}, bf16[320,256]{1,0:T(8,128)(2,1)S(1)}, u32[]{:S(2)}, u32[]{:S(2)}) collective-permute-start(bf16[320,256]{1,0:T(8,128)(2,1)S(1)} %get-tuple-element.37), channel_id=1, source_target_pairs={{0,1},{1,0},{2,3},{3,2},{4,5},{5,4},{6,7},{7,6},{8,9},{9,8},{10,11... | collective-permute-start | bytes 491528 | tf_op jit(solution)/shard_map/ppermute | solution.py:158
  18.8 0.5 %shard_map.117 = (bf16[320,512]{1,0:T(8,128)(2,1)S(1)}, bf16[320,256]{1,0:T(8,128)(2,1)S(1)}, bf16[320,256]{1,0:T(8,128)(2,1)S(1)}) custom-call(bf16[320,512]{1,0:T(8,128)(2,1)S(1)} %shard_map.115.rows_ref, bf16[512,1024]{1,0:T(8,128)(2,1)S(1)} %get-tuple-element.42.weight_ref), custom_call_target="tpu_custom_call" | custom-call | flops 335544320 | bytes 2686976 | tf_op jit(solution)/shard_map/pallas_call | solution.py:121
  19.3 0.1 collective-permute-start.5
  19.5 0.5 %shard_map.118 = (f32[320,512]{1,0:T(8,128)S(1)}, f32[320,256]{1,0:T(8,128)S(1)}, f32[320,256]{1,0:T(8,128)S(1)}) custom-call(bf16[320,512]{1,0:T(8,128)(2,1)S(1)} %shard_map.115.rows_ref, bf16[512,1024]{1,0:T(8,128)(2,1)S(1)} %get-tuple-element.41.weight_ref), custom_call_target="tpu_custom_call" | custom-call | flops 335544320 | bytes 2686976 | tf_op jit(solution)/shard_map/pallas_call | solution.py:121
  20.0 0.0 collective-permute-done.6.refs_1_
  20.0 0.1 shard_map.121
  20.0 1.4 %collective-permute-start.7 = (bf16[320,512]{1,0:T(8,128)(2,1)S(1)}, bf16[320,512]{1,0:T(8,128)(2,1)S(1)}, u32[]{:S(2)}, u32[]{:S(2)}) collective-permute-start(bf16[320,512]{1,0:T(8,128)(2,1)S(1)} %shard_map.121), channel_id=1, source_target_pairs={{0,2},{2,0},{1,3},{3,1},{4,6},{6,4},{5,7},{7,5},{8,10},{10,8},{9,1... | collective-permute-start | bytes 983048 | tf_op jit(solution)/shard_map/ppermute | solution.py:158
  21.4 0.2 collective-permute-start.3
  21.6 0.3 collective-permute-start.8
  22.0 0.0 collective-permute-done.9.refs_1_
  22.0 0.8 %collective-permute-start.10 = (bf16[320,256]{1,0:T(8,128)(2,1)S(1)}, bf16[320,256]{1,0:T(8,128)(2,1)S(1)}, u32[]{:S(2)}, u32[]{:S(2)}) collective-permute-start(bf16[320,256]{1,0:T(8,128)(2,1)S(1)} %shard_map.122), channel_id=1, source_target_pairs={{0,2},{2,0},{1,3},{3,1},{4,6},{6,4},{5,7},{7,5},{8,10},{10,8},{9,1... | collective-permute-start | bytes 491528 | tf_op jit(solution)/shard_map/ppermute | solution.py:158
  22.8 0.1 collective-permute-done.3.refs_1_
  22.8 0.2 collective-permute-start.2
  23.0 0.0 collective-permute-done.8.rest_4_
  23.1 1.1 %collective-permute-start.4 = (bf16[320,256]{1,0:T(8,128)(2,1)S(1)}, bf16[320,256]{1,0:T(8,128)(2,1)S(1)}, u32[]{:S(2)}, u32[]{:S(2)}) collective-permute-start(bf16[320,256]{1,0:T(8,128)(2,1)S(1)} %shard_map.120), channel_id=1, source_target_pairs={{0,2},{2,0},{1,3},{3,1},{4,6},{6,4},{5,7},{7,5},{8,10},{10,8},{9,1... | collective-permute-start | bytes 491528 | tf_op jit(solution)/shard_map/ppermute | solution.py:158
  24.2 0.5 %shard_map.116 = (f32[320,512]{1,0:T(8,128)S(1)}, f32[320,256]{1,0:T(8,128)S(1)}, f32[320,256]{1,0:T(8,128)S(1)}) custom-call(bf16[320,512]{1,0:T(8,128)(2,1)S(1)} %shard_map.115.rows_ref, bf16[512,1024]{1,0:T(8,128)(2,1)S(1)} %get-tuple-element.43.weight_ref), custom_call_target="tpu_custom_call" | custom-call | flops 335544320 | bytes 2686976 | tf_op jit(solution)/shard_map/pallas_call | solution.py:121
  24.7 0.0 collective-permute-done.5.rest_1_
  24.7 9.4 %collective-permute-done.10.rest_5_ = bf16[320,256]{1,0:T(8,128)(2,1)S(1)} collective-permute-done((bf16[320,256]{1,0:T(8,128)(2,1)S(1)}, bf16[320,256]{1,0:T(8,128)(2,1)S(1)}, u32[]{:S(2)}, u32[]{:S(2)}) %collective-permute-start.10) | collective-permute-done | bytes 163872 | tf_op jit(solution)/shard_map/ppermute | solution.py:158
  34.1 0.0 collective-permute-done.7.rest_2_
  34.1 0.9 %shard_map.123 = (bf16[192,1024]{1,0:T(8,128)(2,1)}, bf16[2,64,1024]{2,1,0:T(8,128)(2,1)}) custom-call(f32[320,512]{1,0:T(8,128)S(1)} %get-tuple-element.30.rest_0_, bf16[320,512]{1,0:T(8,128)(2,1)S(1)} %collective-permute-done.5.rest_1_, bf16[320,512]{1,0:T(8,128)(2,1)S(1)} %collective-permute-done.7.rest_2_, f32[320,256]{1,0:T(8,128)S(1)} %get-tuple-element.34.rest_3_, ...), custom_call_target="tpu_custom_call" | custom-call | flops 1474560 | bytes 5898240 | tf_op jit(solution)/shard_map/pallas_call | solution.py:149
  35.1 0.0 collective-permute-done.2.rest_1_
  35.1 2.1 %collective-permute-done.4.rest_2_ = bf16[320,256]{1,0:T(8,128)(2,1)S(1)} collective-permute-done((bf16[320,256]{1,0:T(8,128)(2,1)S(1)}, bf16[320,256]{1,0:T(8,128)(2,1)S(1)}, u32[]{:S(2)}, u32[]{:S(2)}) %collective-permute-start.4) | collective-permute-done | bytes 163872 | tf_op jit(solution)/shard_map/ppermute | solution.py:158
  37.2 0.7 %shard_map.124 = (bf16[192,1024]{1,0:T(8,128)(2,1)}, bf16[2,64,1024]{2,1,0:T(8,128)(2,1)}) custom-call(f32[320,256]{1,0:T(8,128)S(1)} %get-tuple-element.26.rest_0_, bf16[320,256]{1,0:T(8,128)(2,1)S(1)} %collective-permute-done.2.rest_1_, bf16[320,256]{1,0:T(8,128)(2,1)S(1)} %collective-permute-done.4.rest_2_, ...), custom_call_target="tpu_custom_call", output_to_operand_aliasing={{0}: (3, {}), {1}: (4, {})} | custom-call | flops 245760 | bytes 983040 | tf_op jit(solution)/shard_map/pallas_call | solution.py:149
  (3 shorter events, 0.1 us)
Async XLA Ops:
  2.0 6.6 %collective-permute-start = (bf16[4,128,128]{2,1,0:T(8,128)(2,1)S(1)}, bf16[4,128,128]{2,1,0:T(8,128)(2,1)S(1)}, u32[]{:S(2)}, u32[]{:S(2)}) collective-permute-start(bf16[4,128,128]{2,1,0:T(8,128)(2,1)S(1)} %convolution_convert_fusion.refs_0_), channel_id=1, source_target_pairs={{0,4},{4,0},{8,12},{12,8},{1,5},{5,1},{9,13},{13,9},{2,6},{6,2},{1... | collective-permute-start | bytes 393224 | tf_op jit(solution)/shard_map/ppermute | solution.py:162
  5.1 6.4 %copy-start = (f32[192,512]{1,0:T(8,128)S(1)}, f32[192,512]{1,0:T(8,128)}, u32[]{:S(2)}) copy-start(f32[192,512]{1,0:T(8,128)} %k_ref.1) | copy-start | bytes 1179652
  5.1 6.4 %copy-start.1 = (f32[192,512]{1,0:T(8,128)S(1)}, f32[192,512]{1,0:T(8,128)}, u32[]{:S(2)}) copy-start(f32[192,512]{1,0:T(8,128)} %v_ref.1) | copy-start | bytes 1179652
  5.1 6.4 %copy-start.2 = (f32[192,512]{1,0:T(8,128)S(1)}, f32[192,512]{1,0:T(8,128)}, u32[]{:S(2)}) copy-start(f32[192,512]{1,0:T(8,128)} %q_ref.1) | copy-start | bytes 1179652
  5.1 6.4 %copy-start.3 = (f32[2,64,512]{2,1,0:T(8,128)S(1)}, f32[2,64,512]{2,1,0:T(8,128)}, u32[]{:S(2)}) copy-start(f32[2,64,512]{2,1,0:T(8,128)} %oq_ref.1) | copy-start | bytes 786436
  5.1 6.4 %copy-start.4 = (f32[2,64,512]{2,1,0:T(8,128)S(1)}, f32[2,64,512]{2,1,0:T(8,128)}, u32[]{:S(2)}) copy-start(f32[2,64,512]{2,1,0:T(8,128)} %ok_ref.1) | copy-start | bytes 786436
  5.1 6.4 %copy-start.5 = (f32[2,64,512]{2,1,0:T(8,128)S(1)}, f32[2,64,512]{2,1,0:T(8,128)}, u32[]{:S(2)}) copy-start(f32[2,64,512]{2,1,0:T(8,128)} %ov_ref.1) | copy-start | bytes 786436
  5.1 6.4 %copy-start.6 = (f32[512]{0:T(512)S(1)}, f32[512]{0:T(512)}, u32[]{:S(2)}) copy-start(f32[512]{0:T(512)} %param.18) | copy-start | bytes 6148
  5.2 6.4 %copy-start.7 = (s32[2]{0:T(128)S(1)}, s32[2]{0:T(128)}, u32[]{:S(2)}) copy-start(s32[2]{0:T(128)} %offsets_ref.1) | copy-start | bytes 28
  5.2 6.4 %copy-start.8 = (s32[2]{0:T(128)S(1)}, s32[2]{0:T(128)}, u32[]{:S(2)}) copy-start(s32[2]{0:T(128)} %lengths_ref.1) | copy-start | bytes 28
  8.6 8.5 %collective-permute-start.1 = (bf16[4,128,128]{2,1,0:T(8,128)(2,1)S(1)}, bf16[4,128,128]{2,1,0:T(8,128)(2,1)S(1)}, u32[]{:S(2)}, u32[]{:S(2)}) collective-permute-start(bf16[4,128,128]{2,1,0:T(8,128)(2,1)S(1)} %shard_map.113.after_ref), channel_id=1, source_target_pairs={{0,8},{4,12},{8,0},{12,4},{1,9},{5,13},{9,1},{13,5},{2,10},{6,14},... | collective-permute-start | bytes 393224 | tf_op jit(solution)/shard_map/ppermute | solution.py:162
  18.2 1.7 %collective-permute-start.6 = (bf16[320,512]{1,0:T(8,128)(2,1)S(1)}, bf16[320,512]{1,0:T(8,128)(2,1)S(1)}, u32[]{:S(2)}, u32[]{:S(2)}) collective-permute-start(bf16[320,512]{1,0:T(8,128)(2,1)S(1)} %get-tuple-element.33), channel_id=1, source_target_pairs={{0,1},{1,0},{2,3},{3,2},{4,5},{5,4},{6,7},{7,6},{8,9},{9,8},{10,11... | collective-permute-start | bytes 983048 | tf_op jit(solution)/shard_map/ppermute | solution.py:158
  18.3 3.6 %collective-permute-start.9 = (bf16[320,256]{1,0:T(8,128)(2,1)S(1)}, bf16[320,256]{1,0:T(8,128)(2,1)S(1)}, u32[]{:S(2)}, u32[]{:S(2)}) collective-permute-start(bf16[320,256]{1,0:T(8,128)(2,1)S(1)} %get-tuple-element.37), channel_id=1, source_target_pairs={{0,1},{1,0},{2,3},{3,2},{4,5},{5,4},{6,7},{7,6},{8,9},{9,8},{10,11... | collective-permute-start | bytes 491528 | tf_op jit(solution)/shard_map/ppermute | solution.py:158
  19.3 5.4 %collective-permute-start.5 = (bf16[320,512]{1,0:T(8,128)(2,1)S(1)}, bf16[320,512]{1,0:T(8,128)(2,1)S(1)}, u32[]{:S(2)}, u32[]{:S(2)}) collective-permute-start(bf16[320,512]{1,0:T(8,128)(2,1)S(1)} %get-tuple-element.31), channel_id=1, source_target_pairs={{0,1},{1,0},{2,3},{3,2},{4,5},{5,4},{6,7},{7,6},{8,9},{9,8},{10,11... | collective-permute-start | bytes 983048 | tf_op jit(solution)/shard_map/ppermute | solution.py:158
  20.0 14.1 %collective-permute-start.7 = (bf16[320,512]{1,0:T(8,128)(2,1)S(1)}, bf16[320,512]{1,0:T(8,128)(2,1)S(1)}, u32[]{:S(2)}, u32[]{:S(2)}) collective-permute-start(bf16[320,512]{1,0:T(8,128)(2,1)S(1)} %shard_map.121), channel_id=1, source_target_pairs={{0,2},{2,0},{1,3},{3,1},{4,6},{6,4},{5,7},{7,5},{8,10},{10,8},{9,1... | collective-permute-start | bytes 983048 | tf_op jit(solution)/shard_map/ppermute | solution.py:158
  21.4 1.4 %collective-permute-start.3 = (bf16[320,256]{1,0:T(8,128)(2,1)S(1)}, bf16[320,256]{1,0:T(8,128)(2,1)S(1)}, u32[]{:S(2)}, u32[]{:S(2)}) collective-permute-start(bf16[320,256]{1,0:T(8,128)(2,1)S(1)} %get-tuple-element.29), channel_id=1, source_target_pairs={{0,1},{1,0},{2,3},{3,2},{4,5},{5,4},{6,7},{7,6},{8,9},{9,8},{10,11... | collective-permute-start | bytes 491528 | tf_op jit(solution)/shard_map/ppermute | solution.py:158
  21.6 1.5 %collective-permute-start.8 = (bf16[320,256]{1,0:T(8,128)(2,1)S(1)}, bf16[320,256]{1,0:T(8,128)(2,1)S(1)}, u32[]{:S(2)}, u32[]{:S(2)}) collective-permute-start(bf16[320,256]{1,0:T(8,128)(2,1)S(1)} %get-tuple-element.35), channel_id=1, source_target_pairs={{0,1},{1,0},{2,3},{3,2},{4,5},{5,4},{6,7},{7,6},{8,9},{9,8},{10,11... | collective-permute-start | bytes 491528 | tf_op jit(solution)/shard_map/ppermute | solution.py:158
  22.0 12.1 %collective-permute-start.10 = (bf16[320,256]{1,0:T(8,128)(2,1)S(1)}, bf16[320,256]{1,0:T(8,128)(2,1)S(1)}, u32[]{:S(2)}, u32[]{:S(2)}) collective-permute-start(bf16[320,256]{1,0:T(8,128)(2,1)S(1)} %shard_map.122), channel_id=1, source_target_pairs={{0,2},{2,0},{1,3},{3,1},{4,6},{6,4},{5,7},{7,5},{8,10},{10,8},{9,1... | collective-permute-start | bytes 491528 | tf_op jit(solution)/shard_map/ppermute | solution.py:158
  22.8 12.3 %collective-permute-start.2 = (bf16[320,256]{1,0:T(8,128)(2,1)S(1)}, bf16[320,256]{1,0:T(8,128)(2,1)S(1)}, u32[]{:S(2)}, u32[]{:S(2)}) collective-permute-start(bf16[320,256]{1,0:T(8,128)(2,1)S(1)} %get-tuple-element.27), channel_id=1, source_target_pairs={{0,1},{1,0},{2,3},{3,2},{4,5},{5,4},{6,7},{7,6},{8,9},{9,8},{10,11... | collective-permute-start | bytes 491528 | tf_op jit(solution)/shard_map/ppermute | solution.py:158
  23.1 14.1 %collective-permute-start.4 = (bf16[320,256]{1,0:T(8,128)(2,1)S(1)}, bf16[320,256]{1,0:T(8,128)(2,1)S(1)}, u32[]{:S(2)}, u32[]{:S(2)}) collective-permute-start(bf16[320,256]{1,0:T(8,128)(2,1)S(1)} %shard_map.120), channel_id=1, source_target_pairs={{0,2},{2,0},{1,3},{3,1},{4,6},{6,4},{5,7},{7,5},{8,10},{10,8},{9,1... | collective-permute-start | bytes 491528 | tf_op jit(solution)/shard_map/ppermute | solution.py:158

commit v4 on v3

v4 whole, which is shorter than its diff:
```python
import functools

import jax
import jax.numpy as jnp
from jax import lax
from jax.experimental import pallas as pl
from jax.experimental.pallas import tpu as pltpu
from jax.sharding import PartitionSpec as P

DH = 128
EPS = 1e-05
SPANS = ((0, 2), (2, 3), (3, 4))
OWN_SPANS = ((0, 1), (1, 2), (2, 3), (3, 4))
f32 = jnp.float32
bf16 = jnp.bfloat16
HIGHEST = lax.Precision.HIGHEST
VMEM_LIMIT = 32 * 1024 * 1024

VMEM = pl.BlockSpec(memory_space=pltpu.VMEM)
SMEM = pl.BlockSpec(memory_space=pltpu.SMEM)
HBM = pl.BlockSpec(memory_space=pltpu.HBM)
ANY = pl.BlockSpec(memory_space=pl.ANY)
Shape = jax.ShapeDtypeStruct


def call(body, out_shape, specs, flops, nbytes, out_specs=None, limit=VMEM_LIMIT, **more):
    single = not isinstance(out_shape, (tuple, list))
    if out_specs is None:
        out_specs = VMEM if single else [VMEM] * len(out_shape)
    return pl.pallas_call(
        body,
        out_shape=out_shape,
        in_specs=specs,
        out_specs=out_specs,
        compiler_params=pltpu.CompilerParams(vmem_limit_bytes=limit),
        cost_estimate=pl.CostEstimate(flops=flops, bytes_accessed=nbytes, transcendentals=0),
        **more,
    )


def columns(h):
    return slice(h * DH, (h + 1) * DH)


def dot(a, b, dims):
    return lax.dot_general(a, b, (dims, ((), ())), preferred_element_type=f32)


def base_kernel(
    offsets_ref, lengths_ref, q_ref, k_ref, v_ref, oq_ref, ok_ref, ov_ref, after_ref, out_ref, queries_ref, valid_ref
):
    tokens, (opts, slots, _) = q_ref.shape[0], oq_ref.shape
    rows, most = tokens + opts * slots, opts * slots
    row = lax.broadcasted_iota(jnp.int32, (rows, 1), 0)
    limit, end = row + 1, jnp.full((rows, 1), tokens, jnp.int32)
    for o in range(opts):
        start = tokens + o * slots
        limit = jnp.where(row >= start, offsets_ref[:, o:o + 1], limit)
        end = jnp.where(row >= start, start + lengths_ref[:, o:o + 1], end)
    valid_ref[...] = jnp.broadcast_to((row < end).astype(f32), valid_ref.shape)
    mask = lax.broadcasted_iota(jnp.int32, (rows, tokens), 1) < limit
    i = lax.broadcasted_iota(jnp.int32, (most, most), 0)
    j = lax.broadcasted_iota(jnp.int32, (most, most), 1)
    own = j <= i
    for o in range(1, opts):
        own = own & ((i < o * slots) | (j >= o * slots))
    for h in range(out_ref.shape[1] // DH):
        cols = columns(h)
        oq, ok, ov = (jnp.concatenate([ref[o, :, cols].astype(bf16) for o in range(opts)]) for ref in (oq_ref, ok_ref, ov_ref))
        q = jnp.concatenate([q_ref[:, cols].astype(bf16), oq])
        queries_ref[:, cols] = q
        scores = jnp.where(mask, dot(q, k_ref[:, cols].astype(bf16), ((1,), (1,))), 0.0).astype(bf16)
        own_scores = jnp.where(own, dot(oq, ok, ((1,), (1,))), 0.0).astype(bf16)
        out = dot(scores, v_ref[:, cols].astype(bf16), ((1,), (0,)))
        out_ref[:tokens, cols] = out[:tokens]
        out_ref[tokens:, cols] = out[tokens:] + dot(own_scores, ov, ((1,), (0,)))


def add_kernel(*refs):
    out_ref = refs[-1]
    total = refs[0][:out_ref.shape[0]].astype(f32)
    for ref in refs[1:-1]:
        total = total + ref[:out_ref.shape[0]].astype(f32)
    out_ref[...] = total.astype(out_ref.dtype)


def add(*terms, rows=None):
    shape = (rows or terms[0].shape[0],) + terms[0].shape[1:]
    return call(
        add_kernel, Shape(shape, bf16), [VMEM] * len(terms), len(terms) * terms[0].size, 6 * len(terms) * terms[0].size,
    )(*terms)


def normed_kernel(spans, use_ref, valid_ref, gain_ref, queries_ref, base_ref, *rest):
    parts, out_ref = rest[:-1], rest[-1]
    for h in range(out_ref.shape[1] // DH):
        prefix = jnp.zeros((DH, DH), f32)
        for n, (low, high) in enumerate(spans):
            if low <= h < high:
                prefix = prefix + jnp.where(use_ref[n:n + 1] > 0.0, parts[n][h - low].astype(f32), 0.0)
        cols = columns(h)
        out = base_ref[:, cols] + dot(queries_ref[:, cols], prefix.astype(bf16), ((1,), (0,)))
        scale = lax.rsqrt(jnp.mean(out * out, axis=1, keepdims=True) + EPS)
        out_ref[:, cols] = (out * (scale * valid_ref[...]) * gain_ref[:, cols]).astype(out_ref.dtype)


def project_kernel(spans, rows_ref, weight_ref, *outs):
    for (start, end), out in zip(spans, outs):
        out[...] = jnp.dot(rows_ref[...], weight_ref[:, start:end], preferred_element_type=f32).astype(out.dtype)


def project(rows, weight, spans, dtype):
    count, (depth, width) = rows.shape[0], weight.shape
    return call(
        functools.partial(project_kernel, spans), [Shape((count, b - a), dtype) for a, b in spans], [VMEM] * 2,
        2 * count * depth * width, 2 * depth * (count + width) + 4 * count * width,
    )(rows, weight)


def final_kernel(spans, counts, starts, n_before, *rest):
    terms, (ctx_ref, opt_ref, buf, sem) = rest[:len(starts)], rest[-4:]
    tokens, (opts, slots, _) = ctx_ref.shape[0], opt_ref.shape
    low, high = spans[0][0], spans[-1][1]
    flat = iter(zip(terms, starts))
    for (at, end), count in zip(spans, counts):
        total = 0.0
        for term, start in [next(flat) for _ in range(count)]:
            total = total + term[:, start:start + end - at].astype(f32)
        buf[:, at - low:end - low] = total.astype(buf.dtype)
    copies = [pltpu.make_async_copy(buf.at[:tokens], ctx_ref.at[:, low:high], sem.at[0])]
    for o in range(opts):
        start = tokens + o * slots
        copies.append(pltpu.make_async_copy(buf.at[start:start + slots], opt_ref.at[o, :, low:high], sem.at[o + 1]))
    for copy in copies:
        copy.start()
    for copy in copies:
        copy.wait()


def final(spans, terms, shapes, before=()):
    flat, starts = zip(*sum(terms, []))
    rows, width, opts, n = flat[0].shape[0], spans[-1][1] - spans[0][0], shapes[1].shape[0], len(flat)
    return call(
        functools.partial(final_kernel, spans, [len(some) for some in terms], starts, len(before)), shapes,
        [VMEM] * n + [HBM] * len(before),
        rows * width * n, 4 * rows * width * n, out_specs=[HBM, HBM],
        input_output_aliases={n: 0, n + 1: 1} if before else {},
        scratch_shapes=[pltpu.VMEM((rows, width), bf16), pltpu.SemaphoreType.DMA((1 + opts,))],
    )(*flat, *before)


def ring(value, axis, size, shift):
    return lax.ppermute(value, axis, [(i, (i + shift) % size) for i in range(size)])


def swap(value, axis, size, mask):
    return lax.ppermute(value, axis, [(i, i ^ mask) for i in range(size)])


def upward(value, axis, size, mask):
    return lax.ppermute(value, axis, [(i, i ^ mask) for i in range(size) if not i & mask])


def exclusive(state, axis, size):
    place = lax.axis_index(axis)
    parts, use, windows, step = [], [], [state], 1
    while step < size:
        send = upward if 2 * step == size else swap
        parts.append(send(windows[-1], axis, size, step))
        use.append(place & step != 0)
        step *= 2
        if step < size:
            windows.append(add(windows[-1], parts[-1]))
    return parts, use, windows[:2][-1]


def on_device(sizes, q, k, v, oq, ok, ov, offsets, lengths, gain, weight):
    n_seq, n_head, n_sub = sizes
    tokens, feats = q.shape
    opts, slots, _ = oq.shape
    rows = tokens + opts * slots
    heads = feats // DH
    width = weight.shape[1] // (n_head * n_sub)
    head, sub = lax.axis_index("head"), lax.axis_index("sub")

    state = lax.cond(
        lax.axis_index("seq") < n_seq - 1,
        lambda: jnp.einsum(
            "thd,the->hde", k.reshape(tokens, heads, DH), v.reshape(tokens, heads, DH), precision=lax.Precision.DEFAULT
        ).astype(bf16),
        lambda: jnp.zeros((heads, DH, DH), bf16),
    )
    parts, use, window = exclusive(state, "seq", n_seq)
    parts = [(part, (0, heads), used) for part, used in zip(parts, use)]

    base, queries, valid = call(
        base_kernel, [Shape((rows, feats), f32), Shape((rows, feats), bf16), Shape((rows, DH), f32)], [VMEM] * 8 + [ANY],
        4 * rows * rows * feats, 16 * rows * feats,
    )(offsets[None], lengths[None], q, k, v, oq, ok, ov, window)
    use = jnp.broadcast_to(jnp.stack([p[2] for p in parts]).astype(f32)[:, None], (len(parts), DH))
    normed = call(
        functools.partial(normed_kernel, [p[1] for p in parts]), Shape((rows, feats), bf16),
        [VMEM] * (5 + len(parts)), 2 * rows * DH * feats, 10 * rows * feats,
    )(use, valid, gain[None], queries, base, *[p[0] for p in parts])

    def blocks(d):
        at = [((head + d) % n_head * n_sub + (sub + s) % n_sub) * width for s in range(n_sub)]
        return [lax.dynamic_slice_in_dim(later, x, width, 1) for x in at]

    def summed(d, spans, first=0):
        ours, *theirs = weights[d]
        some = [spans for spans in (spans[:first], spans[first:]) if spans]
        theirs = [sum([list(project(normed, w, spans, bf16)) for spans in some], []) for w in theirs]
        ours = sum([list(project(normed, ours, spans, f32)) for spans in some], [])
        theirs = [[ring(x, "sub", n_sub, s + 1) for x in xs] for s, xs in enumerate(theirs)]
        return list(zip(ours, *theirs))

    later, _ = lax.optimization_barrier((weight, state))
    weights = [blocks(d) for d in range(n_head)]
    spans, own_spans = ([(width * a // 4, width * b // 4) for a, b in some] for some in (SPANS, OWN_SPANS))
    received = []
    for d in range(1, n_head):
        for (low, high), terms in zip(spans, summed(d, spans, 1)):
            received.append((low, high, ring(add(*terms), "head", n_head, d)))
    own = summed(0, own_spans)
    shapes = (Shape((tokens, width), bf16), Shape((opts, slots, width), bf16))
    out, last = (), spans[-1][0]
    for some in ([span for span in own_spans if span[1] <= last], [span for span in own_spans if span[0] >= last]):
        if some:
            terms = [
                [(x, 0) for x in own[own_spans.index(span)]]
                + [(x, span[0] - low) for low, high, x in received if low <= span[0] and span[1] <= high]
                for span in some
            ]
            out = final(some, terms, shapes, out)
    return tuple(out)


def solution(mesh):
    placed = (
        P(("grp", "seq"), ("head", "sub")),
        P(("grp", "seq"), ("head", "sub")),
        P(("grp", "seq"), ("head", "sub")),
        P(("grp", "seq"), None, ("head", "sub")),
        P(("grp", "seq"), None, ("head", "sub")),
        P(("grp", "seq"), None, ("head", "sub")),
        P(("grp", "seq")),
        P(("grp", "seq")),
        P(("head", "sub")),
        P(("head", "sub"), None),
    )
    sizes = tuple(mesh.shape[a] for a in ("seq", "head", "sub"))
    return jax.shard_map(
        functools.partial(on_device, sizes),
        mesh=mesh,
        in_specs=placed,
        out_specs=(P(("grp", "seq"), ("head", "sub")), P(("grp", "seq"), None, ("head", "sub"))),
        check_vma=False,
    )
```

time: 38.1 us -> 36.5 us (0.958)
  waiting for transfers between devices: 15 us -> 12.1 us
  starting transfers between devices: 10.6 us -> 13.1 us
  Pallas kernels: 7.15 us -> 5.61 us
    ppermute x0 -> x1, starting transfers between devices: none -> 4.66 us  [upward(): lax.ppermute(value, axis, [(i, i ^ mask) for i in range(size) if not i &...]
    ppermute x2 -> x1, starting transfers between devices: 5.91 us -> 3.09 us  [swap(): return lax.ppermute(value, axis, [(i, i ^ mask) for i in range(size)])]
    ppermute x2 -> x1, waiting for transfers between devices: 3.38 us -> 0.66 us  [swap(): return lax.ppermute(value, axis, [(i, i ^ mask) for i in range(size)])]
    pallas_call x3, Pallas kernels: 4.45 us -> 2.71 us  [the longest x2 1.68 us: final(): call(functools.partial(final_kernel, spans, [len(some) for some in terms]...]
    ppermute x9 -> x10, waiting for transfers between devices: 11.6 us -> 10.1 us  [ring(): lax.ppermute(value, axis, [(i, (i + shift) % size) for i in range(size)])]
    ppermute x0 -> x1, waiting for transfers between devices: none -> 1.33 us  [upward(): lax.ppermute(value, axis, [(i, i ^ mask) for i in range(size) if not i &...]
    ppermute x9 -> x10, starting transfers between devices: 4.67 us -> 5.3 us  [ring(): lax.ppermute(value, axis, [(i, (i + shift) % size) for i in range(size)])]
    pallas_call x4 -> x6, Pallas kernels: 2 us -> 2.32 us  [project(): call(functools.partial(project_kernel, spans), [Shape((count, b - a), dty...]
  transfers between devices with their start and end apart: 11 -> 12, of which waited for: 5 -> 5; matrix products, arithmetic and copies ran while one was open for 7% -> 8% of each run, Pallas kernels for 14% -> 11%
where the time goes in v4:
time: 36.5 us; the launch traced here: 36 us
  starting transfers between devices  13.1 us (36%)
  waiting for transfers between devices  12.1 us (33%)
  Pallas kernels  5.61 us (15%)
  local copies, waits for them, and re-layouts  2.88 us (8%)
  matrix products  1.39 us (4%)
  between operations  0.88 us (2%)
    ppermute x10, waiting for transfers between devices, ring(): lax.ppermute(value, axis, [(i, (i + shift) % size) for i in range(size)])  10.1 us
    ppermute x10, starting transfers between devices, ring(): lax.ppermute(value, axis, [(i, (i + shift) % size) for i in range(size)])  5.3 us
    ppermute x1, starting transfers between devices, upward(): lax.ppermute(value, axis, [(i, i ^ mask) for i in range(size) if not i &...  4.66 us
    ppermute x1, starting transfers between devices, swap(): return lax.ppermute(value, axis, [(i, i ^ mask) for i in range(size)])  3.09 us
    dynamic_slice x1, local copies, waits for them, and re-layouts, blocks(): return [lax.dynamic_slice_in_dim(later, x, width, 1) for x in at]  2.76 us
    pallas_call x6, Pallas kernels, project(): call(functools.partial(project_kernel, spans), [Shape((count, b - a), dty...  2.32 us
    pallas_call x2, Pallas kernels, final(): call(functools.partial(final_kernel, spans, [len(some) for some in terms]...  1.68 us
    dot_general x1, matrix products, on_device(): jnp.einsum('thd,the->hde', k.reshape(tokens, heads, DH), v.reshape(tokens...  1.39 us
  transfers between devices with their start and end apart: 12, of which 5 were waited for; matrix products, arithmetic and copies ran while one was open for 8% of the time, Pallas kernels for 11%

profile of v4, /device:TPU:0, one launch (start us, length us, event | category | flops | bytes accessed | tf_op | source)
XLA Modules:
  0.0 36.0 jit_solution(9942993400249779875)
XLA Ops:
  0.6 1.4 %conditional.1 = (bf16[4,128,128]{2,1,0:T(8,128)(2,1)S(1)}) conditional(s32[]{:T(128)} %convert_element_type.14, () %tuple.14, (f32[192,512]{1,0:T(8,128)}, f32[192,512]{1,0:T(8,128)}) %tuple.15), branch_computations={%region_0.0_spmd, %region_1.0_spmd} | conditional | flops 25165824 | bytes 917512 | solution.py:186
  0.7 1.4 %convolution_convert_fusion = bf16[4,128,128]{2,1,0:T(8,128)(2,1)S(1)} fusion(f32[192,512]{1,0:T(8,128)} %get-tuple-element.8, f32[192,512]{1,0:T(8,128)} %get-tuple-element.4), kind=kOutput, calls=%fused_computation | convolution fusion | flops 25165824 | bytes 917504 | tf_op jit(solution)/shard_map/cond/branch_1_fun/thd,the->hde/dot_general | solution.py:188
  2.0 3.1 %collective-permute-start = (bf16[4,128,128]{2,1,0:T(8,128)(2,1)S(1)}, bf16[4,128,128]{2,1,0:T(8,128)(2,1)S(1)}, u32[]{:S(2)}, u32[]{:S(2)}) collective-permute-start(bf16[4,128,128]{2,1,0:T(8,128)(2,1)S(1)} %get-tuple-element.51.refs_0_), channel_id=1, source_target_pairs={{0,4},{4,0},{8,12},{12,8},{1,5},{5,1},{9,13},{13,9},{2,6},{6,2},{1... | collective-permute-start | bytes 393224 | tf_op jit(solution)/shard_map/ppermute | solution.py:157
  5.1 0.0 copy-start
  5.1 0.0 copy-start.1
  5.1 0.0 copy-start.2
  5.1 0.0 copy-start.3
  5.1 0.0 copy-start.5
  5.2 0.0 copy-start.6
  5.2 0.0 copy-start.7
  5.2 0.0 copy-start.8
  5.2 0.0 copy-start.4
  5.2 2.8 %constant_dynamic-slice_fusion = (bf16[512,1024]{1,0:T(8,128)(2,1)S(1)}, bf16[512,1024]{1,0:T(8,128)(2,1)S(1)}, bf16[512,1024]{1,0:T(8,128)(2,1)S(1)}, bf16[512,1024]{1,0:T(8,128)(2,1)S(1)}) fusion(bf16[512,4096]{1,0:T(8,128)(2,1)} %param.21, s32[]{:T(128)S(6)} %select_n.46, s32[]{:T(128)S(6)} %select_n.45, s32[]{:T(128)S(6)} %select_n.43, s32[]{:T(128)S(6)} %select_n.41), kind=kLoop, calls=%fused_computation.6 | loop fusion | bytes 8388624 | tf_op jit(solution)/shard_map/dynamic_slice | solution.py:208
  8.0 0.7 %collective-permute-done.refs_1_.rest_0_ = bf16[4,128,128]{2,1,0:T(8,128)(2,1)S(1)} collective-permute-done((bf16[4,128,128]{2,1,0:T(8,128)(2,1)S(1)}, bf16[4,128,128]{2,1,0:T(8,128)(2,1)S(1)}, u32[]{:S(2)}, u32[]{:S(2)}) %collective-permute-start) | collective-permute-done | bytes 131104 | tf_op jit(solution)/shard_map/ppermute | solution.py:157
  8.7 4.7 %collective-permute-start.1 = (bf16[4,128,128]{2,1,0:T(8,128)(2,1)S(1)}, bf16[4,128,128]{2,1,0:T(8,128)(2,1)S(1)}, u32[]{:S(2)}, u32[]{:S(2)}) collective-permute-start(bf16[4,128,128]{2,1,0:T(8,128)(2,1)S(1)} %shard_map.113.after_ref), channel_id=1, source_target_pairs={{0,8},{4,12},{1,9},{5,13},{2,10},{6,14},{3,11},{7,15},{16,24},{20,... | collective-permute-start | bytes 393224 | tf_op jit(solution)/shard_map/ppermute | solution.py:161
  13.3 0.1 add_convert_fusion
  13.4 0.0 copy-done
  13.4 0.0 copy-done.1
  13.4 0.0 copy-done.2
  13.4 0.0 copy-done.3
  13.4 0.0 copy-done.5
  13.5 0.0 copy-done.6
  13.5 0.0 copy-done.7
  13.5 0.0 copy-done.8
  13.5 1.0 %shard_map.114 = (f32[320,512]{1,0:T(8,128)S(1)}, bf16[320,512]{1,0:T(8,128)(2,1)S(1)}, f32[320,128]{1,0:T(8,128)S(1)}) custom-call(s32[1,2]{1,0:T(1,128)S(1)} %bitcast.20, s32[1,2]{1,0:T(1,128)S(1)} %bitcast.21, f32[192,512]{1,0:T(8,128)S(1)} %copy-done, f32[192,512]{1,0:T(8,128)S(1)} %copy-done.7, f32[192,512]{1,0:T(8,128)S(1)} %copy-done.8, ...), custom_call_target="tpu_custom_call" | custom-call | flops 209715200 | bytes 2621440 | tf_op jit(solution)/shard_map/pallas_call | solution.py:196
  14.5 1.3 %collective-permute-done.1.rest_1_ = bf16[4,128,128]{2,1,0:T(8,128)(2,1)S(1)} collective-permute-done((bf16[4,128,128]{2,1,0:T(8,128)(2,1)S(1)}, bf16[4,128,128]{2,1,0:T(8,128)(2,1)S(1)}, u32[]{:S(2)}, u32[]{:S(2)}) %collective-permute-start.1) | collective-permute-done | bytes 131104 | tf_op jit(solution)/shard_map/ppermute | solution.py:161
  15.8 0.1 broadcast_in_dim.15.use_ref
  15.9 0.0 copy-done.4
  15.9 0.4 %shard_map.115.rows_ref = bf16[320,512]{1,0:T(8,128)(2,1)S(1)} custom-call(f32[2,128]{1,0:T(2,128)S(1)} %broadcast_in_dim.15.use_ref, f32[320,128]{1,0:T(8,128)S(1)} %get-tuple-element.29.valid_ref, f32[1,512]{1,0:T(1,128)S(1)} %bitcast.19, bf16[320,512]{1,0:T(8,128)(2,1)S(1)} %get-tuple-element.30.queries_ref, f32[320,512]{1,0:T(8,128)S(1)} %get-tuple-element.31.base_ref, ...), custom_call_target="tpu_custom_call" | custom-call | flops 41943040 | bytes 1638400 | tf_op jit(solution)/shard_map/pallas_call | solution.py:201
  16.4 0.3 shard_map.122
  16.7 0.1 collective-permute-start.6
  16.8 0.3 shard_map.119
  17.1 0.6 %collective-permute-start.3 = (bf16[320,256]{1,0:T(8,128)(2,1)S(1)}, bf16[320,256]{1,0:T(8,128)(2,1)S(1)}, u32[]{:S(2)}, u32[]{:S(2)}) collective-permute-start(bf16[320,256]{1,0:T(8,128)(2,1)S(1)} %get-tuple-element.36), channel_id=1, source_target_pairs={{0,1},{1,0},{2,3},{3,2},{4,5},{5,4},{6,7},{7,6},{8,9},{9,8},{10,11... | collective-permute-start | bytes 491528 | tf_op jit(solution)/shard_map/ppermute | solution.py:153
  17.7 0.1 collective-permute-start.10
  17.8 0.3 shard_map.121.refs_0_
  18.1 0.3 collective-permute-done.6.refs_1_
  18.4 0.1 shard_map.123
  18.5 1.6 %collective-permute-start.7 = (bf16[320,512]{1,0:T(8,128)(2,1)S(1)}, bf16[320,512]{1,0:T(8,128)(2,1)S(1)}, u32[]{:S(2)}, u32[]{:S(2)}) collective-permute-start(bf16[320,512]{1,0:T(8,128)(2,1)S(1)} %shard_map.123), channel_id=1, source_target_pairs={{0,2},{2,0},{1,3},{3,1},{4,6},{6,4},{5,7},{7,5},{8,10},{10,8},{9,1... | collective-permute-start | bytes 983048 | tf_op jit(solution)/shard_map/ppermute | solution.py:153
  20.0 0.5 %shard_map.117 = (bf16[320,256]{1,0:T(8,128)(2,1)S(1)}, bf16[320,256]{1,0:T(8,128)(2,1)S(1)}, bf16[320,256]{1,0:T(8,128)(2,1)S(1)}, bf16[320,256]{1,0:T(8,128)(2,1)S(1)}) custom-call(bf16[320,512]{1,0:T(8,128)(2,1)S(1)} %shard_map.115.rows_ref, bf16[512,1024]{1,0:T(8,128)(2,1)S(1)} %get-tuple-element.49.weight_ref), custom_call_target="tpu_custom_call" | custom-call | flops 335544320 | bytes 2686976 | tf_op jit(solution)/shard_map/pallas_call | solution.py:114
  20.5 0.1 collective-permute-start.5
  20.6 0.5 %collective-permute-start.8 = (bf16[320,256]{1,0:T(8,128)(2,1)S(1)}, bf16[320,256]{1,0:T(8,128)(2,1)S(1)}, u32[]{:S(2)}, u32[]{:S(2)}) collective-permute-start(bf16[320,256]{1,0:T(8,128)(2,1)S(1)} %get-tuple-element.40), channel_id=1, source_target_pairs={{0,1},{1,0},{2,3},{3,2},{4,5},{5,4},{6,7},{7,6},{8,9},{9,8},{10,11... | collective-permute-start | bytes 491528 | tf_op jit(solution)/shard_map/ppermute | solution.py:153
  21.1 0.3 shard_map.118
  21.4 0.0 collective-permute-done.10.refs_1_
  21.4 0.1 collective-permute-start.9
  21.6 0.0 collective-permute-done.3.refs_1_
  21.6 0.6 %collective-permute-start.11 = (bf16[320,256]{1,0:T(8,128)(2,1)S(1)}, bf16[320,256]{1,0:T(8,128)(2,1)S(1)}, u32[]{:S(2)}, u32[]{:S(2)}) collective-permute-start(bf16[320,256]{1,0:T(8,128)(2,1)S(1)} %shard_map.124), channel_id=1, source_target_pairs={{0,2},{2,0},{1,3},{3,1},{4,6},{6,4},{5,7},{7,5},{8,10},{10,8},{9,1... | collective-permute-start | bytes 491528 | tf_op jit(solution)/shard_map/ppermute | solution.py:153
  22.3 0.0 collective-permute-done.5.rest_1_
  22.3 0.2 collective-permute-start.2
  22.5 0.0 collective-permute-done.8.rest_4_
  22.5 1.5 %collective-permute-start.4 = (bf16[320,256]{1,0:T(8,128)(2,1)S(1)}, bf16[320,256]{1,0:T(8,128)(2,1)S(1)}, u32[]{:S(2)}, u32[]{:S(2)}) collective-permute-start(bf16[320,256]{1,0:T(8,128)(2,1)S(1)} %shard_map.120), channel_id=1, source_target_pairs={{0,2},{2,0},{1,3},{3,1},{4,6},{6,4},{5,7},{7,5},{8,10},{10,8},{9,1... | collective-permute-start | bytes 491528 | tf_op jit(solution)/shard_map/ppermute | solution.py:153
  24.0 0.5 %shard_map.116 = (f32[320,256]{1,0:T(8,128)S(1)}, f32[320,256]{1,0:T(8,128)S(1)}, f32[320,256]{1,0:T(8,128)S(1)}, f32[320,256]{1,0:T(8,128)S(1)}) custom-call(bf16[320,512]{1,0:T(8,128)(2,1)S(1)} %shard_map.115.rows_ref, bf16[512,1024]{1,0:T(8,128)(2,1)S(1)} %get-tuple-element.50.weight_ref), custom_call_target="tpu_custom_call" | custom-call | flops 335544320 | bytes 2686976 | tf_op jit(solution)/shard_map/pallas_call | solution.py:114
  24.5 0.0 collective-permute-done.9.rest_7_
  24.5 8.1 %collective-permute-done.11.rest_8_ = bf16[320,256]{1,0:T(8,128)(2,1)S(1)} collective-permute-done((bf16[320,256]{1,0:T(8,128)(2,1)S(1)}, bf16[320,256]{1,0:T(8,128)(2,1)S(1)}, u32[]{:S(2)}, u32[]{:S(2)}) %collective-permute-start.11) | collective-permute-done | bytes 163872 | tf_op jit(solution)/shard_map/ppermute | solution.py:153
  32.6 0.0 collective-permute-done.7.rest_2_.rest_5_
  32.6 0.9 %shard_map.125 = (bf16[192,1024]{1,0:T(8,128)(2,1)}, bf16[2,64,1024]{2,1,0:T(8,128)(2,1)}) custom-call(f32[320,256]{1,0:T(8,128)S(1)} %get-tuple-element.37.rest_0_, bf16[320,256]{1,0:T(8,128)(2,1)S(1)} %collective-permute-done.5.rest_1_, bf16[320,512]{1,0:T(8,128)(2,1)S(1)} %collective-permute-done.7.rest_2_.rest_5_, ...), custom_call_target="tpu_custom_call" | custom-call | flops 2211840 | bytes 8847360 | tf_op jit(solution)/shard_map/pallas_call | solution.py:143
  33.5 0.0 collective-permute-done.2.rest_1_
  33.6 1.8 %collective-permute-done.4.rest_2_ = bf16[320,256]{1,0:T(8,128)(2,1)S(1)} collective-permute-done((bf16[320,256]{1,0:T(8,128)(2,1)S(1)}, bf16[320,256]{1,0:T(8,128)(2,1)S(1)}, u32[]{:S(2)}, u32[]{:S(2)}) %collective-permute-start.4) | collective-permute-done | bytes 163872 | tf_op jit(solution)/shard_map/ppermute | solution.py:153
  35.3 0.7 %shard_map.126 = (bf16[192,1024]{1,0:T(8,128)(2,1)}, bf16[2,64,1024]{2,1,0:T(8,128)(2,1)}) custom-call(f32[320,256]{1,0:T(8,128)S(1)} %get-tuple-element.33.rest_0_, bf16[320,256]{1,0:T(8,128)(2,1)S(1)} %collective-permute-done.2.rest_1_, bf16[320,256]{1,0:T(8,128)(2,1)S(1)} %collective-permute-done.4.rest_2_, ...), custom_call_target="tpu_custom_call", output_to_operand_aliasing={{0}: (3, {}), {1}: (4, {})} | custom-call | flops 245760 | bytes 983040 | tf_op jit(solution)/shard_map/pallas_call | solution.py:143
  (3 shorter events, 0.1 us)
Async XLA Ops:
  2.0 6.6 %collective-permute-start = (bf16[4,128,128]{2,1,0:T(8,128)(2,1)S(1)}, bf16[4,128,128]{2,1,0:T(8,128)(2,1)S(1)}, u32[]{:S(2)}, u32[]{:S(2)}) collective-permute-start(bf16[4,128,128]{2,1,0:T(8,128)(2,1)S(1)} %get-tuple-element.51.refs_0_), channel_id=1, source_target_pairs={{0,4},{4,0},{8,12},{12,8},{1,5},{5,1},{9,13},{13,9},{2,6},{6,2},{1... | collective-permute-start | bytes 393224 | tf_op jit(solution)/shard_map/ppermute | solution.py:157
  5.1 8.3 %copy-start = (f32[192,512]{1,0:T(8,128)S(1)}, f32[192,512]{1,0:T(8,128)}, u32[]{:S(2)}) copy-start(f32[192,512]{1,0:T(8,128)} %q_ref.1) | copy-start | bytes 1179652
  5.1 8.3 %copy-start.1 = (f32[2,64,512]{2,1,0:T(8,128)S(1)}, f32[2,64,512]{2,1,0:T(8,128)}, u32[]{:S(2)}) copy-start(f32[2,64,512]{2,1,0:T(8,128)} %oq_ref.1) | copy-start | bytes 786436
  5.1 8.3 %copy-start.2 = (f32[2,64,512]{2,1,0:T(8,128)S(1)}, f32[2,64,512]{2,1,0:T(8,128)}, u32[]{:S(2)}) copy-start(f32[2,64,512]{2,1,0:T(8,128)} %ok_ref.1) | copy-start | bytes 786436
  5.1 8.3 %copy-start.3 = (f32[2,64,512]{2,1,0:T(8,128)S(1)}, f32[2,64,512]{2,1,0:T(8,128)}, u32[]{:S(2)}) copy-start(f32[2,64,512]{2,1,0:T(8,128)} %ov_ref.1) | copy-start | bytes 786436
  5.1 8.3 %copy-start.5 = (s32[2]{0:T(128)S(1)}, s32[2]{0:T(128)}, u32[]{:S(2)}) copy-start(s32[2]{0:T(128)} %param.18) | copy-start | bytes 28
  5.2 8.3 %copy-start.6 = (s32[2]{0:T(128)S(1)}, s32[2]{0:T(128)}, u32[]{:S(2)}) copy-start(s32[2]{0:T(128)} %param.19) | copy-start | bytes 28
  5.2 8.3 %copy-start.7 = (f32[192,512]{1,0:T(8,128)S(1)}, f32[192,512]{1,0:T(8,128)}, u32[]{:S(2)}) copy-start(f32[192,512]{1,0:T(8,128)} %k_ref.1) | copy-start | bytes 1179652
  5.2 8.3 %copy-start.8 = (f32[192,512]{1,0:T(8,128)S(1)}, f32[192,512]{1,0:T(8,128)}, u32[]{:S(2)}) copy-start(f32[192,512]{1,0:T(8,128)} %v_ref.1) | copy-start | bytes 1179652
  5.2 10.7 %copy-start.4 = (f32[512]{0:T(512)S(1)}, f32[512]{0:T(512)}, u32[]{:S(2)}) copy-start(f32[512]{0:T(512)} %param.20) | copy-start | bytes 6148
  8.7 7.2 %collective-permute-start.1 = (bf16[4,128,128]{2,1,0:T(8,128)(2,1)S(1)}, bf16[4,128,128]{2,1,0:T(8,128)(2,1)S(1)}, u32[]{:S(2)}, u32[]{:S(2)}) collective-permute-start(bf16[4,128,128]{2,1,0:T(8,128)(2,1)S(1)} %shard_map.113.after_ref), channel_id=1, source_target_pairs={{0,8},{4,12},{1,9},{5,13},{2,10},{6,14},{3,11},{7,15},{16,24},{20,... | collective-permute-start | bytes 393224 | tf_op jit(solution)/shard_map/ppermute | solution.py:161
  16.7 1.7 %collective-permute-start.6 = (bf16[320,512]{1,0:T(8,128)(2,1)S(1)}, bf16[320,512]{1,0:T(8,128)(2,1)S(1)}, u32[]{:S(2)}, u32[]{:S(2)}) collective-permute-start(bf16[320,512]{1,0:T(8,128)(2,1)S(1)} %shard_map.122), channel_id=1, source_target_pairs={{0,1},{1,0},{2,3},{3,2},{4,5},{5,4},{6,7},{7,6},{8,9},{9,8},{10,11... | collective-permute-start | bytes 983048 | tf_op jit(solution)/shard_map/ppermute | solution.py:153
  17.1 4.5 %collective-permute-start.3 = (bf16[320,256]{1,0:T(8,128)(2,1)S(1)}, bf16[320,256]{1,0:T(8,128)(2,1)S(1)}, u32[]{:S(2)}, u32[]{:S(2)}) collective-permute-start(bf16[320,256]{1,0:T(8,128)(2,1)S(1)} %get-tuple-element.36), channel_id=1, source_target_pairs={{0,1},{1,0},{2,3},{3,2},{4,5},{5,4},{6,7},{7,6},{8,9},{9,8},{10,11... | collective-permute-start | bytes 491528 | tf_op jit(solution)/shard_map/ppermute | solution.py:153
  17.7 3.8 %collective-permute-start.10 = (bf16[320,256]{1,0:T(8,128)(2,1)S(1)}, bf16[320,256]{1,0:T(8,128)(2,1)S(1)}, u32[]{:S(2)}, u32[]{:S(2)}) collective-permute-start(bf16[320,256]{1,0:T(8,128)(2,1)S(1)} %get-tuple-element.44), channel_id=1, source_target_pairs={{0,1},{1,0},{2,3},{3,2},{4,5},{5,4},{6,7},{7,6},{8,9},{9,8},{10,11... | collective-permute-start | bytes 491528 | tf_op jit(solution)/shard_map/ppermute | solution.py:153
  18.5 14.1 %collective-permute-start.7 = (bf16[320,512]{1,0:T(8,128)(2,1)S(1)}, bf16[320,512]{1,0:T(8,128)(2,1)S(1)}, u32[]{:S(2)}, u32[]{:S(2)}) collective-permute-start(bf16[320,512]{1,0:T(8,128)(2,1)S(1)} %shard_map.123), channel_id=1, source_target_pairs={{0,2},{2,0},{1,3},{3,1},{4,6},{6,4},{5,7},{7,5},{8,10},{10,8},{9,1... | collective-permute-start | bytes 983048 | tf_op jit(solution)/shard_map/ppermute | solution.py:153
  20.5 1.7 %collective-permute-start.5 = (bf16[320,256]{1,0:T(8,128)(2,1)S(1)}, bf16[320,256]{1,0:T(8,128)(2,1)S(1)}, u32[]{:S(2)}, u32[]{:S(2)}) collective-permute-start(bf16[320,256]{1,0:T(8,128)(2,1)S(1)} %get-tuple-element.38), channel_id=1, source_target_pairs={{0,1},{1,0},{2,3},{3,2},{4,5},{5,4},{6,7},{7,6},{8,9},{9,8},{10,11... | collective-permute-start | bytes 491528 | tf_op jit(solution)/shard_map/ppermute | solution.py:153
  20.6 1.9 %collective-permute-start.8 = (bf16[320,256]{1,0:T(8,128)(2,1)S(1)}, bf16[320,256]{1,0:T(8,128)(2,1)S(1)}, u32[]{:S(2)}, u32[]{:S(2)}) collective-permute-start(bf16[320,256]{1,0:T(8,128)(2,1)S(1)} %get-tuple-element.40), channel_id=1, source_target_pairs={{0,1},{1,0},{2,3},{3,2},{4,5},{5,4},{6,7},{7,6},{8,9},{9,8},{10,11... | collective-permute-start | bytes 491528 | tf_op jit(solution)/shard_map/ppermute | solution.py:153
  21.4 3.1 %collective-permute-start.9 = (bf16[320,256]{1,0:T(8,128)(2,1)S(1)}, bf16[320,256]{1,0:T(8,128)(2,1)S(1)}, u32[]{:S(2)}, u32[]{:S(2)}) collective-permute-start(bf16[320,256]{1,0:T(8,128)(2,1)S(1)} %get-tuple-element.42), channel_id=1, source_target_pairs={{0,1},{1,0},{2,3},{3,2},{4,5},{5,4},{6,7},{7,6},{8,9},{9,8},{10,11... | collective-permute-start | bytes 491528 | tf_op jit(solution)/shard_map/ppermute | solution.py:153
  21.6 11.0 %collective-permute-start.11 = (bf16[320,256]{1,0:T(8,128)(2,1)S(1)}, bf16[320,256]{1,0:T(8,128)(2,1)S(1)}, u32[]{:S(2)}, u32[]{:S(2)}) collective-permute-start(bf16[320,256]{1,0:T(8,128)(2,1)S(1)} %shard_map.124), channel_id=1, source_target_pairs={{0,2},{2,0},{1,3},{3,1},{4,6},{6,4},{5,7},{7,5},{8,10},{10,8},{9,1... | collective-permute-start | bytes 491528 | tf_op jit(solution)/shard_map/ppermute | solution.py:153
  22.3 11.3 %collective-permute-start.2 = (bf16[320,256]{1,0:T(8,128)(2,1)S(1)}, bf16[320,256]{1,0:T(8,128)(2,1)S(1)}, u32[]{:S(2)}, u32[]{:S(2)}) collective-permute-start(bf16[320,256]{1,0:T(8,128)(2,1)S(1)} %get-tuple-element.34), channel_id=1, source_target_pairs={{0,1},{1,0},{2,3},{3,2},{4,5},{5,4},{6,7},{7,6},{8,9},{9,8},{10,11... | collective-permute-start | bytes 491528 | tf_op jit(solution)/shard_map/ppermute | solution.py:153
  22.5 12.8 %collective-permute-start.4 = (bf16[320,256]{1,0:T(8,128)(2,1)S(1)}, bf16[320,256]{1,0:T(8,128)(2,1)S(1)}, u32[]{:S(2)}, u32[]{:S(2)}) collective-permute-start(bf16[320,256]{1,0:T(8,128)(2,1)S(1)} %shard_map.120), channel_id=1, source_target_pairs={{0,2},{2,0},{1,3},{3,1},{4,6},{6,4},{5,7},{7,5},{8,10},{10,8},{9,1... | collective-permute-start | bytes 491528 | tf_op jit(solution)/shard_map/ppermute | solution.py:153

commit v5 on v4

--- a/solution.py
+++ b/solution.py
@@ -9,8 +9,8 @@
 
 DH = 128
 EPS = 1e-05
-SPANS = ((0, 2), (2, 3), (3, 4))
-OWN_SPANS = ((0, 1), (1, 2), (2, 3), (3, 4))
+SPANS = ((0, 4), (4, 6), (6, 8))
+OWN_SPANS = ((0, 2), (2, 4), (4, 6), (6, 8))
 f32 = jnp.float32
 bf16 = jnp.bfloat16
 HIGHEST = lax.Precision.HIGHEST
@@ -47,7 +47,7 @@
 
 
 def base_kernel(
-    offsets_ref, lengths_ref, q_ref, k_ref, v_ref, oq_ref, ok_ref, ov_ref, after_ref, out_ref, queries_ref, valid_ref
+    offsets_ref, lengths_ref, q_ref, k_ref, v_ref, oq_ref, ok_ref, ov_ref, after_ref, use_ref, out_ref, queries_ref, valid_ref
 ):
     tokens, (opts, slots, _) = q_ref.shape[0], oq_ref.shape
     rows, most = tokens + opts * slots, opts * slots
@@ -78,28 +78,43 @@
 
 def add_kernel(*refs):
     out_ref = refs[-1]
-    total = refs[0][:out_ref.shape[0]].astype(f32)
+    total = refs[0][...].astype(f32)
     for ref in refs[1:-1]:
-        total = total + ref[:out_ref.shape[0]].astype(f32)
+        total = total + ref[...].astype(f32)
     out_ref[...] = total.astype(out_ref.dtype)
 
 
-def add(*terms, rows=None):
-    shape = (rows or terms[0].shape[0],) + terms[0].shape[1:]
-    return call(
-        add_kernel, Shape(shape, bf16), [VMEM] * len(terms), len(terms) * terms[0].size, 6 * len(terms) * terms[0].size,
+def add(*terms):
+    return call(
+        add_kernel, Shape(terms[0].shape, bf16), [VMEM] * len(terms),
+        len(terms) * terms[0].size, 6 * len(terms) * terms[0].size,
     )(*terms)
 
 
+def halves_kernel(a_ref, b_ref, first_ref, second_ref):
+    total = a_ref[...].astype(f32) + b_ref[...].astype(f32)
+    cut = first_ref.shape[0]
+    first_ref[...] = total[:cut].astype(first_ref.dtype)
+    second_ref[...] = total[cut:].astype(second_ref.dtype)
+
+
+def add_halves(a, b, cut):
+    count, *rest = a.shape
+    return call(
+        halves_kernel, [Shape((n, *rest), bf16) for n in (cut, count - cut)], [VMEM] * 2, 2 * a.size, 8 * a.size
+    )(a, b)
+
+
 def normed_kernel(spans, use_ref, valid_ref, gain_ref, queries_ref, base_ref, *rest):
-    parts, out_ref = rest[:-1], rest[-1]
+    parts, out_ref, prefix_ref = rest[:-2], rest[-2], rest[-1]
+    for n, ((low, high), part) in enumerate(zip(spans, parts)):
+        part = jnp.where(use_ref[n:n + 1] > 0.0, part[...].astype(f32), 0.0)
+        if n:
+            part = part + prefix_ref[low:high]
+        prefix_ref[low:high] = part
     for h in range(out_ref.shape[1] // DH):
-        prefix = jnp.zeros((DH, DH), f32)
-        for n, (low, high) in enumerate(spans):
-            if low <= h < high:
-                prefix = prefix + jnp.where(use_ref[n:n + 1] > 0.0, parts[n][h - low].astype(f32), 0.0)
         cols = columns(h)
-        out = base_ref[:, cols] + dot(queries_ref[:, cols], prefix.astype(bf16), ((1,), (0,)))
+        out = base_ref[:, cols] + dot(queries_ref[:, cols], prefix_ref[cols].astype(bf16), ((1,), (0,)))
         scale = lax.rsqrt(jnp.mean(out * out, axis=1, keepdims=True) + EPS)
         out_ref[:, cols] = (out * (scale * valid_ref[...]) * gain_ref[:, cols]).astype(out_ref.dtype)
 
@@ -162,16 +177,24 @@
 
 
 def exclusive(state, axis, size):
-    place = lax.axis_index(axis)
-    parts, use, windows, step = [], [], [state], 1
+    count, place = state.shape[0], lax.axis_index(axis)
+    parts, sent, step = [], state, 1
     while step < size:
-        send = upward if 2 * step == size else swap
-        parts.append(send(windows[-1], axis, size, step))
-        use.append(place & step != 0)
+        used = place & step != 0
+        if step > 1 and 2 * step == size:
+            cut = count * 15 // 32 // 16 * 16
+            pieces = add_halves(window[0], window[1], cut)
+            parts += [
+                (swap(pieces[0], axis, size, step), (0, cut), used), (upward(pieces[1], axis, size, step), (cut, count), used)
+            ]
+            sent = pieces[0] if step == 2 else sent
+        else:
+            total = state if step == 1 else add(*window)
+            sent = total if step == 2 else sent
+            parts.append((swap(total, axis, size, step), (0, count), used))
+            window = (total, parts[-1][0])
         step *= 2
-        if step < size:
-            windows.append(add(windows[-1], parts[-1]))
-    return parts, use, windows[:2][-1]
+    return parts, sent
 
 
 def on_device(sizes, q, k, v, oq, ok, ov, offsets, lengths, gain, weight):
@@ -187,20 +210,20 @@
         lax.axis_index("seq") < n_seq - 1,
         lambda: jnp.einsum(
             "thd,the->hde", k.reshape(tokens, heads, DH), v.reshape(tokens, heads, DH), precision=lax.Precision.DEFAULT
-        ).astype(bf16),
-        lambda: jnp.zeros((heads, DH, DH), bf16),
-    )
-    parts, use, window = exclusive(state, "seq", n_seq)
-    parts = [(part, (0, heads), used) for part, used in zip(parts, use)]
-
+        ).astype(bf16).reshape(feats, DH),
+        lambda: jnp.zeros((feats, DH), bf16),
+    )
+    parts, window = exclusive(state, "seq", n_seq)
+
+    use = jnp.broadcast_to(jnp.stack([p[2] for p in parts]).astype(f32)[:, None], (len(parts), DH))
     base, queries, valid = call(
-        base_kernel, [Shape((rows, feats), f32), Shape((rows, feats), bf16), Shape((rows, DH), f32)], [VMEM] * 8 + [ANY],
+        base_kernel, [Shape((rows, feats), f32), Shape((rows, feats), bf16), Shape((rows, DH), f32)], [VMEM] * 8 + [ANY] * 2,
         4 * rows * rows * feats, 16 * rows * feats,
-    )(offsets[None], lengths[None], q, k, v, oq, ok, ov, window)
-    use = jnp.broadcast_to(jnp.stack([p[2] for p in parts]).astype(f32)[:, None], (len(parts), DH))
+    )(offsets[None], lengths[None], q, k, v, oq, ok, ov, window, use)
     normed = call(
         functools.partial(normed_kernel, [p[1] for p in parts]), Shape((rows, feats), bf16),
         [VMEM] * (5 + len(parts)), 2 * rows * DH * feats, 10 * rows * feats,
+        scratch_shapes=[pltpu.VMEM((feats, DH), f32)],
     )(use, valid, gain[None], queries, base, *[p[0] for p in parts])
 
     def blocks(d):
@@ -217,21 +240,19 @@
 
     later, _ = lax.optimization_barrier((weight, state))
     weights = [blocks(d) for d in range(n_head)]
-    spans, own_spans = ([(width * a // 4, width * b // 4) for a, b in some] for some in (SPANS, OWN_SPANS))
-    received = []
+    spans, own_spans = ([(width * a // 8, width * b // 8) for a, b in some] for some in (SPANS, OWN_SPANS))
+    parts = []
     for d in range(1, n_head):
-        for (low, high), terms in zip(spans, summed(d, spans, 1)):
-            received.append((low, high, ring(add(*terms), "head", n_head, d)))
-    own = summed(0, own_spans)
-    shapes = (Shape((tokens, width), bf16), Shape((opts, slots, width), bf16))
-    out, last = (), spans[-1][0]
-    for some in ([span for span in own_spans if span[1] <= last], [span for span in own_spans if span[0] >= last]):
+        for span, terms in zip(spans, summed(d, spans, 1)):
+            parts.append((*span, ring(add(*terms), "head", n_head, d)))
+    for span, terms in zip(own_spans, summed(0, own_spans)):
+        parts += [(*span, x) for x in terms]
+    cuts = sorted({low for low, _, _ in parts} | {width})
+    steps, last = list(zip(cuts, cuts[1:])), spans[-1][0]
+    shapes, out = (Shape((tokens, width), bf16), Shape((opts, slots, width), bf16)), ()
+    for some in ([step for step in steps if step[1] <= last], [step for step in steps if step[0] >= last]):
         if some:
-            terms = [
-                [(x, 0) for x in own[own_spans.index(span)]]
-                + [(x, span[0] - low) for low, high, x in received if low <= span[0] and span[1] <= high]
-                for span in some
-            ]
+            terms = [[(x, at - low) for low, high, x in parts if low <= at and end <= high] for at, end in some]
             out = final(some, terms, shapes, out)
     return tuple(out)
 

time: 36.5 us -> 35.8 us (0.981)
  waiting for transfers between devices: 12.1 us -> 11.3 us
    ppermute x1 -> x2, starting transfers between devices: 3.09 us -> 5.91 us  [swap(): return lax.ppermute(value, axis, [(i, i ^ mask) for i in range(size)])]
    ppermute x1, starting transfers between devices: 4.66 us -> 2.07 us  [upward(): lax.ppermute(value, axis, [(i, i ^ mask) for i in range(size) if not i &...]
    ppermute x1, waiting for transfers between devices: 1.33 us -> 0.66 us  [upward(): lax.ppermute(value, axis, [(i, i ^ mask) for i in range(size) if not i &...]
  transfers between devices with their start and end apart: 12 -> 13, of which waited for: 5 -> 5; matrix products, arithmetic and copies ran while one was open for 8% -> 8% of each run, Pallas kernels for 11% -> 11%
where the time goes in v5:
time: 35.8 us; the launch traced here: 35.6 us
  starting transfers between devices  13.4 us (37%)
  waiting for transfers between devices  11.3 us (32%)
  Pallas kernels  5.61 us (16%)
  local copies, waits for them, and re-layouts  2.88 us (8%)
  matrix products  1.39 us (4%)
  between operations  0.89 us (2%)
    ppermute x10, waiting for transfers between devices, ring(): lax.ppermute(value, axis, [(i, (i + shift) % size) for i in range(size)])  9.98 us
    ppermute x2, starting transfers between devices, swap(): return lax.ppermute(value, axis, [(i, i ^ mask) for i in range(size)])  5.91 us
    ppermute x10, starting transfers between devices, ring(): lax.ppermute(value, axis, [(i, (i + shift) % size) for i in range(size)])  5.46 us
    dynamic_slice x1, local copies, waits for them, and re-layouts, blocks(): return [lax.dynamic_slice_in_dim(later, x, width, 1) for x in at]  2.76 us
    pallas_call x6, Pallas kernels, project(): call(functools.partial(project_kernel, spans), [Shape((count, b - a), dty...  2.32 us
    ppermute x1, starting transfers between devices, upward(): lax.ppermute(value, axis, [(i, i ^ mask) for i in range(size) if not i &...  2.07 us
    pallas_call x2, Pallas kernels, final(): call(functools.partial(final_kernel, spans, [len(some) for some in terms]...  1.68 us
    dot_general x1, matrix products, on_device(): jnp.einsum('thd,the->hde', k.reshape(tokens, heads, DH), v.reshape(tokens...  1.39 us
  transfers between devices with their start and end apart: 13, of which 5 were waited for; matrix products, arithmetic and copies ran while one was open for 8% of the time, Pallas kernels for 11%

profile of v5, /device:TPU:0, one launch (start us, length us, event | category | flops | bytes accessed | tf_op | source)
XLA Modules:
  0.0 35.6 jit_solution(2434851765104221080)
XLA Ops:
  0.6 1.4 %conditional.1 = (bf16[512,128]{1,0:T(8,128)(2,1)S(1)}) conditional(s32[]{:T(128)} %convert_element_type.14, () %tuple.14, (f32[192,512]{1,0:T(8,128)}, f32[192,512]{1,0:T(8,128)}) %tuple.15), branch_computations={%region_0.0_spmd, %region_1.0_spmd} | conditional | flops 25165824 | bytes 917512 | solution.py:209
  0.7 1.4 %convolution_convert_fusion = bf16[4,128,128]{2,1,0:T(8,128)(2,1)S(1)} fusion(f32[192,512]{1,0:T(8,128)} %get-tuple-element.8, f32[192,512]{1,0:T(8,128)} %get-tuple-element.4), kind=kOutput, calls=%fused_computation | convolution fusion | flops 25165824 | bytes 917504 | tf_op jit(solution)/shard_map/cond/branch_1_fun/thd,the->hde/dot_general | solution.py:211
  2.0 3.1 %collective-permute-start = (bf16[512,128]{1,0:T(8,128)(2,1)S(1)}, bf16[512,128]{1,0:T(8,128)(2,1)S(1)}, u32[]{:S(2)}, u32[]{:S(2)}) collective-permute-start(bf16[512,128]{1,0:T(8,128)(2,1)S(1)} %get-tuple-element.55.a_ref), channel_id=1, source_target_pairs={{0,4},{4,0},{8,12},{12,8},{1,5},{5,1},{9,13},{13,9},{2,6},{6,2},{1... | collective-permute-start | bytes 393224 | tf_op jit(solution)/shard_map/ppermute | solution.py:172
  5.1 0.0 copy-start
  5.1 0.0 copy-start.1
  5.1 0.0 copy-start.2
  5.1 0.0 copy-start.3
  5.1 0.0 copy-start.5
  5.2 0.0 copy-start.6
  5.2 0.0 copy-start.7
  5.2 0.0 copy-start.8
  5.2 0.0 copy-start.4
  5.2 2.8 %constant_dynamic-slice_fusion = (bf16[512,1024]{1,0:T(8,128)(2,1)S(1)}, bf16[512,1024]{1,0:T(8,128)(2,1)S(1)}, bf16[512,1024]{1,0:T(8,128)(2,1)S(1)}, bf16[512,1024]{1,0:T(8,128)(2,1)S(1)}) fusion(bf16[512,4096]{1,0:T(8,128)(2,1)} %param.21, s32[]{:T(128)S(6)} %select_n.46, s32[]{:T(128)S(6)} %select_n.45, s32[]{:T(128)S(6)} %select_n.43, s32[]{:T(128)S(6)} %select_n.41), kind=kLoop, calls=%fused_computation.6 | loop fusion | bytes 8388624 | tf_op jit(solution)/shard_map/dynamic_slice | solution.py:231
  8.0 0.7 %collective-permute-done.b_ref.rest_0_ = bf16[512,128]{1,0:T(8,128)(2,1)S(1)} collective-permute-done((bf16[512,128]{1,0:T(8,128)(2,1)S(1)}, bf16[512,128]{1,0:T(8,128)(2,1)S(1)}, u32[]{:S(2)}, u32[]{:S(2)}) %collective-permute-start) | collective-permute-done | bytes 131104 | tf_op jit(solution)/shard_map/ppermute | solution.py:172
  8.7 2.8 %collective-permute-start.1 = (bf16[240,128]{1,0:T(8,128)(2,1)S(1)}, bf16[240,128]{1,0:T(8,128)(2,1)S(1)}, u32[]{:S(2)}, u32[]{:S(2)}) collective-permute-start(bf16[240,128]{1,0:T(8,128)(2,1)S(1)} %get-tuple-element.31.after_ref), channel_id=1, source_target_pairs={{0,8},{4,12},{8,0},{12,4},{1,9},{5,13},{9,1},{13,5},{2,10},{6,14},... | collective-permute-start | bytes 184328 | tf_op jit(solution)/shard_map/ppermute | solution.py:172
  11.5 2.1 %collective-permute-start.2 = (bf16[272,128]{1,0:T(8,128)(2,1)S(1)}, bf16[272,128]{1,0:T(8,128)(2,1)S(1)}, u32[]{:S(2)}, u32[]{:S(2)}) collective-permute-start(bf16[272,128]{1,0:T(8,128)(2,1)S(1)} %get-tuple-element.35), channel_id=1, source_target_pairs={{0,8},{4,12},{1,9},{5,13},{2,10},{6,14},{3,11},{7,15},{16,24},{20,... | collective-permute-start | bytes 208904 | tf_op jit(solution)/shard_map/ppermute | solution.py:176
  13.6 0.1 add_convert_fusion
  13.6 0.1 broadcast_in_dim.15.use_ref
  13.7 0.0 copy-done
  13.7 0.0 copy-done.1
  13.7 0.0 copy-done.2
  13.7 0.0 copy-done.3
  13.7 0.0 copy-done.5
  13.7 0.0 copy-done.6
  13.8 0.0 copy-done.7
  13.8 0.0 copy-done.8
  13.8 1.0 %shard_map.114 = (f32[320,512]{1,0:T(8,128)S(1)}, bf16[320,512]{1,0:T(8,128)(2,1)S(1)}, f32[320,128]{1,0:T(8,128)S(1)}) custom-call(s32[1,2]{1,0:T(1,128)S(1)} %bitcast.21, s32[1,2]{1,0:T(1,128)S(1)} %bitcast.22, f32[192,512]{1,0:T(8,128)S(1)} %copy-done, f32[192,512]{1,0:T(8,128)S(1)} %copy-done.7, f32[192,512]{1,0:T(8,128)S(1)} %copy-done.8, ...), custom_call_target="tpu_custom_call" | custom-call | flops 209715200 | bytes 2621440 | tf_op jit(solution)/shard_map/pallas_call | solution.py:219
  14.8 0.0 collective-permute-done.1.rest_1_
  14.8 0.7 %collective-permute-done.2.rest_2_ = bf16[272,128]{1,0:T(8,128)(2,1)S(1)} collective-permute-done((bf16[272,128]{1,0:T(8,128)(2,1)S(1)}, bf16[272,128]{1,0:T(8,128)(2,1)S(1)}, u32[]{:S(2)}, u32[]{:S(2)}) %collective-permute-start.2) | collective-permute-done | bytes 69664 | tf_op jit(solution)/shard_map/ppermute | solution.py:176
  15.5 0.0 copy-done.4
  15.5 0.4 %shard_map.115.rows_ref = bf16[320,512]{1,0:T(8,128)(2,1)S(1)} custom-call(f32[3,128]{1,0:T(4,128)S(1)} %broadcast_in_dim.15.use_ref, f32[320,128]{1,0:T(8,128)S(1)} %get-tuple-element.32.valid_ref, f32[1,512]{1,0:T(1,128)S(1)} %bitcast.20, bf16[320,512]{1,0:T(8,128)(2,1)S(1)} %get-tuple-element.33.queries_ref, f32[320,512]{1,0:T(8,128)S(1)} %get-tuple-element.34.base_ref, ...), custom_call_target="tpu_custom_call" | custom-call | flops 41943040 | bytes 1638400 | tf_op jit(solution)/shard_map/pallas_call | solution.py:223
  15.9 0.3 shard_map.122
  16.3 0.1 collective-permute-start.6
  16.3 0.3 shard_map.117
  16.7 0.6 %collective-permute-start.3 = (bf16[320,256]{1,0:T(8,128)(2,1)S(1)}, bf16[320,256]{1,0:T(8,128)(2,1)S(1)}, u32[]{:S(2)}, u32[]{:S(2)}) collective-permute-start(bf16[320,256]{1,0:T(8,128)(2,1)S(1)} %get-tuple-element.38), channel_id=1, source_target_pairs={{0,1},{1,0},{2,3},{3,2},{4,5},{5,4},{6,7},{7,6},{8,9},{9,8},{10,11... | collective-permute-start | bytes 491528 | tf_op jit(solution)/shard_map/ppermute | solution.py:168
  17.2 0.1 collective-permute-start.10
  17.3 0.3 shard_map.121.refs_0_
  17.7 0.3 collective-permute-done.6.refs_1_
  18.0 0.1 shard_map.123
  18.0 1.7 %collective-permute-start.7 = (bf16[320,512]{1,0:T(8,128)(2,1)S(1)}, bf16[320,512]{1,0:T(8,128)(2,1)S(1)}, u32[]{:S(2)}, u32[]{:S(2)}) collective-permute-start(bf16[320,512]{1,0:T(8,128)(2,1)S(1)} %shard_map.123), channel_id=1, source_target_pairs={{0,2},{2,0},{1,3},{3,1},{4,6},{6,4},{5,7},{7,5},{8,10},{10,8},{9,1... | collective-permute-start | bytes 983048 | tf_op jit(solution)/shard_map/ppermute | solution.py:168
  19.7 0.5 %shard_map.120 = (bf16[320,256]{1,0:T(8,128)(2,1)S(1)}, bf16[320,256]{1,0:T(8,128)(2,1)S(1)}, bf16[320,256]{1,0:T(8,128)(2,1)S(1)}, bf16[320,256]{1,0:T(8,128)(2,1)S(1)}) custom-call(bf16[320,512]{1,0:T(8,128)(2,1)S(1)} %shard_map.115.rows_ref, bf16[512,1024]{1,0:T(8,128)(2,1)S(1)} %get-tuple-element.51.weight_ref), custom_call_target="tpu_custom_call" | custom-call | flops 335544320 | bytes 2686976 | tf_op jit(solution)/shard_map/pallas_call | solution.py:129
  20.2 0.1 collective-permute-start.8
  20.3 0.5 %collective-permute-start.9 = (bf16[320,256]{1,0:T(8,128)(2,1)S(1)}, bf16[320,256]{1,0:T(8,128)(2,1)S(1)}, u32[]{:S(2)}, u32[]{:S(2)}) collective-permute-start(bf16[320,256]{1,0:T(8,128)(2,1)S(1)} %get-tuple-element.44), channel_id=1, source_target_pairs={{0,1},{1,0},{2,3},{3,2},{4,5},{5,4},{6,7},{7,6},{8,9},{9,8},{10,11... | collective-permute-start | bytes 491528 | tf_op jit(solution)/shard_map/ppermute | solution.py:168
  20.8 0.3 shard_map.116
  21.2 0.0 collective-permute-done.10.refs_1_
  21.2 0.1 collective-permute-start.12
  21.3 0.0 collective-permute-done.3.refs_1_
  21.4 0.4 %collective-permute-start.11 = (bf16[320,256]{1,0:T(8,128)(2,1)S(1)}, bf16[320,256]{1,0:T(8,128)(2,1)S(1)}, u32[]{:S(2)}, u32[]{:S(2)}) collective-permute-start(bf16[320,256]{1,0:T(8,128)(2,1)S(1)} %shard_map.124), channel_id=1, source_target_pairs={{0,2},{2,0},{1,3},{3,1},{4,6},{6,4},{5,7},{7,5},{8,10},{10,8},{9,1... | collective-permute-start | bytes 491528 | tf_op jit(solution)/shard_map/ppermute | solution.py:168
  21.8 0.0 collective-permute-done.8.rest_2_
  21.8 0.2 collective-permute-start.5
  22.1 0.0 collective-permute-done.9.rest_5_
  22.1 1.7 %collective-permute-start.4 = (bf16[320,256]{1,0:T(8,128)(2,1)S(1)}, bf16[320,256]{1,0:T(8,128)(2,1)S(1)}, u32[]{:S(2)}, u32[]{:S(2)}) collective-permute-start(bf16[320,256]{1,0:T(8,128)(2,1)S(1)} %shard_map.118), channel_id=1, source_target_pairs={{0,2},{2,0},{1,3},{3,1},{4,6},{6,4},{5,7},{7,5},{8,10},{10,8},{9,1... | collective-permute-start | bytes 491528 | tf_op jit(solution)/shard_map/ppermute | solution.py:168
  23.7 0.5 %shard_map.119 = (f32[320,256]{1,0:T(8,128)S(1)}, f32[320,256]{1,0:T(8,128)S(1)}, f32[320,256]{1,0:T(8,128)S(1)}, f32[320,256]{1,0:T(8,128)S(1)}) custom-call(bf16[320,512]{1,0:T(8,128)(2,1)S(1)} %shard_map.115.rows_ref, bf16[512,1024]{1,0:T(8,128)(2,1)S(1)} %get-tuple-element.52.weight_ref), custom_call_target="tpu_custom_call" | custom-call | flops 335544320 | bytes 2686976 | tf_op jit(solution)/shard_map/pallas_call | solution.py:129
  24.2 0.0 collective-permute-done.12.rest_8_
  24.2 7.9 %collective-permute-done.11.rest_6_ = bf16[320,256]{1,0:T(8,128)(2,1)S(1)} collective-permute-done((bf16[320,256]{1,0:T(8,128)(2,1)S(1)}, bf16[320,256]{1,0:T(8,128)(2,1)S(1)}, u32[]{:S(2)}, u32[]{:S(2)}) %collective-permute-start.11) | collective-permute-done | bytes 163872 | tf_op jit(solution)/shard_map/ppermute | solution.py:168
  32.2 0.0 collective-permute-done.7.rest_0_.rest_3_
  32.2 0.9 %shard_map.125 = (bf16[192,1024]{1,0:T(8,128)(2,1)}, bf16[2,64,1024]{2,1,0:T(8,128)(2,1)}) custom-call(bf16[320,512]{1,0:T(8,128)(2,1)S(1)} %collective-permute-done.7.rest_0_.rest_3_, f32[320,256]{1,0:T(8,128)S(1)} %get-tuple-element.41.rest_1_, bf16[320,256]{1,0:T(8,128)(2,1)S(1)} %collective-permute-done.8.rest_2_, ...), custom_call_target="tpu_custom_call" | custom-call | flops 2211840 | bytes 8847360 | tf_op jit(solution)/shard_map/pallas_call | solution.py:158
  33.1 0.0 collective-permute-done.5.rest_2_
  33.1 1.8 %collective-permute-done.4.rest_0_ = bf16[320,256]{1,0:T(8,128)(2,1)S(1)} collective-permute-done((bf16[320,256]{1,0:T(8,128)(2,1)S(1)}, bf16[320,256]{1,0:T(8,128)(2,1)S(1)}, u32[]{:S(2)}, u32[]{:S(2)}) %collective-permute-start.4) | collective-permute-done | bytes 163872 | tf_op jit(solution)/shard_map/ppermute | solution.py:168
  34.9 0.7 %shard_map.126 = (bf16[192,1024]{1,0:T(8,128)(2,1)}, bf16[2,64,1024]{2,1,0:T(8,128)(2,1)}) custom-call(bf16[320,256]{1,0:T(8,128)(2,1)S(1)} %collective-permute-done.4.rest_0_, f32[320,256]{1,0:T(8,128)S(1)} %get-tuple-element.39.rest_1_, bf16[320,256]{1,0:T(8,128)(2,1)S(1)} %collective-permute-done.5.rest_2_, ...), custom_call_target="tpu_custom_call", output_to_operand_aliasing={{0}: (3, {}), {1}: (4, {})} | custom-call | flops 245760 | bytes 983040 | tf_op jit(solution)/shard_map/pallas_call | solution.py:158
  (3 shorter events, 0.1 us)
Async XLA Ops:
  2.0 6.6 %collective-permute-start = (bf16[512,128]{1,0:T(8,128)(2,1)S(1)}, bf16[512,128]{1,0:T(8,128)(2,1)S(1)}, u32[]{:S(2)}, u32[]{:S(2)}) collective-permute-start(bf16[512,128]{1,0:T(8,128)(2,1)S(1)} %get-tuple-element.55.a_ref), channel_id=1, source_target_pairs={{0,4},{4,0},{8,12},{12,8},{1,5},{5,1},{9,13},{13,9},{2,6},{6,2},{1... | collective-permute-start | bytes 393224 | tf_op jit(solution)/shard_map/ppermute | solution.py:172
  5.1 8.6 %copy-start = (f32[192,512]{1,0:T(8,128)S(1)}, f32[192,512]{1,0:T(8,128)}, u32[]{:S(2)}) copy-start(f32[192,512]{1,0:T(8,128)} %q_ref.1) | copy-start | bytes 1179652
  5.1 8.6 %copy-start.1 = (f32[2,64,512]{2,1,0:T(8,128)S(1)}, f32[2,64,512]{2,1,0:T(8,128)}, u32[]{:S(2)}) copy-start(f32[2,64,512]{2,1,0:T(8,128)} %oq_ref.1) | copy-start | bytes 786436
  5.1 8.6 %copy-start.2 = (f32[2,64,512]{2,1,0:T(8,128)S(1)}, f32[2,64,512]{2,1,0:T(8,128)}, u32[]{:S(2)}) copy-start(f32[2,64,512]{2,1,0:T(8,128)} %ok_ref.1) | copy-start | bytes 786436
  5.1 8.6 %copy-start.3 = (f32[2,64,512]{2,1,0:T(8,128)S(1)}, f32[2,64,512]{2,1,0:T(8,128)}, u32[]{:S(2)}) copy-start(f32[2,64,512]{2,1,0:T(8,128)} %ov_ref.1) | copy-start | bytes 786436
  5.1 8.6 %copy-start.5 = (s32[2]{0:T(128)S(1)}, s32[2]{0:T(128)}, u32[]{:S(2)}) copy-start(s32[2]{0:T(128)} %param.18) | copy-start | bytes 28
  5.2 8.6 %copy-start.6 = (s32[2]{0:T(128)S(1)}, s32[2]{0:T(128)}, u32[]{:S(2)}) copy-start(s32[2]{0:T(128)} %param.19) | copy-start | bytes 28
  5.2 8.6 %copy-start.7 = (f32[192,512]{1,0:T(8,128)S(1)}, f32[192,512]{1,0:T(8,128)}, u32[]{:S(2)}) copy-start(f32[192,512]{1,0:T(8,128)} %k_ref.1) | copy-start | bytes 1179652
  5.2 8.6 %copy-start.8 = (f32[192,512]{1,0:T(8,128)S(1)}, f32[192,512]{1,0:T(8,128)}, u32[]{:S(2)}) copy-start(f32[192,512]{1,0:T(8,128)} %v_ref.1) | copy-start | bytes 1179652
  5.2 10.3 %copy-start.4 = (f32[512]{0:T(512)S(1)}, f32[512]{0:T(512)}, u32[]{:S(2)}) copy-start(f32[512]{0:T(512)} %param.20) | copy-start | bytes 6148
  8.7 6.1 %collective-permute-start.1 = (bf16[240,128]{1,0:T(8,128)(2,1)S(1)}, bf16[240,128]{1,0:T(8,128)(2,1)S(1)}, u32[]{:S(2)}, u32[]{:S(2)}) collective-permute-start(bf16[240,128]{1,0:T(8,128)(2,1)S(1)} %get-tuple-element.31.after_ref), channel_id=1, source_target_pairs={{0,8},{4,12},{8,0},{12,4},{1,9},{5,13},{9,1},{13,5},{2,10},{6,14},... | collective-permute-start | bytes 184328 | tf_op jit(solution)/shard_map/ppermute | solution.py:172
  11.5 4.0 %collective-permute-start.2 = (bf16[272,128]{1,0:T(8,128)(2,1)S(1)}, bf16[272,128]{1,0:T(8,128)(2,1)S(1)}, u32[]{:S(2)}, u32[]{:S(2)}) collective-permute-start(bf16[272,128]{1,0:T(8,128)(2,1)S(1)} %get-tuple-element.35), channel_id=1, source_target_pairs={{0,8},{4,12},{1,9},{5,13},{2,10},{6,14},{3,11},{7,15},{16,24},{20,... | collective-permute-start | bytes 208904 | tf_op jit(solution)/shard_map/ppermute | solution.py:176
  16.3 1.7 %collective-permute-start.6 = (bf16[320,512]{1,0:T(8,128)(2,1)S(1)}, bf16[320,512]{1,0:T(8,128)(2,1)S(1)}, u32[]{:S(2)}, u32[]{:S(2)}) collective-permute-start(bf16[320,512]{1,0:T(8,128)(2,1)S(1)} %shard_map.122), channel_id=1, source_target_pairs={{0,1},{1,0},{2,3},{3,2},{4,5},{5,4},{6,7},{7,6},{8,9},{9,8},{10,11... | collective-permute-start | bytes 983048 | tf_op jit(solution)/shard_map/ppermute | solution.py:168
  16.7 4.7 %collective-permute-start.3 = (bf16[320,256]{1,0:T(8,128)(2,1)S(1)}, bf16[320,256]{1,0:T(8,128)(2,1)S(1)}, u32[]{:S(2)}, u32[]{:S(2)}) collective-permute-start(bf16[320,256]{1,0:T(8,128)(2,1)S(1)} %get-tuple-element.38), channel_id=1, source_target_pairs={{0,1},{1,0},{2,3},{3,2},{4,5},{5,4},{6,7},{7,6},{8,9},{9,8},{10,11... | collective-permute-start | bytes 491528 | tf_op jit(solution)/shard_map/ppermute | solution.py:168
  17.2 3.9 %collective-permute-start.10 = (bf16[320,256]{1,0:T(8,128)(2,1)S(1)}, bf16[320,256]{1,0:T(8,128)(2,1)S(1)}, u32[]{:S(2)}, u32[]{:S(2)}) collective-permute-start(bf16[320,256]{1,0:T(8,128)(2,1)S(1)} %get-tuple-element.46), channel_id=1, source_target_pairs={{0,1},{1,0},{2,3},{3,2},{4,5},{5,4},{6,7},{7,6},{8,9},{9,8},{10,11... | collective-permute-start | bytes 491528 | tf_op jit(solution)/shard_map/ppermute | solution.py:168
  18.0 14.1 %collective-permute-start.7 = (bf16[320,512]{1,0:T(8,128)(2,1)S(1)}, bf16[320,512]{1,0:T(8,128)(2,1)S(1)}, u32[]{:S(2)}, u32[]{:S(2)}) collective-permute-start(bf16[320,512]{1,0:T(8,128)(2,1)S(1)} %shard_map.123), channel_id=1, source_target_pairs={{0,2},{2,0},{1,3},{3,1},{4,6},{6,4},{5,7},{7,5},{8,10},{10,8},{9,1... | collective-permute-start | bytes 983048 | tf_op jit(solution)/shard_map/ppermute | solution.py:168
  20.2 1.6 %collective-permute-start.8 = (bf16[320,256]{1,0:T(8,128)(2,1)S(1)}, bf16[320,256]{1,0:T(8,128)(2,1)S(1)}, u32[]{:S(2)}, u32[]{:S(2)}) collective-permute-start(bf16[320,256]{1,0:T(8,128)(2,1)S(1)} %get-tuple-element.42), channel_id=1, source_target_pairs={{0,1},{1,0},{2,3},{3,2},{4,5},{5,4},{6,7},{7,6},{8,9},{9,8},{10,11... | collective-permute-start | bytes 491528 | tf_op jit(solution)/shard_map/ppermute | solution.py:168
  20.3 1.7 %collective-permute-start.9 = (bf16[320,256]{1,0:T(8,128)(2,1)S(1)}, bf16[320,256]{1,0:T(8,128)(2,1)S(1)}, u32[]{:S(2)}, u32[]{:S(2)}) collective-permute-start(bf16[320,256]{1,0:T(8,128)(2,1)S(1)} %get-tuple-element.44), channel_id=1, source_target_pairs={{0,1},{1,0},{2,3},{3,2},{4,5},{5,4},{6,7},{7,6},{8,9},{9,8},{10,11... | collective-permute-start | bytes 491528 | tf_op jit(solution)/shard_map/ppermute | solution.py:168
  21.2 3.1 %collective-permute-start.12 = (bf16[320,256]{1,0:T(8,128)(2,1)S(1)}, bf16[320,256]{1,0:T(8,128)(2,1)S(1)}, u32[]{:S(2)}, u32[]{:S(2)}) collective-permute-start(bf16[320,256]{1,0:T(8,128)(2,1)S(1)} %get-tuple-element.48), channel_id=1, source_target_pairs={{0,1},{1,0},{2,3},{3,2},{4,5},{5,4},{6,7},{7,6},{8,9},{9,8},{10,11... | collective-permute-start | bytes 491528 | tf_op jit(solution)/shard_map/ppermute | solution.py:168
  21.4 10.8 %collective-permute-start.11 = (bf16[320,256]{1,0:T(8,128)(2,1)S(1)}, bf16[320,256]{1,0:T(8,128)(2,1)S(1)}, u32[]{:S(2)}, u32[]{:S(2)}) collective-permute-start(bf16[320,256]{1,0:T(8,128)(2,1)S(1)} %shard_map.124), channel_id=1, source_target_pairs={{0,2},{2,0},{1,3},{3,1},{4,6},{6,4},{5,7},{7,5},{8,10},{10,8},{9,1... | collective-permute-start | bytes 491528 | tf_op jit(solution)/shard_map/ppermute | solution.py:168
  21.8 11.3 %collective-permute-start.5 = (bf16[320,256]{1,0:T(8,128)(2,1)S(1)}, bf16[320,256]{1,0:T(8,128)(2,1)S(1)}, u32[]{:S(2)}, u32[]{:S(2)}) collective-permute-start(bf16[320,256]{1,0:T(8,128)(2,1)S(1)} %get-tuple-element.40), channel_id=1, source_target_pairs={{0,1},{1,0},{2,3},{3,2},{4,5},{5,4},{6,7},{7,6},{8,9},{9,8},{10,11... | collective-permute-start | bytes 491528 | tf_op jit(solution)/shard_map/ppermute | solution.py:168
  22.1 12.8 %collective-permute-start.4 = (bf16[320,256]{1,0:T(8,128)(2,1)S(1)}, bf16[320,256]{1,0:T(8,128)(2,1)S(1)}, u32[]{:S(2)}, u32[]{:S(2)}) collective-permute-start(bf16[320,256]{1,0:T(8,128)(2,1)S(1)} %shard_map.118), channel_id=1, source_target_pairs={{0,2},{2,0},{1,3},{3,1},{4,6},{6,4},{5,7},{7,5},{8,10},{10,8},{9,1... | collective-permute-start | bytes 491528 | tf_op jit(solution)/shard_map/ppermute | solution.py:168

commit v6 on v5

--- a/solution.py
+++ b/solution.py
@@ -91,25 +91,24 @@
     )(*terms)
 
 
-def halves_kernel(a_ref, b_ref, first_ref, second_ref):
-    total = a_ref[...].astype(f32) + b_ref[...].astype(f32)
-    cut = first_ref.shape[0]
-    first_ref[...] = total[:cut].astype(first_ref.dtype)
-    second_ref[...] = total[cut:].astype(second_ref.dtype)
-
-
-def add_halves(a, b, cut):
-    count, *rest = a.shape
-    return call(
-        halves_kernel, [Shape((n, *rest), bf16) for n in (cut, count - cut)], [VMEM] * 2, 2 * a.size, 8 * a.size
-    )(a, b)
-
-
-def normed_kernel(spans, use_ref, valid_ref, gain_ref, queries_ref, base_ref, *rest):
-    parts, out_ref, prefix_ref = rest[:-2], rest[-2], rest[-1]
+def split_kernel(x_ref, *outs):
+    at = 0
+    for out in outs:
+        out[...] = x_ref[at:at + out.shape[0]]
+        at += out.shape[0]
+
+
+def split(x, spans):
+    shapes = [Shape((high - low, *x.shape[1:]), x.dtype) for low, high in spans]
+    return call(split_kernel, shapes, [VMEM], 0, 4 * x.size)(x)
+
+
+def normed_kernel(spans, width, after, use_ref, valid_ref, gain_ref, queries_ref, base_ref, *rest):
+    parts, prefix_ref, outs = rest[:len(spans)], rest[-1], rest[len(spans) + after:-1]
+    weights, out_ref, firsts = outs[:len(outs) // 2], outs[len(outs) // 2], outs[len(outs) // 2 + 1:]
     for n, ((low, high), part) in enumerate(zip(spans, parts)):
         part = jnp.where(use_ref[n:n + 1] > 0.0, part[...].astype(f32), 0.0)
-        if n:
+        if n > 1:
             part = part + prefix_ref[low:high]
         prefix_ref[low:high] = part
     for h in range(out_ref.shape[1] // DH):
@@ -117,6 +116,8 @@
         out = base_ref[:, cols] + dot(queries_ref[:, cols], prefix_ref[cols].astype(bf16), ((1,), (0,)))
         scale = lax.rsqrt(jnp.mean(out * out, axis=1, keepdims=True) + EPS)
         out_ref[:, cols] = (out * (scale * valid_ref[...]) * gain_ref[:, cols]).astype(out_ref.dtype)
+    for weight, first in zip(weights, firsts):
+        first[...] = jnp.dot(out_ref[...], weight[:, :width], preferred_element_type=f32).astype(first.dtype)
 
 
 def project_kernel(spans, rows_ref, weight_ref, *outs):
@@ -178,23 +179,17 @@
 
 def exclusive(state, axis, size):
     count, place = state.shape[0], lax.axis_index(axis)
-    parts, sent, step = [], state, 1
+    cut = count * 15 // 32 // 16 * 16
+    spans = [(0, cut), (cut, count)]
+    windows, parts, step = split(state, spans), [], 1
     while step < size:
-        used = place & step != 0
-        if step > 1 and 2 * step == size:
-            cut = count * 15 // 32 // 16 * 16
-            pieces = add_halves(window[0], window[1], cut)
-            parts += [
-                (swap(pieces[0], axis, size, step), (0, cut), used), (upward(pieces[1], axis, size, step), (cut, count), used)
-            ]
-            sent = pieces[0] if step == 2 else sent
-        else:
-            total = state if step == 1 else add(*window)
-            sent = total if step == 2 else sent
-            parts.append((swap(total, axis, size, step), (0, count), used))
-            window = (total, parts[-1][0])
+        sends = [swap, upward if step > 1 and 2 * step == size else swap]
+        got = [send(x, axis, size, step) for send, x in zip(sends, windows)]
+        parts += [(x, span, place & step != 0) for x, span in zip(got, spans)]
         step *= 2
-    return parts, sent
+        if step < size:
+            windows = [add(x, y) for x, y in zip(windows, got)]
+    return parts, windows[1]
 
 
 def on_device(sizes, q, k, v, oq, ok, ov, offsets, lengths, gain, weight):
@@ -220,30 +215,35 @@
         base_kernel, [Shape((rows, feats), f32), Shape((rows, feats), bf16), Shape((rows, DH), f32)], [VMEM] * 8 + [ANY] * 2,
         4 * rows * rows * feats, 16 * rows * feats,
     )(offsets[None], lengths[None], q, k, v, oq, ok, ov, window, use)
-    normed = call(
-        functools.partial(normed_kernel, [p[1] for p in parts]), Shape((rows, feats), bf16),
-        [VMEM] * (5 + len(parts)), 2 * rows * DH * feats, 10 * rows * feats,
-        scratch_shapes=[pltpu.VMEM((feats, DH), f32)],
-    )(use, valid, gain[None], queries, base, *[p[0] for p in parts])
-
-    def blocks(d):
+    def blocks(d, after):
+        later, _ = lax.optimization_barrier((weight, after))
         at = [((head + d) % n_head * n_sub + (sub + s) % n_sub) * width for s in range(n_sub)]
         return [lax.dynamic_slice_in_dim(later, x, width, 1) for x in at]
 
-    def summed(d, spans, first=0):
+    weights = [blocks(d, state if d else base) for d in range(n_head)]
+    spans, own_spans = ([(width * a // 8, width * b // 8) for a, b in some] for some in (SPANS, OWN_SPANS))
+    first, early = spans[0][1], weights[1][1:] if n_head > 1 else []
+    normed, *firsts = call(
+        functools.partial(normed_kernel, [p[1] for p in parts], first, n_sub),
+        [Shape((rows, feats), bf16)] + [Shape((rows, first), bf16)] * len(early),
+        [VMEM] * (5 + len(parts)) + [ANY] * n_sub + [VMEM] * len(early),
+        2 * rows * DH * feats, 10 * rows * feats, scratch_shapes=[pltpu.VMEM((feats, DH), f32)],
+    )(use, valid, gain[None], queries, base, *[p[0] for p in parts], *weights[0], *early)
+
+    def summed(d, spans, done=()):
         ours, *theirs = weights[d]
-        some = [spans for spans in (spans[:first], spans[first:]) if spans]
-        theirs = [sum([list(project(normed, w, spans, bf16)) for spans in some], []) for w in theirs]
+        some = [spans for spans in (spans[:1], spans[1:]) if spans] if d == 1 else [spans]
+        theirs = [
+            list(early) + sum([list(project(normed, w, spans, bf16)) for spans in some[len(early):]], [])
+            for w, early in zip(theirs, [[x] for x in done] or [[]] * len(theirs))
+        ]
         ours = sum([list(project(normed, ours, spans, f32)) for spans in some], [])
         theirs = [[ring(x, "sub", n_sub, s + 1) for x in xs] for s, xs in enumerate(theirs)]
         return list(zip(ours, *theirs))
 
-    later, _ = lax.optimization_barrier((weight, state))
-    weights = [blocks(d) for d in range(n_head)]
-    spans, own_spans = ([(width * a // 8, width * b // 8) for a, b in some] for some in (SPANS, OWN_SPANS))
     parts = []
     for d in range(1, n_head):
-        for span, terms in zip(spans, summed(d, spans, 1)):
+        for span, terms in zip(spans, summed(d, spans, firsts if d == 1 else ())):
             parts.append((*span, ring(add(*terms), "head", n_head, d)))
     for span, terms in zip(own_spans, summed(0, own_spans)):
         parts += [(*span, x) for x in terms]

time: 35.8 us -> 35.6 us (level)
  starting transfers between devices: 13.4 us -> 14.3 us
  local copies, waits for them, and re-layouts: 2.88 us -> 2.17 us
    dynamic_slice x1 -> x2, local copies, waits for them, and re-layouts: 2.76 us -> 2.05 us  [blocks(): return [lax.dynamic_slice_in_dim(later, x, width, 1) for x in at]]
    ppermute x2 -> x3, starting transfers between devices: 5.91 us -> 6.43 us  [swap(): return lax.ppermute(value, axis, [(i, i ^ mask) for i in range(size)])]
    ppermute x1, starting transfers between devices: 2.07 us -> 2.56 us  [upward(): lax.ppermute(value, axis, [(i, i ^ mask) for i in range(size) if not i &...]
    ppermute x2 -> x3, waiting for transfers between devices: 0.66 us -> 0.26 us  [swap(): return lax.ppermute(value, axis, [(i, i ^ mask) for i in range(size)])]
    pallas_call x6 -> x5, Pallas kernels: 2.32 us -> 1.98 us  [project(): call(functools.partial(project_kernel, spans), [Shape((count, b - a), dty...]
  transfers between devices with their start and end apart: 13 -> 14, of which waited for: 5 -> 5; matrix products, arithmetic and copies ran while one was open for 8% -> 6% of each run, Pallas kernels for 11% -> 12%
where the time goes in v6:
time: 35.6 us; the launch traced here: 35.4 us
  starting transfers between devices  14.3 us (40%)
  waiting for transfers between devices  11 us (31%)
  Pallas kernels  5.49 us (15%)
  local copies, waits for them, and re-layouts  2.17 us (6%)
  matrix products  1.47 us (4%)
  between operations  0.94 us (3%)
    ppermute x10, waiting for transfers between devices, ring(): lax.ppermute(value, axis, [(i, (i + shift) % size) for i in range(size)])  10.1 us
    ppermute x3, starting transfers between devices, swap(): return lax.ppermute(value, axis, [(i, i ^ mask) for i in range(size)])  6.43 us
    ppermute x10, starting transfers between devices, ring(): lax.ppermute(value, axis, [(i, (i + shift) % size) for i in range(size)])  5.29 us
    ppermute x1, starting transfers between devices, upward(): lax.ppermute(value, axis, [(i, i ^ mask) for i in range(size) if not i &...  2.56 us
    dynamic_slice x2, local copies, waits for them, and re-layouts, blocks(): return [lax.dynamic_slice_in_dim(later, x, width, 1) for x in at]  2.05 us
    pallas_call x5, Pallas kernels, project(): call(functools.partial(project_kernel, spans), [Shape((count, b - a), dty...  1.98 us
    pallas_call x2, Pallas kernels, final(): call(functools.partial(final_kernel, spans, [len(some) for some in terms]...  1.68 us
    dot_general x1, matrix products, on_device(): jnp.einsum('thd,the->hde', k.reshape(tokens, heads, DH), v.reshape(tokens...  1.47 us
  transfers between devices with their start and end apart: 14, of which 5 were waited for; matrix products, arithmetic and copies ran while one was open for 6% of the time, Pallas kernels for 12%

profile of v6, /device:TPU:0, one launch (start us, length us, event | category | flops | bytes accessed | tf_op | source)
XLA Modules:
  0.0 35.4 jit_solution(11006383058942194467)
XLA Ops:
  0.6 0.0 copy-start.6
  0.6 0.0 copy-start.5
  0.7 0.0 copy-start.3
  0.7 0.0 copy-start.2
  0.7 0.0 copy-start.1
  0.7 0.0 copy-start
  0.7 1.5 %conditional.1 = (bf16[512,128]{1,0:T(8,128)(2,1)S(1)}) conditional(s32[]{:T(128)} %convert_element_type.14, () %tuple.15, (f32[192,512]{1,0:T(8,128)}, f32[192,512]{1,0:T(8,128)}) %tuple.16), branch_computations={%region_0.0_spmd, %region_1.0_spmd} | conditional | flops 25165824 | bytes 917512 | solution.py:204
  0.7 1.5 %convolution_convert_fusion = bf16[4,128,128]{2,1,0:T(8,128)(2,1)S(1)} fusion(f32[192,512]{1,0:T(8,128)} %get-tuple-element.8, f32[192,512]{1,0:T(8,128)} %get-tuple-element.4), kind=kOutput, calls=%fused_computation | convolution fusion | flops 25165824 | bytes 917504 | tf_op jit(solution)/shard_map/cond/branch_1_fun/thd,the->hde/dot_general | solution.py:206
  2.2 0.0 copy-start.8
  2.2 0.0 copy-start.9
  2.2 3.1 %collective-permute-start.1 = (bf16[240,128]{1,0:T(8,128)(2,1)S(1)}, bf16[240,128]{1,0:T(8,128)(2,1)S(1)}, u32[]{:S(2)}, u32[]{:S(2)}) collective-permute-start(bf16[240,128]{1,0:T(8,128)(2,1)S(1)} %get-tuple-element.38.refs_0_), channel_id=1, source_target_pairs={{0,4},{4,0},{8,12},{12,8},{1,5},{5,1},{9,13},{13,9},{2,6},{6,2},{1... | collective-permute-start | bytes 184328 | tf_op jit(solution)/shard_map/ppermute | solution.py:173
  5.3 0.1 collective-permute-start
  5.4 0.0 copy-start.7
  5.4 1.9 %constant_dynamic-slice_fusion = (bf16[512,1024]{1,0:T(8,128)(2,1)S(1)}, bf16[512,1024]{1,0:T(8,128)(2,1)S(1)}) fusion(bf16[512,4096]{1,0:T(8,128)(2,1)} %param.21, s32[]{:T(128)S(6)} %select_n.46, s32[]{:T(128)S(6)} %select_n.45), kind=kLoop, calls=%fused_computation.6 | loop fusion | bytes 4194312 | tf_op jit(solution)/shard_map/dynamic_slice | solution.py:221
  7.3 0.0 copy-start.4
  7.3 0.1 add_convert_fusion
  7.4 0.3 collective-permute-done.1.refs_1_.rest_0_
  7.7 3.3 %collective-permute-start.2 = (bf16[240,128]{1,0:T(8,128)(2,1)S(1)}, bf16[240,128]{1,0:T(8,128)(2,1)S(1)}, u32[]{:S(2)}, u32[]{:S(2)}) collective-permute-start(bf16[240,128]{1,0:T(8,128)(2,1)S(1)} %shard_map.116), channel_id=1, source_target_pairs={{0,8},{4,12},{8,0},{12,4},{1,9},{5,13},{9,1},{13,5},{2,10},{6,14},... | collective-permute-start | bytes 184328 | tf_op jit(solution)/shard_map/ppermute | solution.py:173
  10.9 0.0 collective-permute-done.refs_1_.rest_1_
  10.9 2.6 %collective-permute-start.3 = (bf16[272,128]{1,0:T(8,128)(2,1)S(1)}, bf16[272,128]{1,0:T(8,128)(2,1)S(1)}, u32[]{:S(2)}, u32[]{:S(2)}) collective-permute-start(bf16[272,128]{1,0:T(8,128)(2,1)S(1)} %shard_map.114.after_ref), channel_id=1, source_target_pairs={{0,8},{4,12},{1,9},{5,13},{2,10},{6,14},{3,11},{7,15},{16,24},{20,... | collective-permute-start | bytes 208904 | tf_op jit(solution)/shard_map/ppermute | solution.py:177
  13.5 0.1 broadcast_in_dim.15.use_ref
  13.6 0.0 copy-done.6
  13.6 0.0 copy-done.5
  13.6 0.0 copy-done.3
  13.6 0.0 copy-done.2
  13.6 0.0 copy-done.1
  13.6 0.0 copy-done
  13.6 0.0 copy-done.8
  13.6 0.0 copy-done.9
  13.6 1.0 %shard_map.115 = (f32[320,512]{1,0:T(8,128)S(1)}, bf16[320,512]{1,0:T(8,128)(2,1)S(1)}, f32[320,128]{1,0:T(8,128)S(1)}) custom-call(s32[1,2]{1,0:T(1,128)S(1)} %bitcast.21, s32[1,2]{1,0:T(1,128)S(1)} %bitcast.22, f32[192,512]{1,0:T(8,128)S(1)} %copy-done, f32[192,512]{1,0:T(8,128)S(1)} %copy-done.8, f32[192,512]{1,0:T(8,128)S(1)} %copy-done.9, ...), custom_call_target="tpu_custom_call" | custom-call | flops 209715200 | bytes 2621440 | tf_op jit(solution)/shard_map/pallas_call | solution.py:214
  14.7 0.0 copy-done.7
  14.7 0.2 constant_dynamic-slice_fusion.2
  14.9 0.0 collective-permute-done.2.rest_2_
  14.9 0.5 %collective-permute-done.3.rest_3_ = bf16[272,128]{1,0:T(8,128)(2,1)S(1)} collective-permute-done((bf16[272,128]{1,0:T(8,128)(2,1)S(1)}, bf16[272,128]{1,0:T(8,128)(2,1)S(1)}, u32[]{:S(2)}, u32[]{:S(2)}) %collective-permute-start.3) | collective-permute-done | bytes 69664 | tf_op jit(solution)/shard_map/ppermute | solution.py:177
  15.4 0.0 copy-done.4
  15.4 0.6 %shard_map.117 = (bf16[320,512]{1,0:T(8,128)(2,1)S(1)}, bf16[320,512]{1,0:T(8,128)(2,1)S(1)}) custom-call(f32[4,128]{1,0:T(4,128)S(1)} %broadcast_in_dim.15.use_ref, f32[320,128]{1,0:T(8,128)S(1)} %get-tuple-element.35.valid_ref, f32[1,512]{1,0:T(1,128)S(1)} %bitcast.20, bf16[320,512]{1,0:T(8,128)(2,1)S(1)} %get-tuple-element.36.queries_ref, ...), custom_call_target="tpu_custom_call" | custom-call | flops 41943040 | bytes 1638400 | tf_op jit(solution)/shard_map/pallas_call | solution.py:226
  16.1 0.1 collective-permute-start.7
  16.2 0.3 shard_map.119
  16.5 0.6 %collective-permute-start.4 = (bf16[320,256]{1,0:T(8,128)(2,1)S(1)}, bf16[320,256]{1,0:T(8,128)(2,1)S(1)}, u32[]{:S(2)}, u32[]{:S(2)}) collective-permute-start(bf16[320,256]{1,0:T(8,128)(2,1)S(1)} %get-tuple-element.43), channel_id=1, source_target_pairs={{0,1},{1,0},{2,3},{3,2},{4,5},{5,4},{6,7},{7,6},{8,9},{9,8},{10,11... | collective-permute-start | bytes 491528 | tf_op jit(solution)/shard_map/ppermute | solution.py:169
  17.1 0.1 collective-permute-start.11
  17.1 0.3 shard_map.123.refs_0_
  17.5 0.3 collective-permute-done.7.refs_1_
  17.8 0.1 shard_map.124
  17.8 1.6 %collective-permute-start.8 = (bf16[320,512]{1,0:T(8,128)(2,1)S(1)}, bf16[320,512]{1,0:T(8,128)(2,1)S(1)}, u32[]{:S(2)}, u32[]{:S(2)}) collective-permute-start(bf16[320,512]{1,0:T(8,128)(2,1)S(1)} %shard_map.124), channel_id=1, source_target_pairs={{0,2},{2,0},{1,3},{3,1},{4,6},{6,4},{5,7},{7,5},{8,10},{10,8},{9,1... | collective-permute-start | bytes 983048 | tf_op jit(solution)/shard_map/ppermute | solution.py:169
  19.4 0.5 %shard_map.122 = (bf16[320,256]{1,0:T(8,128)(2,1)S(1)}, bf16[320,256]{1,0:T(8,128)(2,1)S(1)}, bf16[320,256]{1,0:T(8,128)(2,1)S(1)}, bf16[320,256]{1,0:T(8,128)(2,1)S(1)}) custom-call(bf16[320,512]{1,0:T(8,128)(2,1)S(1)} %get-tuple-element.41.rows_ref, bf16[512,1024]{1,0:T(8,128)(2,1)S(1)} %get-tuple-element.59.rest_5_.weight_ref), custom_call_target="tpu_custom_call" | custom-call | flops 335544320 | bytes 2686976 | tf_op jit(solution)/shard_map/pallas_call | solution.py:130
  19.9 0.1 collective-permute-start.9
  20.0 0.5 %collective-permute-start.10 = (bf16[320,256]{1,0:T(8,128)(2,1)S(1)}, bf16[320,256]{1,0:T(8,128)(2,1)S(1)}, u32[]{:S(2)}, u32[]{:S(2)}) collective-permute-start(bf16[320,256]{1,0:T(8,128)(2,1)S(1)} %get-tuple-element.50), channel_id=1, source_target_pairs={{0,1},{1,0},{2,3},{3,2},{4,5},{5,4},{6,7},{7,6},{8,9},{9,8},{10,11... | collective-permute-start | bytes 491528 | tf_op jit(solution)/shard_map/ppermute | solution.py:169
  20.5 0.3 shard_map.118
  20.8 0.0 collective-permute-done.11.refs_1_
  20.8 0.1 collective-permute-start.13
  21.0 0.0 collective-permute-done.4.refs_1_
  21.0 0.6 %collective-permute-start.12 = (bf16[320,256]{1,0:T(8,128)(2,1)S(1)}, bf16[320,256]{1,0:T(8,128)(2,1)S(1)}, u32[]{:S(2)}, u32[]{:S(2)}) collective-permute-start(bf16[320,256]{1,0:T(8,128)(2,1)S(1)} %shard_map.125), channel_id=1, source_target_pairs={{0,2},{2,0},{1,3},{3,1},{4,6},{6,4},{5,7},{7,5},{8,10},{10,8},{9,1... | collective-permute-start | bytes 491528 | tf_op jit(solution)/shard_map/ppermute | solution.py:169
  21.6 0.0 collective-permute-done.9.rest_2_
  21.7 0.2 collective-permute-start.6
  21.9 0.0 collective-permute-done.10.rest_5_
  21.9 1.5 %collective-permute-start.5 = (bf16[320,256]{1,0:T(8,128)(2,1)S(1)}, bf16[320,256]{1,0:T(8,128)(2,1)S(1)}, u32[]{:S(2)}, u32[]{:S(2)}) collective-permute-start(bf16[320,256]{1,0:T(8,128)(2,1)S(1)} %shard_map.120), channel_id=1, source_target_pairs={{0,2},{2,0},{1,3},{3,1},{4,6},{6,4},{5,7},{7,5},{8,10},{10,8},{9,1... | collective-permute-start | bytes 491528 | tf_op jit(solution)/shard_map/ppermute | solution.py:169
  23.4 0.5 %shard_map.121 = (f32[320,256]{1,0:T(8,128)S(1)}, f32[320,256]{1,0:T(8,128)S(1)}, f32[320,256]{1,0:T(8,128)S(1)}, f32[320,256]{1,0:T(8,128)S(1)}) custom-call(bf16[320,512]{1,0:T(8,128)(2,1)S(1)} %get-tuple-element.41.rows_ref, bf16[512,1024]{1,0:T(8,128)(2,1)S(1)} %get-tuple-element.60.rest_4_.weight_ref), custom_call_target="tpu_custom_call" | custom-call | flops 335544320 | bytes 2686976 | tf_op jit(solution)/shard_map/pallas_call | solution.py:130
  23.9 0.0 collective-permute-done.13.rest_8_
  23.9 8.1 %collective-permute-done.12.rest_6_ = bf16[320,256]{1,0:T(8,128)(2,1)S(1)} collective-permute-done((bf16[320,256]{1,0:T(8,128)(2,1)S(1)}, bf16[320,256]{1,0:T(8,128)(2,1)S(1)}, u32[]{:S(2)}, u32[]{:S(2)}) %collective-permute-start.12) | collective-permute-done | bytes 163872 | tf_op jit(solution)/shard_map/ppermute | solution.py:169
  32.0 0.0 collective-permute-done.8.rest_0_.rest_3_
  32.0 0.9 %shard_map.126 = (bf16[192,1024]{1,0:T(8,128)(2,1)}, bf16[2,64,1024]{2,1,0:T(8,128)(2,1)}) custom-call(bf16[320,512]{1,0:T(8,128)(2,1)S(1)} %collective-permute-done.8.rest_0_.rest_3_, f32[320,256]{1,0:T(8,128)S(1)} %get-tuple-element.47.rest_1_, bf16[320,256]{1,0:T(8,128)(2,1)S(1)} %collective-permute-done.9.rest_2_, ...), custom_call_target="tpu_custom_call" | custom-call | flops 2211840 | bytes 8847360 | tf_op jit(solution)/shard_map/pallas_call | solution.py:159
  32.9 0.0 collective-permute-done.6.rest_2_
  32.9 1.8 %collective-permute-done.5.rest_0_ = bf16[320,256]{1,0:T(8,128)(2,1)S(1)} collective-permute-done((bf16[320,256]{1,0:T(8,128)(2,1)S(1)}, bf16[320,256]{1,0:T(8,128)(2,1)S(1)}, u32[]{:S(2)}, u32[]{:S(2)}) %collective-permute-start.5) | collective-permute-done | bytes 163872 | tf_op jit(solution)/shard_map/ppermute | solution.py:169
  34.7 0.7 %shard_map.127 = (bf16[192,1024]{1,0:T(8,128)(2,1)}, bf16[2,64,1024]{2,1,0:T(8,128)(2,1)}) custom-call(bf16[320,256]{1,0:T(8,128)(2,1)S(1)} %collective-permute-done.5.rest_0_, f32[320,256]{1,0:T(8,128)S(1)} %get-tuple-element.44.rest_1_, bf16[320,256]{1,0:T(8,128)(2,1)S(1)} %collective-permute-done.6.rest_2_, ...), custom_call_target="tpu_custom_call", output_to_operand_aliasing={{0}: (3, {}), {1}: (4, {})} | custom-call | flops 245760 | bytes 983040 | tf_op jit(solution)/shard_map/pallas_call | solution.py:159
  (5 shorter events, 0.1 us)
Async XLA Ops:
  0.6 13.0 %copy-start.6 = (s32[2]{0:T(128)S(1)}, s32[2]{0:T(128)}, u32[]{:S(2)}) copy-start(s32[2]{0:T(128)} %param.19) | copy-start | bytes 28
  0.6 12.9 %copy-start.5 = (s32[2]{0:T(128)S(1)}, s32[2]{0:T(128)}, u32[]{:S(2)}) copy-start(s32[2]{0:T(128)} %param.18) | copy-start | bytes 28
  0.7 12.9 %copy-start.3 = (f32[2,64,512]{2,1,0:T(8,128)S(1)}, f32[2,64,512]{2,1,0:T(8,128)}, u32[]{:S(2)}) copy-start(f32[2,64,512]{2,1,0:T(8,128)} %ov_ref.1) | copy-start | bytes 786436
  0.7 12.9 %copy-start.2 = (f32[2,64,512]{2,1,0:T(8,128)S(1)}, f32[2,64,512]{2,1,0:T(8,128)}, u32[]{:S(2)}) copy-start(f32[2,64,512]{2,1,0:T(8,128)} %ok_ref.1) | copy-start | bytes 786436
  0.7 12.9 %copy-start.1 = (f32[2,64,512]{2,1,0:T(8,128)S(1)}, f32[2,64,512]{2,1,0:T(8,128)}, u32[]{:S(2)}) copy-start(f32[2,64,512]{2,1,0:T(8,128)} %oq_ref.1) | copy-start | bytes 786436
  0.7 12.9 %copy-start = (f32[192,512]{1,0:T(8,128)S(1)}, f32[192,512]{1,0:T(8,128)}, u32[]{:S(2)}) copy-start(f32[192,512]{1,0:T(8,128)} %q_ref.1) | copy-start | bytes 1179652
  2.2 11.4 %copy-start.8 = (f32[192,512]{1,0:T(8,128)S(1)}, f32[192,512]{1,0:T(8,128)}, u32[]{:S(2)}) copy-start(f32[192,512]{1,0:T(8,128)} %k_ref.1) | copy-start | bytes 1179652
  2.2 11.4 %copy-start.9 = (f32[192,512]{1,0:T(8,128)S(1)}, f32[192,512]{1,0:T(8,128)}, u32[]{:S(2)}) copy-start(f32[192,512]{1,0:T(8,128)} %v_ref.1) | copy-start | bytes 1179652
  2.2 5.4 %collective-permute-start.1 = (bf16[240,128]{1,0:T(8,128)(2,1)S(1)}, bf16[240,128]{1,0:T(8,128)(2,1)S(1)}, u32[]{:S(2)}, u32[]{:S(2)}) collective-permute-start(bf16[240,128]{1,0:T(8,128)(2,1)S(1)} %get-tuple-element.38.refs_0_), channel_id=1, source_target_pairs={{0,4},{4,0},{8,12},{12,8},{1,5},{5,1},{9,13},{13,9},{2,6},{6,2},{1... | collective-permute-start | bytes 184328 | tf_op jit(solution)/shard_map/ppermute | solution.py:173
  5.3 5.6 %collective-permute-start = (bf16[272,128]{1,0:T(8,128)(2,1)S(1)}, bf16[272,128]{1,0:T(8,128)(2,1)S(1)}, u32[]{:S(2)}, u32[]{:S(2)}) collective-permute-start(bf16[272,128]{1,0:T(8,128)(2,1)S(1)} %get-tuple-element.34.refs_0_), channel_id=1, source_target_pairs={{0,4},{4,0},{8,12},{12,8},{1,5},{5,1},{9,13},{13,9},{2,6},{6,2},{1... | collective-permute-start | bytes 208904 | tf_op jit(solution)/shard_map/ppermute | solution.py:173
  5.4 9.3 %copy-start.7 = (bf16[512,4096]{1,0:T(8,128)(2,1)S(1)}, bf16[512,4096]{1,0:T(8,128)(2,1)}, u32[]{:S(2)}) copy-start(bf16[512,4096]{1,0:T(8,128)(2,1)} %param.21) | copy-start | bytes 12582916
  7.3 8.2 %copy-start.4 = (f32[512]{0:T(512)S(1)}, f32[512]{0:T(512)}, u32[]{:S(2)}) copy-start(f32[512]{0:T(512)} %param.20) | copy-start | bytes 6148
  7.7 7.2 %collective-permute-start.2 = (bf16[240,128]{1,0:T(8,128)(2,1)S(1)}, bf16[240,128]{1,0:T(8,128)(2,1)S(1)}, u32[]{:S(2)}, u32[]{:S(2)}) collective-permute-start(bf16[240,128]{1,0:T(8,128)(2,1)S(1)} %shard_map.116), channel_id=1, source_target_pairs={{0,8},{4,12},{8,0},{12,4},{1,9},{5,13},{9,1},{13,5},{2,10},{6,14},... | collective-permute-start | bytes 184328 | tf_op jit(solution)/shard_map/ppermute | solution.py:173
  10.9 4.5 %collective-permute-start.3 = (bf16[272,128]{1,0:T(8,128)(2,1)S(1)}, bf16[272,128]{1,0:T(8,128)(2,1)S(1)}, u32[]{:S(2)}, u32[]{:S(2)}) collective-permute-start(bf16[272,128]{1,0:T(8,128)(2,1)S(1)} %shard_map.114.after_ref), channel_id=1, source_target_pairs={{0,8},{4,12},{1,9},{5,13},{2,10},{6,14},{3,11},{7,15},{16,24},{20,... | collective-permute-start | bytes 208904 | tf_op jit(solution)/shard_map/ppermute | solution.py:177
  16.1 1.7 %collective-permute-start.7 = (bf16[320,512]{1,0:T(8,128)(2,1)S(1)}, bf16[320,512]{1,0:T(8,128)(2,1)S(1)}, u32[]{:S(2)}, u32[]{:S(2)}) collective-permute-start(bf16[320,512]{1,0:T(8,128)(2,1)S(1)} %get-tuple-element.46), channel_id=1, source_target_pairs={{0,1},{1,0},{2,3},{3,2},{4,5},{5,4},{6,7},{7,6},{8,9},{9,8},{10,11... | collective-permute-start | bytes 983048 | tf_op jit(solution)/shard_map/ppermute | solution.py:169
  16.5 4.5 %collective-permute-start.4 = (bf16[320,256]{1,0:T(8,128)(2,1)S(1)}, bf16[320,256]{1,0:T(8,128)(2,1)S(1)}, u32[]{:S(2)}, u32[]{:S(2)}) collective-permute-start(bf16[320,256]{1,0:T(8,128)(2,1)S(1)} %get-tuple-element.43), channel_id=1, source_target_pairs={{0,1},{1,0},{2,3},{3,2},{4,5},{5,4},{6,7},{7,6},{8,9},{9,8},{10,11... | collective-permute-start | bytes 491528 | tf_op jit(solution)/shard_map/ppermute | solution.py:169
  17.1 3.7 %collective-permute-start.11 = (bf16[320,256]{1,0:T(8,128)(2,1)S(1)}, bf16[320,256]{1,0:T(8,128)(2,1)S(1)}, u32[]{:S(2)}, u32[]{:S(2)}) collective-permute-start(bf16[320,256]{1,0:T(8,128)(2,1)S(1)} %get-tuple-element.52), channel_id=1, source_target_pairs={{0,1},{1,0},{2,3},{3,2},{4,5},{5,4},{6,7},{7,6},{8,9},{9,8},{10,11... | collective-permute-start | bytes 491528 | tf_op jit(solution)/shard_map/ppermute | solution.py:169
  17.8 14.1 %collective-permute-start.8 = (bf16[320,512]{1,0:T(8,128)(2,1)S(1)}, bf16[320,512]{1,0:T(8,128)(2,1)S(1)}, u32[]{:S(2)}, u32[]{:S(2)}) collective-permute-start(bf16[320,512]{1,0:T(8,128)(2,1)S(1)} %shard_map.124), channel_id=1, source_target_pairs={{0,2},{2,0},{1,3},{3,1},{4,6},{6,4},{5,7},{7,5},{8,10},{10,8},{9,1... | collective-permute-start | bytes 983048 | tf_op jit(solution)/shard_map/ppermute | solution.py:169
  19.9 1.8 %collective-permute-start.9 = (bf16[320,256]{1,0:T(8,128)(2,1)S(1)}, bf16[320,256]{1,0:T(8,128)(2,1)S(1)}, u32[]{:S(2)}, u32[]{:S(2)}) collective-permute-start(bf16[320,256]{1,0:T(8,128)(2,1)S(1)} %get-tuple-element.48), channel_id=1, source_target_pairs={{0,1},{1,0},{2,3},{3,2},{4,5},{5,4},{6,7},{7,6},{8,9},{9,8},{10,11... | collective-permute-start | bytes 491528 | tf_op jit(solution)/shard_map/ppermute | solution.py:169
  20.0 1.9 %collective-permute-start.10 = (bf16[320,256]{1,0:T(8,128)(2,1)S(1)}, bf16[320,256]{1,0:T(8,128)(2,1)S(1)}, u32[]{:S(2)}, u32[]{:S(2)}) collective-permute-start(bf16[320,256]{1,0:T(8,128)(2,1)S(1)} %get-tuple-element.50), channel_id=1, source_target_pairs={{0,1},{1,0},{2,3},{3,2},{4,5},{5,4},{6,7},{7,6},{8,9},{9,8},{10,11... | collective-permute-start | bytes 491528 | tf_op jit(solution)/shard_map/ppermute | solution.py:169
  20.8 3.1 %collective-permute-start.13 = (bf16[320,256]{1,0:T(8,128)(2,1)S(1)}, bf16[320,256]{1,0:T(8,128)(2,1)S(1)}, u32[]{:S(2)}, u32[]{:S(2)}) collective-permute-start(bf16[320,256]{1,0:T(8,128)(2,1)S(1)} %get-tuple-element.54), channel_id=1, source_target_pairs={{0,1},{1,0},{2,3},{3,2},{4,5},{5,4},{6,7},{7,6},{8,9},{9,8},{10,11... | collective-permute-start | bytes 491528 | tf_op jit(solution)/shard_map/ppermute | solution.py:169
  21.0 11.0 %collective-permute-start.12 = (bf16[320,256]{1,0:T(8,128)(2,1)S(1)}, bf16[320,256]{1,0:T(8,128)(2,1)S(1)}, u32[]{:S(2)}, u32[]{:S(2)}) collective-permute-start(bf16[320,256]{1,0:T(8,128)(2,1)S(1)} %shard_map.125), channel_id=1, source_target_pairs={{0,2},{2,0},{1,3},{3,1},{4,6},{6,4},{5,7},{7,5},{8,10},{10,8},{9,1... | collective-permute-start | bytes 491528 | tf_op jit(solution)/shard_map/ppermute | solution.py:169
  21.7 11.3 %collective-permute-start.6 = (bf16[320,256]{1,0:T(8,128)(2,1)S(1)}, bf16[320,256]{1,0:T(8,128)(2,1)S(1)}, u32[]{:S(2)}, u32[]{:S(2)}) collective-permute-start(bf16[320,256]{1,0:T(8,128)(2,1)S(1)} %get-tuple-element.45), channel_id=1, source_target_pairs={{0,1},{1,0},{2,3},{3,2},{4,5},{5,4},{6,7},{7,6},{8,9},{9,8},{10,11... | collective-permute-start | bytes 491528 | tf_op jit(solution)/shard_map/ppermute | solution.py:169
  21.9 12.8 %collective-permute-start.5 = (bf16[320,256]{1,0:T(8,128)(2,1)S(1)}, bf16[320,256]{1,0:T(8,128)(2,1)S(1)}, u32[]{:S(2)}, u32[]{:S(2)}) collective-permute-start(bf16[320,256]{1,0:T(8,128)(2,1)S(1)} %shard_map.120), channel_id=1, source_target_pairs={{0,2},{2,0},{1,3},{3,1},{4,6},{6,4},{5,7},{7,5},{8,10},{10,8},{9,1... | collective-permute-start | bytes 491528 | tf_op jit(solution)/shard_map/ppermute | solution.py:169

commit v7 on v6

--- a/solution.py
+++ b/solution.py
@@ -231,15 +231,18 @@
     )(use, valid, gain[None], queries, base, *[p[0] for p in parts], *weights[0], *early)
 
     def summed(d, spans, done=()):
-        ours, *theirs = weights[d]
+        (ours, *theirs), rows = weights[d], normed
         some = [spans for spans in (spans[:1], spans[1:]) if spans] if d == 1 else [spans]
+        mine = list(project(rows, ours, some[0], f32))
+        if done:
+            rows, _ = lax.optimization_barrier((normed, mine))
         theirs = [
-            list(early) + sum([list(project(normed, w, spans, bf16)) for spans in some[len(early):]], [])
+            list(early) + sum([list(project(rows, w, spans, bf16)) for spans in some[len(early):]], [])
             for w, early in zip(theirs, [[x] for x in done] or [[]] * len(theirs))
         ]
-        ours = sum([list(project(normed, ours, spans, f32)) for spans in some], [])
+        mine += sum([list(project(normed, ours, spans, f32)) for spans in some[1:]], [])
         theirs = [[ring(x, "sub", n_sub, s + 1) for x in xs] for s, xs in enumerate(theirs)]
-        return list(zip(ours, *theirs))
+        return list(zip(mine, *theirs))
 
     parts = []
     for d in range(1, n_head):

time: 35.6 us -> 35.6 us (level)
  no operation moved by 1% of the time
where the time goes in v7:
time: 35.6 us; the launch traced here: 35.4 us
  starting transfers between devices  14.3 us (40%)
  waiting for transfers between devices  10.9 us (31%)
  Pallas kernels  5.49 us (15%)
  local copies, waits for them, and re-layouts  2.17 us (6%)
  matrix products  1.47 us (4%)
  between operations  0.94 us (3%)
    ppermute x10, waiting for transfers between devices, ring(): lax.ppermute(value, axis, [(i, (i + shift) % size) for i in range(size)])  10.1 us
    ppermute x3, starting transfers between devices, swap(): return lax.ppermute(value, axis, [(i, i ^ mask) for i in range(size)])  6.43 us
    ppermute x10, starting transfers between devices, ring(): lax.ppermute(value, axis, [(i, (i + shift) % size) for i in range(size)])  5.29 us
    ppermute x1, starting transfers between devices, upward(): lax.ppermute(value, axis, [(i, i ^ mask) for i in range(size) if not i &...  2.56 us
    dynamic_slice x2, local copies, waits for them, and re-layouts, blocks(): return [lax.dynamic_slice_in_dim(later, x, width, 1) for x in at]  2.05 us
    pallas_call x5, Pallas kernels, project(): call(functools.partial(project_kernel, spans), [Shape((count, b - a), dty...  1.99 us
    pallas_call x2, Pallas kernels, final(): call(functools.partial(final_kernel, spans, [len(some) for some in terms]...  1.68 us
    dot_general x1, matrix products, on_device(): jnp.einsum('thd,the->hde', k.reshape(tokens, heads, DH), v.reshape(tokens...  1.47 us
  transfers between devices with their start and end apart: 14, of which 5 were waited for; matrix products, arithmetic and copies ran while one was open for 6% of the time, Pallas kernels for 12%

profile of v7, /device:TPU:0, one launch (start us, length us, event | category | flops | bytes accessed | tf_op | source)
XLA Modules:
  0.0 35.4 jit_solution(16106318300063770205)
XLA Ops:
  0.6 0.0 copy-start.6
  0.6 0.0 copy-start.5
  0.7 0.0 copy-start.3
  0.7 0.0 copy-start.2
  0.7 0.0 copy-start.1
  0.7 0.0 copy-start
  0.7 1.5 %conditional.1 = (bf16[512,128]{1,0:T(8,128)(2,1)S(1)}) conditional(s32[]{:T(128)} %convert_element_type.14, () %tuple.16, (f32[192,512]{1,0:T(8,128)}, f32[192,512]{1,0:T(8,128)}) %tuple.17), branch_computations={%region_0.0_spmd, %region_1.0_spmd} | conditional | flops 25165824 | bytes 917512 | solution.py:204
  0.7 1.5 %convolution_convert_fusion = bf16[4,128,128]{2,1,0:T(8,128)(2,1)S(1)} fusion(f32[192,512]{1,0:T(8,128)} %get-tuple-element.8, f32[192,512]{1,0:T(8,128)} %get-tuple-element.4), kind=kOutput, calls=%fused_computation | convolution fusion | flops 25165824 | bytes 917504 | tf_op jit(solution)/shard_map/cond/branch_1_fun/thd,the->hde/dot_general | solution.py:206
  2.2 0.0 copy-start.8
  2.2 0.0 copy-start.9
  2.2 3.1 %collective-permute-start.1 = (bf16[240,128]{1,0:T(8,128)(2,1)S(1)}, bf16[240,128]{1,0:T(8,128)(2,1)S(1)}, u32[]{:S(2)}, u32[]{:S(2)}) collective-permute-start(bf16[240,128]{1,0:T(8,128)(2,1)S(1)} %get-tuple-element.39.refs_0_), channel_id=1, source_target_pairs={{0,4},{4,0},{8,12},{12,8},{1,5},{5,1},{9,13},{13,9},{2,6},{6,2},{1... | collective-permute-start | bytes 184328 | tf_op jit(solution)/shard_map/ppermute | solution.py:173
  5.3 0.1 collective-permute-start
  5.4 0.0 copy-start.7
  5.4 1.9 %constant_dynamic-slice_fusion = (bf16[512,1024]{1,0:T(8,128)(2,1)S(1)}, bf16[512,1024]{1,0:T(8,128)(2,1)S(1)}) fusion(bf16[512,4096]{1,0:T(8,128)(2,1)} %param.21, s32[]{:T(128)S(6)} %select_n.46, s32[]{:T(128)S(6)} %select_n.45), kind=kLoop, calls=%fused_computation.6 | loop fusion | bytes 4194312 | tf_op jit(solution)/shard_map/dynamic_slice | solution.py:221
  7.3 0.0 copy-start.4
  7.3 0.1 add_convert_fusion
  7.4 0.3 collective-permute-done.1.refs_1_.rest_0_
  7.7 3.3 %collective-permute-start.2 = (bf16[240,128]{1,0:T(8,128)(2,1)S(1)}, bf16[240,128]{1,0:T(8,128)(2,1)S(1)}, u32[]{:S(2)}, u32[]{:S(2)}) collective-permute-start(bf16[240,128]{1,0:T(8,128)(2,1)S(1)} %shard_map.116), channel_id=1, source_target_pairs={{0,8},{4,12},{8,0},{12,4},{1,9},{5,13},{9,1},{13,5},{2,10},{6,14},... | collective-permute-start | bytes 184328 | tf_op jit(solution)/shard_map/ppermute | solution.py:173
  10.9 0.0 collective-permute-done.refs_1_.rest_1_
  10.9 2.6 %collective-permute-start.3 = (bf16[272,128]{1,0:T(8,128)(2,1)S(1)}, bf16[272,128]{1,0:T(8,128)(2,1)S(1)}, u32[]{:S(2)}, u32[]{:S(2)}) collective-permute-start(bf16[272,128]{1,0:T(8,128)(2,1)S(1)} %shard_map.114.after_ref), channel_id=1, source_target_pairs={{0,8},{4,12},{1,9},{5,13},{2,10},{6,14},{3,11},{7,15},{16,24},{20,... | collective-permute-start | bytes 208904 | tf_op jit(solution)/shard_map/ppermute | solution.py:177
  13.5 0.1 broadcast_in_dim.15.use_ref
  13.6 0.0 copy-done.6
  13.6 0.0 copy-done.5
  13.6 0.0 copy-done.3
  13.6 0.0 copy-done.2
  13.6 0.0 copy-done.1
  13.6 0.0 copy-done
  13.6 0.0 copy-done.8
  13.6 0.0 copy-done.9
  13.6 1.0 %shard_map.115 = (f32[320,512]{1,0:T(8,128)S(1)}, bf16[320,512]{1,0:T(8,128)(2,1)S(1)}, f32[320,128]{1,0:T(8,128)S(1)}) custom-call(s32[1,2]{1,0:T(1,128)S(1)} %bitcast.21, s32[1,2]{1,0:T(1,128)S(1)} %bitcast.22, f32[192,512]{1,0:T(8,128)S(1)} %copy-done, f32[192,512]{1,0:T(8,128)S(1)} %copy-done.8, f32[192,512]{1,0:T(8,128)S(1)} %copy-done.9, ...), custom_call_target="tpu_custom_call" | custom-call | flops 209715200 | bytes 2621440 | tf_op jit(solution)/shard_map/pallas_call | solution.py:214
  14.7 0.0 copy-done.7
  14.7 0.2 constant_dynamic-slice_fusion.2
  14.9 0.0 collective-permute-done.2.rest_2_
  14.9 0.5 %collective-permute-done.3.rest_3_ = bf16[272,128]{1,0:T(8,128)(2,1)S(1)} collective-permute-done((bf16[272,128]{1,0:T(8,128)(2,1)S(1)}, bf16[272,128]{1,0:T(8,128)(2,1)S(1)}, u32[]{:S(2)}, u32[]{:S(2)}) %collective-permute-start.3) | collective-permute-done | bytes 69664 | tf_op jit(solution)/shard_map/ppermute | solution.py:177
  15.4 0.0 copy-done.4
  15.4 0.6 %shard_map.117 = (bf16[320,512]{1,0:T(8,128)(2,1)S(1)}, bf16[320,512]{1,0:T(8,128)(2,1)S(1)}) custom-call(f32[4,128]{1,0:T(4,128)S(1)} %broadcast_in_dim.15.use_ref, f32[320,128]{1,0:T(8,128)S(1)} %get-tuple-element.36.valid_ref, f32[1,512]{1,0:T(1,128)S(1)} %bitcast.20, bf16[320,512]{1,0:T(8,128)(2,1)S(1)} %get-tuple-element.37.queries_ref, ...), custom_call_target="tpu_custom_call" | custom-call | flops 41943040 | bytes 1638400 | tf_op jit(solution)/shard_map/pallas_call | solution.py:226
  16.1 0.1 collective-permute-start.7
  16.2 0.3 shard_map.119.refs_0_
  16.5 0.3 shard_map.120
  16.8 0.6 %collective-permute-start.4 = (bf16[320,256]{1,0:T(8,128)(2,1)S(1)}, bf16[320,256]{1,0:T(8,128)(2,1)S(1)}, u32[]{:S(2)}, u32[]{:S(2)}) collective-permute-start(bf16[320,256]{1,0:T(8,128)(2,1)S(1)} %get-tuple-element.45), channel_id=1, source_target_pairs={{0,1},{1,0},{2,3},{3,2},{4,5},{5,4},{6,7},{7,6},{8,9},{9,8},{10,11... | collective-permute-start | bytes 491528 | tf_op jit(solution)/shard_map/ppermute | solution.py:169
  17.4 0.1 collective-permute-start.11
  17.5 0.3 collective-permute-done.7.refs_1_
  17.8 0.1 shard_map.124
  17.8 1.6 %collective-permute-start.8 = (bf16[320,512]{1,0:T(8,128)(2,1)S(1)}, bf16[320,512]{1,0:T(8,128)(2,1)S(1)}, u32[]{:S(2)}, u32[]{:S(2)}) collective-permute-start(bf16[320,512]{1,0:T(8,128)(2,1)S(1)} %shard_map.124), channel_id=1, source_target_pairs={{0,2},{2,0},{1,3},{3,1},{4,6},{6,4},{5,7},{7,5},{8,10},{10,8},{9,1... | collective-permute-start | bytes 983048 | tf_op jit(solution)/shard_map/ppermute | solution.py:169
  19.4 0.5 %shard_map.123 = (bf16[320,256]{1,0:T(8,128)(2,1)S(1)}, bf16[320,256]{1,0:T(8,128)(2,1)S(1)}, bf16[320,256]{1,0:T(8,128)(2,1)S(1)}, bf16[320,256]{1,0:T(8,128)(2,1)S(1)}) custom-call(bf16[320,512]{1,0:T(8,128)(2,1)S(1)} %get-tuple-element.44.rows_ref, bf16[512,1024]{1,0:T(8,128)(2,1)S(1)} %get-tuple-element.61.rest_5_.weight_ref), custom_call_target="tpu_custom_call" | custom-call | flops 335544320 | bytes 2686976 | tf_op jit(solution)/shard_map/pallas_call | solution.py:130
  19.9 0.1 collective-permute-start.9
  20.0 0.5 %collective-permute-start.10 = (bf16[320,256]{1,0:T(8,128)(2,1)S(1)}, bf16[320,256]{1,0:T(8,128)(2,1)S(1)}, u32[]{:S(2)}, u32[]{:S(2)}) collective-permute-start(bf16[320,256]{1,0:T(8,128)(2,1)S(1)} %get-tuple-element.52), channel_id=1, source_target_pairs={{0,1},{1,0},{2,3},{3,2},{4,5},{5,4},{6,7},{7,6},{8,9},{9,8},{10,11... | collective-permute-start | bytes 491528 | tf_op jit(solution)/shard_map/ppermute | solution.py:169
  20.5 0.3 shard_map.118
  20.8 0.0 collective-permute-done.11.refs_1_
  20.8 0.1 collective-permute-start.13
  21.0 0.0 collective-permute-done.4.refs_1_
  21.0 0.6 %collective-permute-start.12 = (bf16[320,256]{1,0:T(8,128)(2,1)S(1)}, bf16[320,256]{1,0:T(8,128)(2,1)S(1)}, u32[]{:S(2)}, u32[]{:S(2)}) collective-permute-start(bf16[320,256]{1,0:T(8,128)(2,1)S(1)} %shard_map.125), channel_id=1, source_target_pairs={{0,2},{2,0},{1,3},{3,1},{4,6},{6,4},{5,7},{7,5},{8,10},{10,8},{9,1... | collective-permute-start | bytes 491528 | tf_op jit(solution)/shard_map/ppermute | solution.py:169
  21.6 0.0 collective-permute-done.9.rest_2_
  21.7 0.2 collective-permute-start.6
  21.9 0.0 collective-permute-done.10.rest_5_
  21.9 1.5 %collective-permute-start.5 = (bf16[320,256]{1,0:T(8,128)(2,1)S(1)}, bf16[320,256]{1,0:T(8,128)(2,1)S(1)}, u32[]{:S(2)}, u32[]{:S(2)}) collective-permute-start(bf16[320,256]{1,0:T(8,128)(2,1)S(1)} %shard_map.121), channel_id=1, source_target_pairs={{0,2},{2,0},{1,3},{3,1},{4,6},{6,4},{5,7},{7,5},{8,10},{10,8},{9,1... | collective-permute-start | bytes 491528 | tf_op jit(solution)/shard_map/ppermute | solution.py:169
  23.4 0.5 %shard_map.122 = (f32[320,256]{1,0:T(8,128)S(1)}, f32[320,256]{1,0:T(8,128)S(1)}, f32[320,256]{1,0:T(8,128)S(1)}, f32[320,256]{1,0:T(8,128)S(1)}) custom-call(bf16[320,512]{1,0:T(8,128)(2,1)S(1)} %get-tuple-element.44.rows_ref, bf16[512,1024]{1,0:T(8,128)(2,1)S(1)} %get-tuple-element.62.rest_4_.weight_ref), custom_call_target="tpu_custom_call" | custom-call | flops 335544320 | bytes 2686976 | tf_op jit(solution)/shard_map/pallas_call | solution.py:130
  23.9 0.0 collective-permute-done.13.rest_8_
  23.9 8.1 %collective-permute-done.12.rest_6_ = bf16[320,256]{1,0:T(8,128)(2,1)S(1)} collective-permute-done((bf16[320,256]{1,0:T(8,128)(2,1)S(1)}, bf16[320,256]{1,0:T(8,128)(2,1)S(1)}, u32[]{:S(2)}, u32[]{:S(2)}) %collective-permute-start.12) | collective-permute-done | bytes 163872 | tf_op jit(solution)/shard_map/ppermute | solution.py:169
  32.0 0.0 collective-permute-done.8.rest_0_.rest_3_
  32.0 0.9 %shard_map.126 = (bf16[192,1024]{1,0:T(8,128)(2,1)}, bf16[2,64,1024]{2,1,0:T(8,128)(2,1)}) custom-call(bf16[320,512]{1,0:T(8,128)(2,1)S(1)} %collective-permute-done.8.rest_0_.rest_3_, f32[320,256]{1,0:T(8,128)S(1)} %get-tuple-element.49.rest_1_, bf16[320,256]{1,0:T(8,128)(2,1)S(1)} %collective-permute-done.9.rest_2_, ...), custom_call_target="tpu_custom_call" | custom-call | flops 2211840 | bytes 8847360 | tf_op jit(solution)/shard_map/pallas_call | solution.py:159
  32.9 0.0 collective-permute-done.6.rest_2_
  32.9 1.7 %collective-permute-done.5.rest_0_ = bf16[320,256]{1,0:T(8,128)(2,1)S(1)} collective-permute-done((bf16[320,256]{1,0:T(8,128)(2,1)S(1)}, bf16[320,256]{1,0:T(8,128)(2,1)S(1)}, u32[]{:S(2)}, u32[]{:S(2)}) %collective-permute-start.5) | collective-permute-done | bytes 163872 | tf_op jit(solution)/shard_map/ppermute | solution.py:169
  34.7 0.7 %shard_map.127 = (bf16[192,1024]{1,0:T(8,128)(2,1)}, bf16[2,64,1024]{2,1,0:T(8,128)(2,1)}) custom-call(bf16[320,256]{1,0:T(8,128)(2,1)S(1)} %collective-permute-done.5.rest_0_, f32[320,256]{1,0:T(8,128)S(1)} %get-tuple-element.46.rest_1_, bf16[320,256]{1,0:T(8,128)(2,1)S(1)} %collective-permute-done.6.rest_2_, ...), custom_call_target="tpu_custom_call", output_to_operand_aliasing={{0}: (3, {}), {1}: (4, {})} | custom-call | flops 245760 | bytes 983040 | tf_op jit(solution)/shard_map/pallas_call | solution.py:159
  (5 shorter events, 0.1 us)
Async XLA Ops:
  0.6 13.0 %copy-start.6 = (s32[2]{0:T(128)S(1)}, s32[2]{0:T(128)}, u32[]{:S(2)}) copy-start(s32[2]{0:T(128)} %param.19) | copy-start | bytes 28
  0.6 12.9 %copy-start.5 = (s32[2]{0:T(128)S(1)}, s32[2]{0:T(128)}, u32[]{:S(2)}) copy-start(s32[2]{0:T(128)} %param.18) | copy-start | bytes 28
  0.7 12.9 %copy-start.3 = (f32[2,64,512]{2,1,0:T(8,128)S(1)}, f32[2,64,512]{2,1,0:T(8,128)}, u32[]{:S(2)}) copy-start(f32[2,64,512]{2,1,0:T(8,128)} %ov_ref.1) | copy-start | bytes 786436
  0.7 12.9 %copy-start.2 = (f32[2,64,512]{2,1,0:T(8,128)S(1)}, f32[2,64,512]{2,1,0:T(8,128)}, u32[]{:S(2)}) copy-start(f32[2,64,512]{2,1,0:T(8,128)} %ok_ref.1) | copy-start | bytes 786436
  0.7 12.9 %copy-start.1 = (f32[2,64,512]{2,1,0:T(8,128)S(1)}, f32[2,64,512]{2,1,0:T(8,128)}, u32[]{:S(2)}) copy-start(f32[2,64,512]{2,1,0:T(8,128)} %oq_ref.1) | copy-start | bytes 786436
  0.7 12.9 %copy-start = (f32[192,512]{1,0:T(8,128)S(1)}, f32[192,512]{1,0:T(8,128)}, u32[]{:S(2)}) copy-start(f32[192,512]{1,0:T(8,128)} %q_ref.1) | copy-start | bytes 1179652
  2.2 11.4 %copy-start.8 = (f32[192,512]{1,0:T(8,128)S(1)}, f32[192,512]{1,0:T(8,128)}, u32[]{:S(2)}) copy-start(f32[192,512]{1,0:T(8,128)} %k_ref.1) | copy-start | bytes 1179652
  2.2 11.4 %copy-start.9 = (f32[192,512]{1,0:T(8,128)S(1)}, f32[192,512]{1,0:T(8,128)}, u32[]{:S(2)}) copy-start(f32[192,512]{1,0:T(8,128)} %v_ref.1) | copy-start | bytes 1179652
  2.2 5.4 %collective-permute-start.1 = (bf16[240,128]{1,0:T(8,128)(2,1)S(1)}, bf16[240,128]{1,0:T(8,128)(2,1)S(1)}, u32[]{:S(2)}, u32[]{:S(2)}) collective-permute-start(bf16[240,128]{1,0:T(8,128)(2,1)S(1)} %get-tuple-element.39.refs_0_), channel_id=1, source_target_pairs={{0,4},{4,0},{8,12},{12,8},{1,5},{5,1},{9,13},{13,9},{2,6},{6,2},{1... | collective-permute-start | bytes 184328 | tf_op jit(solution)/shard_map/ppermute | solution.py:173
  5.3 5.6 %collective-permute-start = (bf16[272,128]{1,0:T(8,128)(2,1)S(1)}, bf16[272,128]{1,0:T(8,128)(2,1)S(1)}, u32[]{:S(2)}, u32[]{:S(2)}) collective-permute-start(bf16[272,128]{1,0:T(8,128)(2,1)S(1)} %get-tuple-element.35.refs_0_), channel_id=1, source_target_pairs={{0,4},{4,0},{8,12},{12,8},{1,5},{5,1},{9,13},{13,9},{2,6},{6,2},{1... | collective-permute-start | bytes 208904 | tf_op jit(solution)/shard_map/ppermute | solution.py:173
  5.4 9.3 %copy-start.7 = (bf16[512,4096]{1,0:T(8,128)(2,1)S(1)}, bf16[512,4096]{1,0:T(8,128)(2,1)}, u32[]{:S(2)}) copy-start(bf16[512,4096]{1,0:T(8,128)(2,1)} %param.21) | copy-start | bytes 12582916
  7.3 8.2 %copy-start.4 = (f32[512]{0:T(512)S(1)}, f32[512]{0:T(512)}, u32[]{:S(2)}) copy-start(f32[512]{0:T(512)} %param.20) | copy-start | bytes 6148
  7.7 7.2 %collective-permute-start.2 = (bf16[240,128]{1,0:T(8,128)(2,1)S(1)}, bf16[240,128]{1,0:T(8,128)(2,1)S(1)}, u32[]{:S(2)}, u32[]{:S(2)}) collective-permute-start(bf16[240,128]{1,0:T(8,128)(2,1)S(1)} %shard_map.116), channel_id=1, source_target_pairs={{0,8},{4,12},{8,0},{12,4},{1,9},{5,13},{9,1},{13,5},{2,10},{6,14},... | collective-permute-start | bytes 184328 | tf_op jit(solution)/shard_map/ppermute | solution.py:173
  10.9 4.5 %collective-permute-start.3 = (bf16[272,128]{1,0:T(8,128)(2,1)S(1)}, bf16[272,128]{1,0:T(8,128)(2,1)S(1)}, u32[]{:S(2)}, u32[]{:S(2)}) collective-permute-start(bf16[272,128]{1,0:T(8,128)(2,1)S(1)} %shard_map.114.after_ref), channel_id=1, source_target_pairs={{0,8},{4,12},{1,9},{5,13},{2,10},{6,14},{3,11},{7,15},{16,24},{20,... | collective-permute-start | bytes 208904 | tf_op jit(solution)/shard_map/ppermute | solution.py:177
  16.1 1.7 %collective-permute-start.7 = (bf16[320,512]{1,0:T(8,128)(2,1)S(1)}, bf16[320,512]{1,0:T(8,128)(2,1)S(1)}, u32[]{:S(2)}, u32[]{:S(2)}) collective-permute-start(bf16[320,512]{1,0:T(8,128)(2,1)S(1)} %get-tuple-element.48), channel_id=1, source_target_pairs={{0,1},{1,0},{2,3},{3,2},{4,5},{5,4},{6,7},{7,6},{8,9},{9,8},{10,11... | collective-permute-start | bytes 983048 | tf_op jit(solution)/shard_map/ppermute | solution.py:169
  16.8 4.2 %collective-permute-start.4 = (bf16[320,256]{1,0:T(8,128)(2,1)S(1)}, bf16[320,256]{1,0:T(8,128)(2,1)S(1)}, u32[]{:S(2)}, u32[]{:S(2)}) collective-permute-start(bf16[320,256]{1,0:T(8,128)(2,1)S(1)} %get-tuple-element.45), channel_id=1, source_target_pairs={{0,1},{1,0},{2,3},{3,2},{4,5},{5,4},{6,7},{7,6},{8,9},{9,8},{10,11... | collective-permute-start | bytes 491528 | tf_op jit(solution)/shard_map/ppermute | solution.py:169
  17.4 3.4 %collective-permute-start.11 = (bf16[320,256]{1,0:T(8,128)(2,1)S(1)}, bf16[320,256]{1,0:T(8,128)(2,1)S(1)}, u32[]{:S(2)}, u32[]{:S(2)}) collective-permute-start(bf16[320,256]{1,0:T(8,128)(2,1)S(1)} %get-tuple-element.54), channel_id=1, source_target_pairs={{0,1},{1,0},{2,3},{3,2},{4,5},{5,4},{6,7},{7,6},{8,9},{9,8},{10,11... | collective-permute-start | bytes 491528 | tf_op jit(solution)/shard_map/ppermute | solution.py:169
  17.8 14.1 %collective-permute-start.8 = (bf16[320,512]{1,0:T(8,128)(2,1)S(1)}, bf16[320,512]{1,0:T(8,128)(2,1)S(1)}, u32[]{:S(2)}, u32[]{:S(2)}) collective-permute-start(bf16[320,512]{1,0:T(8,128)(2,1)S(1)} %shard_map.124), channel_id=1, source_target_pairs={{0,2},{2,0},{1,3},{3,1},{4,6},{6,4},{5,7},{7,5},{8,10},{10,8},{9,1... | collective-permute-start | bytes 983048 | tf_op jit(solution)/shard_map/ppermute | solution.py:169
  19.9 1.8 %collective-permute-start.9 = (bf16[320,256]{1,0:T(8,128)(2,1)S(1)}, bf16[320,256]{1,0:T(8,128)(2,1)S(1)}, u32[]{:S(2)}, u32[]{:S(2)}) collective-permute-start(bf16[320,256]{1,0:T(8,128)(2,1)S(1)} %get-tuple-element.50), channel_id=1, source_target_pairs={{0,1},{1,0},{2,3},{3,2},{4,5},{5,4},{6,7},{7,6},{8,9},{9,8},{10,11... | collective-permute-start | bytes 491528 | tf_op jit(solution)/shard_map/ppermute | solution.py:169
  20.0 1.9 %collective-permute-start.10 = (bf16[320,256]{1,0:T(8,128)(2,1)S(1)}, bf16[320,256]{1,0:T(8,128)(2,1)S(1)}, u32[]{:S(2)}, u32[]{:S(2)}) collective-permute-start(bf16[320,256]{1,0:T(8,128)(2,1)S(1)} %get-tuple-element.52), channel_id=1, source_target_pairs={{0,1},{1,0},{2,3},{3,2},{4,5},{5,4},{6,7},{7,6},{8,9},{9,8},{10,11... | collective-permute-start | bytes 491528 | tf_op jit(solution)/shard_map/ppermute | solution.py:169
  20.8 3.1 %collective-permute-start.13 = (bf16[320,256]{1,0:T(8,128)(2,1)S(1)}, bf16[320,256]{1,0:T(8,128)(2,1)S(1)}, u32[]{:S(2)}, u32[]{:S(2)}) collective-permute-start(bf16[320,256]{1,0:T(8,128)(2,1)S(1)} %get-tuple-element.56), channel_id=1, source_target_pairs={{0,1},{1,0},{2,3},{3,2},{4,5},{5,4},{6,7},{7,6},{8,9},{9,8},{10,11... | collective-permute-start | bytes 491528 | tf_op jit(solution)/shard_map/ppermute | solution.py:169
  21.0 11.0 %collective-permute-start.12 = (bf16[320,256]{1,0:T(8,128)(2,1)S(1)}, bf16[320,256]{1,0:T(8,128)(2,1)S(1)}, u32[]{:S(2)}, u32[]{:S(2)}) collective-permute-start(bf16[320,256]{1,0:T(8,128)(2,1)S(1)} %shard_map.125), channel_id=1, source_target_pairs={{0,2},{2,0},{1,3},{3,1},{4,6},{6,4},{5,7},{7,5},{8,10},{10,8},{9,1... | collective-permute-start | bytes 491528 | tf_op jit(solution)/shard_map/ppermute | solution.py:169
  21.7 11.3 %collective-permute-start.6 = (bf16[320,256]{1,0:T(8,128)(2,1)S(1)}, bf16[320,256]{1,0:T(8,128)(2,1)S(1)}, u32[]{:S(2)}, u32[]{:S(2)}) collective-permute-start(bf16[320,256]{1,0:T(8,128)(2,1)S(1)} %get-tuple-element.47), channel_id=1, source_target_pairs={{0,1},{1,0},{2,3},{3,2},{4,5},{5,4},{6,7},{7,6},{8,9},{9,8},{10,11... | collective-permute-start | bytes 491528 | tf_op jit(solution)/shard_map/ppermute | solution.py:169
  21.9 12.8 %collective-permute-start.5 = (bf16[320,256]{1,0:T(8,128)(2,1)S(1)}, bf16[320,256]{1,0:T(8,128)(2,1)S(1)}, u32[]{:S(2)}, u32[]{:S(2)}) collective-permute-start(bf16[320,256]{1,0:T(8,128)(2,1)S(1)} %shard_map.121), channel_id=1, source_target_pairs={{0,2},{2,0},{1,3},{3,1},{4,6},{6,4},{5,7},{7,5},{8,10},{10,8},{9,1... | collective-permute-start | bytes 491528 | tf_op jit(solution)/shard_map/ppermute | solution.py:169
